TPU v7x, 32 devices: a whole 2x2x4 slice. The times are simulated.
32 devices in a mesh: tm: 8 (over z, x), item: 4 (over y, core).
Axes of the slice: x: 2, y: 2, z: 4, core: 2. Of those that a mesh axis runs over, the one named last changes fastest.
Arguments:
- inputs: float32 [32, 8192, 128], P('item', 'tm'), may hold values from -16 to 16
- lengths: int32 [32], P('item'), may hold values from 4096 to 8192, as said below
- counts: int32 [32], P('item'), may hold values from 2 to 3, as said below
- weight_in: float32 [128, 512], replicated, may hold values from -0.5 to 0.5
- bias_in: float32 [512], replicated, may hold values from -1.75 to 1.75
- slope_in: float32 [512], replicated, may hold values from 0.1 to 0.5
- gain_in: float32 [512], replicated, may hold values from 0.25 to 1.75
- shift_in: float32 [512], replicated, may hold values from -1.75 to 1.75
- channelwise_taps: float32 [3, 512], replicated, may hold values from -3.5 to 3.5
- channelwise_bias: float32 [512], replicated, may hold values from -1.75 to 1.75
- slope_out: float32 [512], replicated, may hold values from 0.1 to 0.5
- gain_out: float32 [512], replicated, may hold values from 0.25 to 1.75
- shift_out: float32 [512], replicated, may hold values from -1.75 to 1.75
- weight_res: float32 [512, 128], replicated, may hold values from -0.25 to 0.25
- bias_res: float32 [128], replicated, may hold values from -1.75 to 1.75
- weight_skip: float32 [512, 128], replicated, may hold values from -0.25 to 0.25
- bias_skip: float32 [128], replicated, may hold values from -1.75 to 1.75
- grad_residual: float32 [32, 8192, 128], P('item', 'tm'), may hold values from -6 to 6
- grad_skip: float32 [32, 3, 8192, 128], P('item', None, 'tm'), may hold values from -3.5 to 3.5
Outputs:
- residual_out: float32 [32, 8192, 128], P('item', 'tm')
- skip_out: float32 [32, 8192, 128], P('item', 'tm')
- grad_inputs: float32 [32, 8192, 128], P('item', 'tm')
- grad_weight_in: float32 [128, 512], replicated
- grad_bias_in: float32 [512], replicated
- grad_slope_in: float32 [512], replicated
- grad_gain_in: float32 [512], replicated
- grad_shift_in: float32 [512], replicated
- grad_depth_taps: float32 [3, 512], replicated
- grad_depth_bias: float32 [512], replicated
- grad_slope_out: float32 [512], replicated
- grad_gain_out: float32 [512], replicated
- grad_shift_out: float32 [512], replicated
- grad_weight_res: float32 [512, 128], replicated
- grad_bias_res: float32 [128], replicated
- grad_weight_skip: float32 [512, 128], replicated
- grad_bias_skip: float32 [128], replicated
Inputs may be any that keep to these rules, and one draw needn't show every extreme that they name: `lengths`: among the 8 items of each index of item, one has all 8192 frames valid. `counts`: both values occur in every draw.
All inputs are finite; a program needn't handle non-finite values.
Results may differ from a plain program's by a relative error of at most 0.0003.
Values sent between devices are 32-bit elements; how exact they have to be, the bound alone decides.
No kernel may reach another device: no remote copies, remote signals or barrier semaphores. Data moves between devices by JAX's collectives and lax.ppermute only.
A program may use at most 256 MiB of HBM per device.

v0:
```python
import jax
import jax.numpy as jnp
from jax import lax
from jax.sharding import PartitionSpec as P

TAP_SPACING = 128


epsilon = 1e-05
highest = lax.Precision.HIGHEST


def padded(array, sides, width):
    for axis, dim in sides:
        size, length = (lax.axis_size(axis), array.shape[dim])
        up = [(i, (i + 1) % size) for i in range(size - 1)]
        down = [(j, i) for i, j in up]
        last = lax.slice_in_dim(array, length - width, length, axis=dim)
        leading = lax.slice_in_dim(array, 0, width, axis=dim)
        before = lax.ppermute(last, axis, up)
        after = lax.ppermute(leading, axis, down)
        array = jnp.concatenate([before, array, after], axis=dim)
    return array


def passed_along(array, axis, by):
    length = lax.axis_size(axis)
    pairs = [(i, i + by) for i in range(length) if 0 <= i + by < length]
    return lax.ppermute(array, axis, pairs)


def soft_prelu(value, slope):
    return jax.nn.softplus(value) - slope * jax.nn.softplus(-value)


def norm_forward(value, mask, count):
    total = jnp.sum(value * mask, axis=(1, 2))
    mean = lax.psum(total, "tm") / count
    centered = (value - mean[:, None, None]) * mask
    variance = lax.psum(jnp.sum(centered * centered, axis=(1, 2)), "tm") / count
    scale = lax.rsqrt(variance + epsilon)
    normal = (value - mean[:, None, None]) * scale[:, None, None]
    return (normal, scale, mean)


def norm_backward(grad_out, normal, scale, mask, count, gain):
    masked = grad_out * mask
    gain_grad = jnp.sum(masked * normal, axis=(0, 1))
    shift_grad = jnp.sum(masked, axis=(0, 1))
    scaled = masked * gain
    first_sum, second_sum = lax.psum(
        (jnp.sum(scaled, axis=(1, 2)), jnp.sum(scaled * normal, axis=(1, 2))), "tm"
    )
    grad_in = (
        scale[:, None, None]
        * mask
        * (
            scaled
            - (first_sum / count)[:, None, None]
            - normal * (second_sum / count)[:, None, None]
        )
    )
    return (grad_in, gain_grad, shift_grad)


def project(left, right):
    return jnp.dot(left, right, precision=highest, preferred_element_type=jnp.float32)


def outer_sum(left, right):
    return jnp.einsum(
        "ifa,ifb->ab", left, right, precision=highest, preferred_element_type=jnp.float32
    )


def body(
    inputs,
    lengths,
    counts,
    weight_in,
    bias_in,
    slope_in,
    gain_in,
    shift_in,
    channelwise_taps,
    channelwise_bias,
    slope_out,
    gain_out,
    shift_out,
    weight_res,
    bias_res,
    weight_skip,
    bias_skip,
    grad_residual,
    grad_skip,
):
    frame_count = inputs.shape[1]
    width = weight_in.shape[1]
    start = lax.axis_index("tm") * frame_count
    position = start + jnp.arange(frame_count, dtype=jnp.int32)
    mask = (position[None, :] < lengths[:, None]).astype(jnp.float32)[:, :, None]
    count = lengths.astype(jnp.float32) * width
    hidden = project(inputs, weight_in) + bias_in
    normal_in, scale_in, mean_in = norm_forward(soft_prelu(hidden, slope_in), mask, count)
    leading_part = (gain_in * normal_in + shift_in) * mask
    extended_hidden = padded(leading_part, (("tm", 1),), TAP_SPACING)
    before = extended_hidden[:, :frame_count]
    later_frames = extended_hidden[:, 2 * TAP_SPACING :]
    convolved_hidden = (
        channelwise_taps[0] * before
        + channelwise_taps[1] * leading_part
        + channelwise_taps[2] * later_frames
        + channelwise_bias
    )
    normal_out, scale_out, mean_out = norm_forward(
        soft_prelu(convolved_hidden, slope_out), mask, count
    )
    second = (gain_out * normal_out + shift_out) * mask
    residual_out = inputs + project(second, weight_res) + bias_res
    skip_out = project(second, weight_skip) + bias_skip
    alive = (jnp.arange(grad_skip.shape[1], dtype=jnp.int32)[None, :] < counts[:, None]).astype(
        jnp.float32
    )
    skip_cot = jnp.sum(grad_skip * alive[:, :, None, None], axis=1)
    grad_second = project(grad_residual, weight_res.T) + project(skip_cot, weight_skip.T)
    grad_weight_res = outer_sum(second, grad_residual)
    grad_bias_res = jnp.sum(grad_residual, axis=(0, 1))
    grad_weight_skip = outer_sum(second, skip_cot)
    grad_bias_skip = jnp.sum(skip_cot, axis=(0, 1))
    grad_act2, grad_gain_out, grad_shift_out = norm_backward(
        grad_second, normal_out, scale_out, mask, count, gain_out
    )
    grad_convolved = grad_act2 * (
        jax.nn.sigmoid(convolved_hidden) + slope_out * jax.nn.sigmoid(-convolved_hidden)
    )
    grad_slope_out = -jnp.sum(grad_act2 * jax.nn.softplus(-convolved_hidden), axis=(0, 1))
    grad_depth_bias = jnp.sum(grad_convolved, axis=(0, 1))
    grad_depth_taps = jnp.stack(
        [
            jnp.sum(grad_convolved * before, axis=(0, 1)),
            jnp.sum(grad_convolved * leading_part, axis=(0, 1)),
            jnp.sum(grad_convolved * later_frames, axis=(0, 1)),
        ]
    )
    lower_border = channelwise_taps[0] * grad_convolved[:, :TAP_SPACING]
    upper_border = channelwise_taps[2] * grad_convolved[:, frame_count - TAP_SPACING :]
    incoming_lower = passed_along(upper_border, "tm", 1)
    incoming_upper = passed_along(lower_border, "tm", -1)
    grad_first = channelwise_taps[1] * grad_convolved
    grad_first = grad_first + jnp.concatenate(
        [channelwise_taps[0] * grad_convolved[:, TAP_SPACING:], incoming_upper], axis=1
    )
    grad_first = grad_first + jnp.concatenate(
        [incoming_lower, channelwise_taps[2] * grad_convolved[:, : frame_count - TAP_SPACING]],
        axis=1,
    )
    grad_act1, grad_gain_in, grad_shift_in = norm_backward(
        grad_first, normal_in, scale_in, mask, count, gain_in
    )
    grad_hidden = grad_act1 * (jax.nn.sigmoid(hidden) + slope_in * jax.nn.sigmoid(-hidden))
    grad_slope_in = -jnp.sum(grad_act1 * jax.nn.softplus(-hidden), axis=(0, 1))
    grad_bias_in = jnp.sum(grad_hidden, axis=(0, 1))
    grad_weight_in = outer_sum(inputs, grad_hidden)
    grad_inputs = grad_residual + project(grad_hidden, weight_in.T)
    summed = lax.psum(
        (
            grad_weight_in,
            grad_bias_in,
            grad_slope_in,
            grad_gain_in,
            grad_shift_in,
            grad_depth_taps,
            grad_depth_bias,
            grad_slope_out,
            grad_gain_out,
            grad_shift_out,
            grad_weight_res,
            grad_bias_res,
            grad_weight_skip,
            grad_bias_skip,
        ),
        ("tm", "item"),
    )
    return (
        residual_out,
        skip_out,
        grad_inputs,
        summed[0],
        summed[1],
        summed[2],
        summed[3],
        summed[4],
        summed[5],
        summed[6],
        summed[7],
        summed[8],
        summed[9],
        summed[10],
        summed[11],
        summed[12],
        summed[13],
    )


def solution(mesh):
    return jax.shard_map(
        body,
        mesh=mesh,
        in_specs=(
            P("item", "tm", None),
            P("item"),
            P("item"),
            P(),
            P(),
            P(),
            P(),
            P(),
            P(),
            P(),
            P(),
            P(),
            P(),
            P(),
            P(),
            P(),
            P(),
            P("item", "tm", None),
            P("item", None, "tm", None),
        ),
        out_specs=(
            P("item", "tm", None),
            P("item", "tm", None),
            P("item", "tm", None),
            P(),
            P(),
            P(),
            P(),
            P(),
            P(),
            P(),
            P(),
            P(),
            P(),
            P(),
            P(),
            P(),
            P(),
        ),
        check_vma=False,
    )
```

profile of v0, /device:TPU:0, one launch (start us, length us, event | category | flops | bytes accessed | tf_op | source)
XLA Modules:
  0.0 828.5 jit_solution(14485831056117559512)
XLA Ops:
  7.2 0.0 copy-start
  7.2 0.0 all-reduce.6.cloned.1.call-start
  7.3 0.8 compare_convert_fusion
  8.0 21.5 %fusion.3 = (u8[1024,512]{1,0:T(8,128)(4,1)S(1)}, u8[1024,512]{1,0:T(8,128)(4,1)S(1)}, f32[8,1024,512]{2,1,0:T(8,128)S(1)}) fusion(f32[512]{0:T(512)} %param.23, f32[8,1024,128]{2,1,0:T(8,128)} %param.19, f32[128,512]{1,0:T(8,128)} %param.22), kind=kOutput, calls=%fused_computation.48 | convolution fusion | flops 6491734016 | bytes 22284288 | tf_op jit(solution)/shard_map/dot_general | solution.py:67
  29.6 0.0 copy-start.27
  29.6 25.6 %multiply_reduce_fusion.12 = (f32[8]{0:T(128)S(1)}, f32[8,1024,512]{2,1,0:T(8,128)}) fusion(f32[8,1024]{1,0:T(8,128)S(1)} %compare_convert_fusion, u8[1024,512]{1,0:T(8,128)(4,1)S(1)} %get-tuple-element.46, f32[512]{0:T(512)S(1)} %copy-done.25, f32[8,1024,512]{2,1,0:T(8,128)S(1)} %get-tuple-element.96, f32[512]{0:T(512)S(1)} %copy-done.23, ...), kind=kLoop, calls=%fused_computation.34 | loop fusion | flops 96468984 | bytes 34639904 | tf_op jit(solution)/shard_map/reduce_sum | solution.py:37
  55.2 0.0 copy-start.31
  55.3 23.1 %psum.154 = f32[8]{0:T(128)S(1)} all-reduce(f32[8]{0:T(128)S(1)} %get-tuple-element.76), channel_id=1, replica_groups=mesh['tm'=8,'item'=4] {'tm'}, use_global_device_ids=true, to_apply=%region_1.2 | all-reduce | flops 8 | bytes 64 | tf_op jit(solution)/shard_map/psum | solution.py:38
  78.4 8.2 multiply_reduce_fusion.11
  86.6 17.1 %psum.155 = f32[8]{0:T(128)S(1)} all-reduce(f32[8]{0:T(128)S(1)} %multiply_reduce_fusion.11), channel_id=1, replica_groups=mesh['tm'=8,'item'=4] {'tm'}, use_global_device_ids=true, to_apply=%region_3.4 | all-reduce | flops 8 | bytes 64 | tf_op jit(solution)/shard_map/psum | solution.py:40
  103.7 0.0 copy-start.35
  103.7 0.0 copy-start.28
  103.8 7.6 add_multiply_fusion.4
  111.3 5.7 copy-done.2
  117.0 2.7 fusion.23
  119.8 4.2 collective-permute-start
  123.9 1.3 collective-permute-start.1
  125.3 0.1 fusion.13
  125.3 11.0 %multiply_reduce_fusion.15 = (f32[128]{0:T(128)}, f32[8,1024,128]{2,1,0:T(8,128)}) fusion(f32[8,3,1024,128]{3,2,1,0:T(8,128)} %param.37, f32[8,3]{1,0:T(8,128)S(1)} %fusion.13), kind=kLoop, calls=%fused_computation.45 | loop fusion | flops 8388480 | bytes 16777824 | tf_op jit(solution)/shard_map/reduce_sum | solution.py:129
  136.3 16.4 %fusion.7 = f32[8,1024,512]{2,1,0:T(8,128)} fusion(f32[8,1024,128]{2,1,0:T(8,128)S(1)} %copy-done.4, f32[512,128]{1,0:T(8,128)S(1)} %copy-done.17), kind=kOutput, calls=%fused_computation.59 | convolution fusion | flops 6442450944 | bytes 21233664 | tf_op jit(solution)/shard_map/dot_general | solution.py:67
  152.7 53.7 %collective-permute-done = f32[8,128,512]{2,1,0:T(8,128)S(1)} collective-permute-done((f32[8,128,512]{2,1,0:T(8,128)}, f32[8,128,512]{2,1,0:T(8,128)S(1)}, u32[]{:S(2)}, u32[]{:S(2)}) %collective-permute-start) | collective-permute-done | bytes 2097184 | tf_op jit(solution)/shard_map/ppermute | solution.py:20
  206.5 33.5 %multiply_reduce_fusion.10 = (f32[8]{0:T(128)S(1)}, f32[8,1024,512]{2,1,0:T(8,128)}) fusion(f32[8,1024]{1,0:T(8,128)S(1)} %compare_convert_fusion, f32[512]{0:T(512)S(1)} %copy-done.22, f32[512]{0:T(512)S(1)} %copy-done.20, f32[8,128,512]{2,1,0:T(8,128)S(1)} %collective-permute-done.1, f32[8,1024,512]{2,1,0:T(8,128)} %copy-done.2, f32[512]{0:T(512)S(1)} %bitcast.54, ...), kind=kLoop, calls=%fused_computation.29 | loop fusion | flops 104857592 | bytes 37791776 | tf_op jit(solution)/shard_map/reduce_sum | solution.py:37
  240.0 0.0 copy-start.19
  240.0 0.0 copy-start.29
  240.0 19.7 %psum.156 = f32[8]{0:T(128)S(1)} all-reduce(f32[8]{0:T(128)S(1)} %get-tuple-element.74), channel_id=1, replica_groups=mesh['tm'=8,'item'=4] {'tm'}, use_global_device_ids=true, to_apply=%region_5.6 | all-reduce | flops 8 | bytes 64 | tf_op jit(solution)/shard_map/psum | solution.py:38
  259.7 8.2 multiply_reduce_fusion.9
  267.9 3.8 reduce_sum.218
  271.7 17.1 %psum.157 = f32[8]{0:T(128)S(1)} all-reduce(f32[8]{0:T(128)S(1)} %multiply_reduce_fusion.9), channel_id=1, replica_groups=mesh['tm'=8,'item'=4] {'tm'}, use_global_device_ids=true, to_apply=%region_7.8 | all-reduce | flops 8 | bytes 64 | tf_op jit(solution)/shard_map/psum | solution.py:40
  288.8 0.1 compare_select_fusion.3
  288.9 0.0 copy-done.19
  288.9 0.0 copy-start.7
  288.9 32.3 %multiply_reduce_fusion.14 = (f32[8]{0:T(128)S(1)}, f32[8]{0:T(128)S(1)}, f32[8,1024,512]{2,1,0:T(8,128)}, f32[8,1024,512]{2,1,0:T(8,128)}) fusion(f32[512]{0:T(512)S(1)} %copy-done.19, f32[8]{0:T(128)S(1)} %add_rsqrt_fusion, f32[8,1024,512]{2,1,0:T(8,128)} %get-tuple-element.75, f32[8]{0:T(128)S(1)} %fusion.18, f32[8,1024]{1,0:T(8,128)S(1)} %compare_convert_fusion, ...), kind=kOutput, calls=%fused_computation.42 | convolution fusion | flops 6488588288 | bytes 71602304 | tf_op jit(solution)/shard_map/dot_general | solution.py:67
  321.3 30.2 %convolution_bitcast_fusion = f32[512,128]{1,0:T(8,128)} fusion(f32[8,1024,512]{2,1,0:T(8,128)} %get-tuple-element.80, f32[8,1024,128]{2,1,0:T(8,128)S(1)} %copy-done.7), kind=kOutput, calls=%fused_computation.54 | convolution fusion | flops 6442450944 | bytes 21233664 | tf_op jit(solution)/shard_map/ifa,ifb->ab/dot_general | solution.py:71
  351.6 0.0 copy-start.11
  351.6 27.7 %convolution_bitcast_fusion.1 = f32[512,128]{1,0:T(8,128)} fusion(f32[8,1024,512]{2,1,0:T(8,128)S(1)} %bitcast.46, f32[8,1024,128]{2,1,0:T(8,128)S(1)} %copy-done.5), kind=kOutput, calls=%fused_computation.55 | convolution fusion | flops 6442450944 | bytes 21233664 | tf_op jit(solution)/shard_map/ifa,ifb->ab/dot_general | solution.py:71
  379.3 19.1 %all-reduce.3 = (f32[8]{0:T(128)S(1)}, f32[8]{0:T(128)S(1)}) all-reduce(f32[8]{0:T(128)S(1)} %get-tuple-element.44, f32[8]{0:T(128)S(1)} %get-tuple-element.43), channel_id=1, replica_groups=mesh['tm'=8,'item'=4] {'tm'}, use_global_device_ids=true, to_apply=%region_12.13 | all-reduce | flops 16 | bytes 128 | tf_op jit(solution)/shard_map/psum | solution.py:51
  398.5 29.6 %multiply_reduce_fusion = (f32[512]{0:T(512)S(1)}, f32[512]{0:T(512)S(1)}, f32[512]{0:T(512)S(1)}) fusion(f32[8,1024,512]{2,1,0:T(8,128)} %get-tuple-element.97, f32[8,1024,512]{2,1,0:T(8,128)} %get-tuple-element.75, f32[8]{0:T(128)S(1)} %add_rsqrt_fusion, f32[8]{0:T(128)S(1)} %fusion.18, f32[512]{0:T(512)S(1)} %copy-done.20, f32[8,128,512]{2,1,0:T(8,128)} %copy-done.12, ...), kind=kLoop, calls=%fused_computation.13 | loop fusion | flops 113244672 | bytes 54575232 | tf_op jit(solution)/shard_map/reduce_sum | solution.py:48
  428.1 0.0 copy-start.8
  428.1 0.0 copy-start.30
  428.1 17.7 %convolution_add_fusion.1 = f32[8,1024,128]{2,1,0:T(8,128)} fusion(f32[8,1024,512]{2,1,0:T(8,128)} %get-tuple-element.80, f32[128]{0:T(128)S(1)} %copy-done.32, f32[512,128]{1,0:T(8,128)S(1)} %copy-done), kind=kOutput, calls=%fused_computation.51 | convolution fusion | flops 6443499520 | bytes 21234176 | tf_op jit(solution)/shard_map/dot_general | solution.py:67
  445.8 15.1 %add_add_fusion.1 = f32[8,1024,128]{2,1,0:T(8,128)} fusion(f32[8,1024,128]{2,1,0:T(8,128)S(1)} %copy-done.8, f32[8,1024,512]{2,1,0:T(8,128)S(1)} %bitcast.48, f32[128]{0:T(128)S(1)} %copy-done.30, f32[512,128]{1,0:T(8,128)S(1)} %copy-done.17), kind=kOutput, calls=%fused_computation.47 | convolution fusion | flops 6444548096 | bytes 25428480 | tf_op jit(solution)/shard_map/dot_general | solution.py:67
  460.9 35.1 %multiply_reduce_fusion.4 = (f32[512]{0:T(512)S(1)}, f32[512]{0:T(512)S(1)}, f32[512]{0:T(512)S(1)}, f32[512]{0:T(512)S(1)}, f32[8,1024,512]{2,1,0:T(8,128)}) fusion(f32[8,1024,512]{2,1,0:T(8,128)} %copy-done.2, f32[8,128,512]{2,1,0:T(8,128)S(1)} %copy-done.11, f32[8,128,512]{2,1,0:T(8,128)} %copy-done.12, f32[512]{0:T(512)S(1)} %copy-done.22, ...), kind=kLoop, calls=%fused_computation.17 | loop fusion | flops 125827072 | bytes 71356544 | tf_op jit(solution)/shard_map/reduce_sum | solution.py:140
  496.0 2.8 slice_multiply_fusion.3
  498.9 1.3 collective-permute-start.2
  500.1 4.7 collective-permute-start.3
  504.9 19.3 %slice_multiply_fusion.1 = (f32[8,896,512]{2,1,0:T(8,128)}, f32[8,896,512]{2,1,0:T(8,128)}) fusion(f32[8,1024,512]{2,1,0:T(8,128)} %get-tuple-element.70, f32[512]{0:T(512)S(1)} %bitcast.53, f32[512]{0:T(512)S(1)} %bitcast.58), kind=kLoop, calls=%fused_computation.44 | loop fusion | flops 7340032 | bytes 58724352 | tf_op jit(solution)/shard_map/mul | solution.py:151
  524.1 11.0 %collective-permute-done.2 = f32[8,128,512]{2,1,0:T(8,128)S(1)} collective-permute-done((f32[8,128,512]{2,1,0:T(8,128)S(1)}, f32[8,128,512]{2,1,0:T(8,128)S(1)}, u32[]{:S(2)}, u32[]{:S(2)}) %collective-permute-start.2) | collective-permute-done | bytes 2097184 | tf_op jit(solution)/shard_map/ppermute | solution.py:29
  535.1 43.4 %collective-permute-done.3 = f32[8,128,512]{2,1,0:T(8,128)S(1)} collective-permute-done((f32[8,128,512]{2,1,0:T(8,128)S(1)}, f32[8,128,512]{2,1,0:T(8,128)S(1)}, u32[]{:S(2)}, u32[]{:S(2)}) %collective-permute-start.3) | collective-permute-done | bytes 2097184 | tf_op jit(solution)/shard_map/ppermute | solution.py:29
  578.5 1.3 copy-done.16
  579.8 28.7 %multiply_reduce_fusion.13 = (f32[8]{0:T(128)S(1)}, f32[8]{0:T(128)S(1)}, f32[8,1024,512]{2,1,0:T(8,128)}) fusion(f32[512]{0:T(512)S(1)} %copy-done.21, f32[8]{0:T(128)S(1)} %add_rsqrt_fusion.1, f32[8,1024,512]{2,1,0:T(8,128)} %get-tuple-element.77, f32[8]{0:T(128)S(1)} %fusion.19, f32[8,1024]{1,0:T(8,128)S(1)} %compare_convert_fusion, ...), kind=kLoop, calls=%fused_computation.41 | loop fusion | flops 50331632 | bytes 83923072 | tf_op jit(solution)/shard_map/reduce_sum | solution.py:52
  608.5 19.6 %all-reduce.2 = (f32[8]{0:T(128)S(1)}, f32[8]{0:T(128)S(1)}) all-reduce(f32[8]{0:T(128)S(1)} %get-tuple-element.42, f32[8]{0:T(128)S(1)} %get-tuple-element.41), channel_id=1, replica_groups=mesh['tm'=8,'item'=4] {'tm'}, use_global_device_ids=true, to_apply=%region_16.17 | all-reduce | flops 16 | bytes 128 | tf_op jit(solution)/shard_map/psum | solution.py:51
  628.1 0.0 copy-start.9
  628.1 27.3 %multiply_reduce_fusion.5 = (f32[512]{0:T(512)S(1)}, f32[512]{0:T(512)S(1)}, f32[512]{0:T(512)S(1)}, f32[512]{0:T(512)S(1)}, f32[8,1024,512]{2,1,0:T(8,128)S(1)}) fusion(f32[8,1024,512]{2,1,0:T(8,128)} %get-tuple-element.73, f32[8,1024,512]{2,1,0:T(8,128)} %get-tuple-element.77, f32[8]{0:T(128)S(1)} %add_rsqrt_fusion.1, f32[8]{0:T(128)S(1)} %fusion.19, ...), kind=kLoop, calls=%fused_computation.18 | loop fusion | flops 130021376 | bytes 67680384 | tf_op jit(solution)/shard_map/reduce_sum | solution.py:48
  655.5 0.0 copy-start.18
  655.5 5.7 copy-done.3
  661.2 27.5 %convolution_bitcast_fusion.2 = f32[128,512]{0,1:T(8,128)} fusion(f32[8,1024,512]{2,1,0:T(8,128)S(1)} %get-tuple-element.79, f32[8,1024,128]{2,1,0:T(8,128)S(1)} %copy-done.9), kind=kOutput, calls=%fused_computation.56 | convolution fusion | flops 6442450944 | bytes 21233664 | tf_op jit(solution)/shard_map/ifa,ifb->ab/dot_general | solution.py:71
  688.7 0.0 all-reduce.6.cloned.1.call-update
  688.7 0.0 copy-start.33
  688.8 18.0 %convolution_add_fusion = f32[8,1024,128]{2,1,0:T(8,128)} fusion(f32[8,1024,128]{2,1,0:T(8,128)} %param.36, f32[8,1024,512]{2,1,0:T(8,128)} %copy-done.3, f32[128,512]{1,0:T(8,128)S(1)} %copy-done.18), kind=kOutput, calls=%fused_computation.50 | convolution fusion | flops 6443499520 | bytes 25427968 | tf_op jit(solution)/shard_map/dot_general | solution.py:67
  706.8 37.8 %all-reduce = (f32[512]{0:T(512)}, f32[512]{0:T(512)}, f32[512]{0:T(512)}, f32[512]{0:T(512)}, f32[3,512]{1,0:T(4,128)}, /*index=5*/f32[512]{0:T(512)}, f32[512]...) all-reduce(f32[512]{0:T(512)S(1)} %get-tuple-element.78, ...), channel_id=1, replica_groups=mesh['tm'=8,'item'=4] {'tm','item'}, use_global_device_ids=true, to_apply=%region_19.20 | all-reduce | flops 5888 | bytes 47104 | tf_op jit(solution)/shard_map/psum | solution.py:165
  744.6 71.7 %all-reduce.6.cloned.1.call-done = (f32[128,512]{0,1:T(8,128)}, f32[512,128]{1,0:T(8,128)}, f32[512,128]{1,0:T(8,128)}) async-done(((f32[128,512]{0,1:T(8,128)}, f32[512,128]{1,0:T(8,128)}, f32[512,128]{1,0:T(8,128)}), (f32[128,512]{0,1:T(8,128)}, f32[512,128]{1,0:T(8,128)}, f32[512,128]{1,0:T(8,128)})) %all-reduce.6.cloned.1.call-update) | async-done | bytes 786448 | tf_op jit(solution)/shard_map/psum | solution.py:165
  816.3 1.8 copy.39
  818.1 1.7 copy.46
  819.8 1.7 copy.47
  (84 shorter events, 0.2 us)
Async XLA Ops:
  7.2 281.7 %copy-start = (f32[512,128]{1,0:T(8,128)S(1)}, f32[512,128]{1,0:T(8,128)}, u32[]{:S(2)}) copy-start(f32[512,128]{1,0:T(8,128)} %param.34) | copy-start | bytes 786436
  7.2 809.1 %all-reduce.6.cloned.1.call-start = ((), (), s32[]{:S(2)}) async-start(), calls=%async_computation | async-start | bytes 1572864 | tf_op jit(solution)/shard_map/psum | solution.py:165
  8.0 21.6 %copy-start.23 = (f32[512]{0:T(512)S(1)}, f32[512]{0:T(512)}, u32[]{:S(2)}) copy-start(f32[512]{0:T(512)} %param.23) | copy-start | bytes 6148
  8.0 21.6 %copy-start.25 = (f32[512]{0:T(512)S(1)}, f32[512]{0:T(512)}, u32[]{:S(2)}) copy-start(f32[512]{0:T(512)} %param.24) | copy-start | bytes 6148
  29.6 25.7 %copy-start.6 = (f32[8,1024,512]{2,1,0:T(8,128)}, f32[8,1024,512]{2,1,0:T(8,128)S(1)}, u32[]{:S(2)}) copy-start(f32[8,1024,512]{2,1,0:T(8,128)S(1)} %get-tuple-element.96) | copy-start | bytes 50331652
  29.6 25.7 %copy-start.13 = (u8[1024,512]{1,0:T(8,128)(4,1)}, u8[1024,512]{1,0:T(8,128)(4,1)S(1)}, u32[]{:S(2)}) copy-start(u8[1024,512]{1,0:T(8,128)(4,1)S(1)} %get-tuple-element.46) | copy-start | bytes 1572868
  29.6 48.7 %copy-start.27 = (s32[8]{0:T(128)S(1)}, s32[8]{0:T(128)}, u32[]{:S(2)}) copy-start(s32[8]{0:T(128)} %param.20) | copy-start | bytes 100
  55.2 48.5 %copy-start.21 = (f32[512]{0:T(512)S(1)}, f32[512]{0:T(512)}, u32[]{:S(2)}) copy-start(f32[512]{0:T(512)} %param.25) | copy-start | bytes 6148
  55.2 48.5 %copy-start.31 = (f32[512]{0:T(512)S(1)}, f32[512]{0:T(512)}, u32[]{:S(2)}) copy-start(f32[512]{0:T(512)} %param.26) | copy-start | bytes 6148
  103.7 21.5 %copy-start.35 = (s32[8]{0:T(128)S(1)}, s32[8]{0:T(128)}, u32[]{:S(2)}) copy-start(s32[8]{0:T(128)} %param.21) | copy-start | bytes 100
  103.7 21.6 %copy-start.28 = (f32[3,512]{1,0:T(4,128)S(1)}, f32[3,512]{1,0:T(4,128)}, u32[]{:S(2)}) copy-start(f32[3,512]{1,0:T(4,128)} %param.27) | copy-start | bytes 18436
  111.3 5.7 copy-start.2
  117.0 19.3 %copy-start.4 = (f32[8,1024,128]{2,1,0:T(8,128)S(1)}, f32[8,1024,128]{2,1,0:T(8,128)}, u32[]{:S(2)}) copy-start(f32[8,1024,128]{2,1,0:T(8,128)} %param.36) | copy-start | bytes 12582916
  117.0 19.3 %copy-start.17 = (f32[512,128]{1,0:T(8,128)S(1)}, f32[512,128]{1,0:T(8,128)}, u32[]{:S(2)}) copy-start(f32[512,128]{1,0:T(8,128)} %param.32) | copy-start | bytes 786436
  119.8 86.7 %collective-permute-start = (f32[8,128,512]{2,1,0:T(8,128)}, f32[8,128,512]{2,1,0:T(8,128)S(1)}, u32[]{:S(2)}, u32[]{:S(2)}) collective-permute-start(f32[8,128,512]{2,1,0:T(8,128)} %get-tuple-element.85), channel_id=1, source_target_pairs={{0,4},{4,8},{8,12},{12,16},{16,20},{20,24},{24,28},{1,5},{5,9},{9,... | collective-permute-start | bytes 6291464 | tf_op jit(solution)/shard_map/ppermute | solution.py:20
  123.9 82.5 %collective-permute-start.1 = (f32[8,128,512]{2,1,0:T(8,128)}, f32[8,128,512]{2,1,0:T(8,128)S(1)}, u32[]{:S(2)}, u32[]{:S(2)}) collective-permute-start(f32[8,128,512]{2,1,0:T(8,128)} %get-tuple-element.86), channel_id=1, source_target_pairs={{4,0},{8,4},{12,8},{16,12},{20,16},{24,20},{28,24},{5,1},{9,5},{13... | collective-permute-start | bytes 6291464 | tf_op jit(solution)/shard_map/ppermute | solution.py:21
  136.3 70.1 %copy-start.20 = (f32[512]{0:T(512)S(1)}, f32[512]{0:T(512)}, u32[]{:S(2)}) copy-start(f32[512]{0:T(512)} %param.28) | copy-start | bytes 6148
  136.3 70.1 %copy-start.22 = (f32[512]{0:T(512)S(1)}, f32[512]{0:T(512)}, u32[]{:S(2)}) copy-start(f32[512]{0:T(512)} %param.29) | copy-start | bytes 6148
  206.4 33.5 %copy-start.10 = (f32[8,128,512]{2,1,0:T(8,128)}, f32[8,128,512]{2,1,0:T(8,128)S(1)}, u32[]{:S(2)}) copy-start(f32[8,128,512]{2,1,0:T(8,128)S(1)} %collective-permute-done) | copy-start | bytes 6291460
  206.4 33.5 %copy-start.12 = (f32[8,128,512]{2,1,0:T(8,128)}, f32[8,128,512]{2,1,0:T(8,128)S(1)}, u32[]{:S(2)}) copy-start(f32[8,128,512]{2,1,0:T(8,128)S(1)} %collective-permute-done.1) | copy-start | bytes 6291460
  240.0 48.9 %copy-start.19 = (f32[512]{0:T(512)S(1)}, f32[512]{0:T(512)}, u32[]{:S(2)}) copy-start(f32[512]{0:T(512)} %param.30) | copy-start | bytes 6148
  240.0 48.9 %copy-start.29 = (f32[512]{0:T(512)S(1)}, f32[512]{0:T(512)}, u32[]{:S(2)}) copy-start(f32[512]{0:T(512)} %param.31) | copy-start | bytes 6148
  288.9 32.4 %copy-start.7 = (f32[8,1024,128]{2,1,0:T(8,128)S(1)}, f32[8,1024,128]{2,1,0:T(8,128)}, u32[]{:S(2)}) copy-start(f32[8,1024,128]{2,1,0:T(8,128)} %get-tuple-element.51) | copy-start | bytes 12582916
  321.3 30.3 %slice-start = ((s8[16777216]{0:T(1024)(128)(4,1)}), s8[4194304]{0:T(1024)(128)(4,1)S(1)}, s32[]{:S(2)}) async-start(s8[16777216]{0:T(1024)(128)(4,1)} %bitcast.45), calls=%async_computation.1 | async-start | bytes 8388608
  321.3 30.3 %copy-start.5 = (f32[8,1024,128]{2,1,0:T(8,128)S(1)}, f32[8,1024,128]{2,1,0:T(8,128)}, u32[]{:S(2)}) copy-start(f32[8,1024,128]{2,1,0:T(8,128)} %param.36) | copy-start | bytes 12582916
  321.3 30.2 %slice-start.1 = ((s8[16777216]{0:T(1024)(128)(4,1)}), s8[4194304]{0:T(1024)(128)(4,1)S(1)}, s32[]{:S(2)}) async-start(s8[16777216]{0:T(1024)(128)(4,1)} %bitcast.45), calls=%async_computation.2 | async-start | bytes 8388608
  321.3 30.2 %slice-start.2 = ((s8[16777216]{0:T(1024)(128)(4,1)}), s8[4194304]{0:T(1024)(128)(4,1)S(1)}, s32[]{:S(2)}) async-start(s8[16777216]{0:T(1024)(128)(4,1)} %bitcast.45), calls=%async_computation.3 | async-start | bytes 8388608
  321.3 30.2 %slice-start.3 = ((s8[16777216]{0:T(1024)(128)(4,1)}), s8[4194304]{0:T(1024)(128)(4,1)S(1)}, s32[]{:S(2)}) async-start(s8[16777216]{0:T(1024)(128)(4,1)} %bitcast.45), calls=%async_computation.4 | async-start | bytes 8388608
  351.6 46.9 %copy-start.11 = (f32[8,128,512]{2,1,0:T(8,128)S(1)}, f32[8,128,512]{2,1,0:T(8,128)}, u32[]{:S(2)}) copy-start(f32[8,128,512]{2,1,0:T(8,128)} %copy-done.10) | copy-start | bytes 6291460
  398.5 29.6 %copy-start.32 = (f32[128]{0:T(128)S(1)}, f32[128]{0:T(128)}, u32[]{:S(2)}) copy-start(f32[128]{0:T(128)} %param.35) | copy-start | bytes 1540
  428.0 17.8 %slice-start.4 = ((s8[16777216]{0:T(1024)(128)(4,1)}), s8[4194304]{0:T(1024)(128)(4,1)S(1)}, s32[]{:S(2)}) async-start(s8[16777216]{0:T(1024)(128)(4,1)} %bitcast.47), calls=%async_computation.5 | async-start | bytes 8388608
  428.1 17.7 %slice-start.5 = ((s8[16777216]{0:T(1024)(128)(4,1)}), s8[4194304]{0:T(1024)(128)(4,1)S(1)}, s32[]{:S(2)}) async-start(s8[16777216]{0:T(1024)(128)(4,1)} %bitcast.47), calls=%async_computation.6 | async-start | bytes 8388608
  428.1 17.7 %slice-start.6 = ((s8[16777216]{0:T(1024)(128)(4,1)}), s8[4194304]{0:T(1024)(128)(4,1)S(1)}, s32[]{:S(2)}) async-start(s8[16777216]{0:T(1024)(128)(4,1)} %bitcast.47), calls=%async_computation.7 | async-start | bytes 8388608
  428.1 17.7 %slice-start.7 = ((s8[16777216]{0:T(1024)(128)(4,1)}), s8[4194304]{0:T(1024)(128)(4,1)S(1)}, s32[]{:S(2)}) async-start(s8[16777216]{0:T(1024)(128)(4,1)} %bitcast.47), calls=%async_computation.8 | async-start | bytes 8388608
  428.1 17.7 %copy-start.8 = (f32[8,1024,128]{2,1,0:T(8,128)S(1)}, f32[8,1024,128]{2,1,0:T(8,128)}, u32[]{:S(2)}) copy-start(f32[8,1024,128]{2,1,0:T(8,128)} %param.19) | copy-start | bytes 12582916
  428.1 17.7 %copy-start.30 = (f32[128]{0:T(128)S(1)}, f32[128]{0:T(128)}, u32[]{:S(2)}) copy-start(f32[128]{0:T(128)} %param.33) | copy-start | bytes 1540
  498.9 36.3 %collective-permute-start.2 = (f32[8,128,512]{2,1,0:T(8,128)S(1)}, f32[8,128,512]{2,1,0:T(8,128)S(1)}, u32[]{:S(2)}, u32[]{:S(2)}) collective-permute-start(f32[8,128,512]{2,1,0:T(8,128)S(1)} %get-tuple-element.83), channel_id=1, source_target_pairs={{4,0},{8,4},{12,8},{16,12},{20,16},{24,20},{28,24},{5,1},{9,5},{13... | collective-permute-start | bytes 6291464 | tf_op jit(solution)/shard_map/ppermute | solution.py:29
  500.1 78.4 %collective-permute-start.3 = (f32[8,128,512]{2,1,0:T(8,128)S(1)}, f32[8,128,512]{2,1,0:T(8,128)S(1)}, u32[]{:S(2)}, u32[]{:S(2)}) collective-permute-start(f32[8,128,512]{2,1,0:T(8,128)S(1)} %get-tuple-element.84), channel_id=1, source_target_pairs={{0,4},{4,8},{8,12},{12,16},{16,20},{20,24},{24,28},{1,5},{5,9},{9,... | collective-permute-start | bytes 6291464 | tf_op jit(solution)/shard_map/ppermute | solution.py:29
  535.1 43.4 %copy-start.15 = (f32[8,128,512]{2,1,0:T(8,128)}, f32[8,128,512]{2,1,0:T(8,128)S(1)}, u32[]{:S(2)}) copy-start(f32[8,128,512]{2,1,0:T(8,128)S(1)} %collective-permute-done.2) | copy-start | bytes 6291460
  578.5 1.3 copy-start.16
  579.8 48.3 %copy-start.14 = (u8[1024,512]{1,0:T(8,128)(4,1)S(1)}, u8[1024,512]{1,0:T(8,128)(4,1)}, u32[]{:S(2)}) copy-start(u8[1024,512]{1,0:T(8,128)(4,1)} %copy-done.13) | copy-start | bytes 1572868
  579.8 48.3 %copy-start.24 = (f32[512]{0:T(512)S(1)}, f32[512]{0:T(512)}, u32[]{:S(2)}) copy-start(f32[512]{0:T(512)} %param.23) | copy-start | bytes 6148
  579.8 48.3 %copy-start.26 = (f32[512]{0:T(512)S(1)}, f32[512]{0:T(512)}, u32[]{:S(2)}) copy-start(f32[512]{0:T(512)} %param.24) | copy-start | bytes 6148
  628.1 33.1 %copy-start.9 = (f32[8,1024,128]{2,1,0:T(8,128)S(1)}, f32[8,1024,128]{2,1,0:T(8,128)}, u32[]{:S(2)}) copy-start(f32[8,1024,128]{2,1,0:T(8,128)} %param.19) | copy-start | bytes 12582916
  655.5 5.7 copy-start.3
  655.5 33.2 %copy-start.18 = (f32[128,512]{1,0:T(8,128)S(1)}, f32[128,512]{1,0:T(8,128)}, u32[]{:S(2)}) copy-start(f32[128,512]{1,0:T(8,128)} %param.22) | copy-start | bytes 786436
  688.7 18.0 %copy-start.33 = (f32[128]{0:T(128)S(1)}, f32[128]{0:T(128)}, u32[]{:S(2)}) copy-start(f32[128]{0:T(128)} %get-tuple-element.50) | copy-start | bytes 1540
  688.8 18.0 %copy-start.34 = (f32[128]{0:T(128)S(1)}, f32[128]{0:T(128)}, u32[]{:S(2)}) copy-start(f32[128]{0:T(128)} %reduce_sum.218) | copy-start | bytes 1540
  688.8 132.7 %copy-start.1 = (f32[512,128]{1,0:T(8,128)S(1)}, f32[512,128]{1,0:T(8,128)}, u32[]{:S(2)}) copy-start(f32[512,128]{1,0:T(8,128)} %param.34) | copy-start | bytes 786436
Sparse Core Ops, SparseCore 0:
  688.9 127.4 all-reduce.5
where the time goes:
time: 836 us; the launch traced here: 829 us
  other arithmetic  242 us (29%)
  matrix products  206 us (25%)
  waiting for transfers between devices  180 us (22%)
  blocking collectives  154 us (18%)
  local copies, waits for them, and re-layouts  20.8 us (2%)
  between operations  14.8 us (2%)
  starting transfers between devices  11.5 us (1%)
    dot_general x6, matrix products, project(): jnp.dot(left, right, precision=highest, preferred_element_type=jnp.float32)  121 us
    dot_general x3, matrix products, outer_sum(): jnp.einsum('ifa,ifb->ab', left, right, precision=highest, preferred_eleme...  85.4 us
    psum x1, waiting for transfers between devices, body(): lax.psum((grad_weight_in, grad_bias_in, grad_slope_in, grad_gain_in, grad...  71.7 us
    reduce_sum x2, other arithmetic, norm_forward(): total = jnp.sum(value * mask, axis=(1, 2))  59.1 us
    reduce_sum x2, other arithmetic, norm_backward(): gain_grad = jnp.sum(masked * normal, axis=(0, 1))  56.9 us
    ppermute x2, waiting for transfers between devices, passed_along(): return lax.ppermute(array, axis, pairs)  54.4 us
    ppermute x1, waiting for transfers between devices, padded(): before = lax.ppermute(last, axis, up)  53.7 us
    psum x2, blocking collectives, norm_forward(): mean = lax.psum(total, 'tm') / count  42.8 us
  transfers between devices with their start and end apart: 5, of which 4 were waited for; matrix products, arithmetic and copies ran while one was open for 8% of the time, Pallas kernels for 0%

commit v1 on v0

v1 whole, which is shorter than its diff:
```python
import functools

import jax
import jax.numpy as jnp
from jax import lax
from jax.experimental import pallas as pl
from jax.experimental.pallas import tpu as pltpu
from jax.sharding import PartitionSpec as P

TAP = 128
LANES = 128
EPSILON = 1e-05
LN2 = 0.6931471805599453
LOG2E = 1.4426950408889634
VMEM = 58 * 2**20
f32 = jnp.float32
bf16 = jnp.bfloat16

BIAS_IN, SLOPE_IN, GAIN_IN, SHIFT_IN, TAP0, TAP1, TAP2, BIAS_DW, SLOPE_OUT, GAIN_OUT, SHIFT_OUT = range(11)
(R_P, R_S, R_SS, R_GD, R_GS, R_H0, R_H1, R_H2, R_HF0, R_HF1, R_HF2, R_PF0, R_PF1, R_PF2,
 R_A0, R_A1, R_A2, R_Z0, R_Z1, R_Z2, R_GM) = range(21)
ROWS = 24


def split(x):
    hi = x.astype(bf16)
    lo = (x - hi.astype(f32)).astype(bf16)
    return hi, lo


def dot(a, b):
    return jnp.dot(a, b, preferred_element_type=f32)


def dot0(a, b):
    return lax.dot_general(a, b, (((0,), (0,)), ((), ())), preferred_element_type=f32)


def product3(x, w3):
    hi, lo = split(x)
    return dot(jnp.concatenate([hi, hi, lo], axis=1), w3)


def stacked3(w):
    hi, lo = split(w)
    return jnp.concatenate([hi, lo, hi], axis=0)


def act(v, a, c):
    e = jnp.exp2(-LOG2E * jnp.abs(v))
    return jnp.maximum(v, a * v) + c * jnp.log2(1.0 + e)


def fold(x):
    rows, cols = x.shape
    return x.reshape(rows // 8, 8, cols).sum(axis=0)


def mask_rows(first, rows, length):
    row = lax.broadcasted_iota(jnp.int32, (rows, 1), 0) + first
    return ((row >= 0) & (row < length)).astype(f32)


def lane_put(values):
    shape = values[0].shape[:-1] + (LANES,)
    lane = lax.broadcasted_iota(jnp.int32, shape, len(shape) - 1)
    out = jnp.zeros(shape, f32)
    for k, v in enumerate(values):
        out = jnp.where(lane == k, jnp.broadcast_to(v, shape), out)
    return out


def first_kernel(rows, len_ref, tm_ref, x_ref, w_ref, pc_ref, v_ref, st_ref, w3):
    i = pl.program_id(0)
    frames, width = v_ref.shape[1:]

    @pl.when(i == 0)
    def _():
        w3[...] = stacked3(w_ref[...])

    length = len_ref[i]
    start = tm_ref[0] * frames
    b, a = pc_ref[BIAS_IN : BIAS_IN + 1], pc_ref[SLOPE_IN : SLOPE_IN + 1]
    c = (1.0 - a) * LN2

    def chunk(k, carry):
        total, square, centre = carry
        r0 = pl.multiple_of(k * rows, rows)
        h = product3(x_ref[0, pl.ds(r0, rows), :], w3[...]) + b
        v = act(h, a, c)
        v_ref[0, pl.ds(r0, rows), :] = v
        centre = jnp.where(k == 0, jnp.broadcast_to(v[0:1], (8, width)), centre)
        m = mask_rows(start + r0, rows, length)
        d = v.reshape(rows // 8, 8, width) - centre[None]
        dm = d * m.reshape(rows // 8, 8, 1)
        return total + dm.sum(axis=0), square + (dm * d).sum(axis=0), centre

    zero = jnp.zeros((8, width), f32)
    total, square, centre = lax.fori_loop(0, frames // rows, chunk, (zero, zero, zero))
    n = jnp.clip(length - start, 0, frames).astype(f32)
    safe = jnp.maximum(jnp.full((1, 1), n, f32), 1.0)
    total = total.sum(axis=0, keepdims=True) / safe
    square = square.sum(axis=0, keepdims=True)
    channel = centre[0:1] + total
    mean = channel.sum(axis=1, keepdims=True) / width
    dev = channel - mean
    spread = (square - safe * total * total + safe * dev * dev).sum(axis=1, keepdims=True)
    some = (n > 0).astype(f32)
    row = lane_put([mean * some, spread * some, jnp.full((1, 1), n, f32)])
    st_ref[:, pl.ds(i, 1), :] = jnp.broadcast_to(row[None], (st_ref.shape[0], 1, LANES))


def merged(gathered, width):
    mean_d, spread_d, n_d = gathered[:, :, 0:1], gathered[:, :, 1:2], gathered[:, :, 2:3]
    n = n_d.sum(axis=0)
    mean = (n_d * mean_d).sum(axis=0) / n
    dev = mean_d - mean[None]
    spread = (spread_d + n_d * width * dev * dev).sum(axis=0)
    count = n * width
    return mean, lax.rsqrt(spread / count + EPSILON), count


def wide(x, width):
    return jnp.broadcast_to(x[:, 0:1], (x.shape[0], width))


def second_kernel(
    rows, len_ref, cnt_ref, tm_ref, v_ref, xb_ref, xa_ref, gr_ref, gk_ref, w_ref, wr_ref, ws_ref, pc_ref, ga_ref,
    f0_ref, f1_ref, f2_ref, z_ref, y_ref, ch_ref, st_ref, bias_ref,
    w3, wt3, wg3, stat, fst, grc, gsc, acc, yacc,
):
    i = pl.program_id(0)
    frames, width = v_ref.shape[1:]
    base = gr_ref.shape[2]
    total_frames = frames * ga_ref.shape[0]

    def par(k):
        return pc_ref[k : k + 1]

    @pl.when(i == 0)
    def _():
        w3[...] = stacked3(w_ref[...])
        both = jnp.concatenate([wr_ref[...], ws_ref[...]], axis=1)
        wt3[...] = stacked3(both.T)
        gain = pc_ref[GAIN_OUT : GAIN_OUT + 1]
        scaled = jnp.concatenate([(wr_ref[...].T * gain).T, (ws_ref[...].T * gain).T], axis=1)
        wg3[...] = stacked3(scaled)
        mean, scale, _ = merged(ga_ref[...], width)
        stat[0] = jnp.broadcast_to(mean, stat.shape[1:])
        stat[1] = jnp.broadcast_to(scale, stat.shape[1:])
        bias_ref[...] = jnp.zeros_like(bias_ref)

    length = len_ref[i]
    start = tm_ref[0] * frames
    mean = wide(stat[0, pl.ds(i, 1), :], width)
    scale = wide(stat[1, pl.ds(i, 1), :], width)
    gain = par(GAIN_IN) * scale
    shift = par(SHIFT_IN) - gain * mean
    a1 = par(SLOPE_IN)
    c1 = (1.0 - a1) * LN2

    for ref, r0 in ((xb_ref, 0), (xa_ref, frames + TAP)):
        h = product3(ref[0], w3[...]) + par(BIAS_IN)
        m = mask_rows(start + r0 - TAP, TAP, length)
        fst[r0 : r0 + TAP, :] = m * (gain * act(h, a1, c1) + shift)

    def lift(k, _):
        r0 = pl.multiple_of(k * rows, rows)
        m = mask_rows(start + r0, rows, length)
        fst[pl.ds(TAP + r0, rows), :] = m * (gain * v_ref[0, pl.ds(r0, rows), :] + shift)
        return 0

    lax.fori_loop(0, frames // rows, lift, 0)

    acc[...] = jnp.zeros_like(acc)
    yacc[...] = jnp.zeros_like(yacc)
    alive = [(s < cnt_ref[i]).astype(f32) for s in range(gk_ref.shape[1])]
    taps = [par(TAP0), par(TAP1), par(TAP2)]
    a2 = par(SLOPE_OUT)

    def chunk(k, _):
        r0 = pl.multiple_of(k * rows, rows)
        g_res = gr_ref[0, pl.ds(r0, rows), :]
        g_skip = alive[0] * gk_ref[0, 0, pl.ds(r0, rows), :]
        for s in range(1, len(alive)):
            g_skip = g_skip + alive[s] * gk_ref[0, s, pl.ds(r0, rows), :]
        m = mask_rows(start + r0, rows, length)
        both = jnp.concatenate([g_res, g_skip], axis=1)
        bias_ref[...] += fold(both)
        both = both * m
        acc[R_GM, :, 0 : 2 * base] += fold(both)
        ghi, glo = split(both)
        gs = dot(jnp.concatenate([ghi, ghi, glo], axis=1), wt3[...])
        his, los = [], []
        for j in range(width // LANES):
            s = slice(j * LANES, (j + 1) * LANES)
            f = (
                taps[0][:, s] * fst[pl.ds(r0, rows), s]
                + taps[1][:, s] * fst[pl.ds(r0 + TAP, rows), s]
                + taps[2][:, s] * fst[pl.ds(r0 + 2 * TAP, rows), s]
                + par(BIAS_DW)[:, s]
            )
            t = jnp.tanh(0.5 * f)
            a = a2[:, s]
            v = jnp.maximum(f, a * f) - ((1.0 - a) * LN2) * jnp.log2(0.5 + 0.5 * jnp.abs(t))
            dm = (0.5 + 0.5 * a) * m + ((0.5 - 0.5 * a) * m) * t

            @pl.when(k == 0)
            def _():
                acc[R_P, :, s] = jnp.broadcast_to(v[0:1], (8, LANES))

            d = v - acc[R_P, 0:1, s]
            g = gs[:, s]
            dd = d * m
            f0 = g * dm
            f2 = d * dm
            f0_ref[0, pl.ds(r0, rows), s] = f0
            f1_ref[0, pl.ds(r0, rows), s] = dm
            f2_ref[0, pl.ds(r0, rows), s] = f2
            acc[R_S, :, s] += fold(dd)
            acc[R_SS, :, s] += fold(dd * d)
            acc[R_GD, :, s] += fold(g * d)
            acc[R_GS, :, s] += fold(g)
            acc[R_H0, :, s] += fold(f0)
            acc[R_H1, :, s] += fold(dm)
            acc[R_H2, :, s] += fold(f2)
            acc[R_HF0, :, s] += fold(f0 * f)
            acc[R_HF1, :, s] += fold(dm * f)
            acc[R_HF2, :, s] += fold(f2 * f)
            acc[R_PF0, :, s] += fold(g * f)
            acc[R_PF1, :, s] += fold(m * f)
            acc[R_PF2, :, s] += fold(dd * f)
            hi, lo = split(d)
            his.append(hi)
            los.append(lo)
        hi, lo = jnp.concatenate(his, axis=1), jnp.concatenate(los, axis=1)
        z_ref[0, pl.ds(r0, rows), :] = dot(jnp.concatenate([hi, hi, lo], axis=1), wg3[...])
        yacc[...] += dot0(jnp.concatenate([ghi, ghi, glo], axis=0), jnp.concatenate([hi, lo, hi], axis=0))

        t0 = start + r0
        for row, near in ((R_A0, t0 < TAP), (R_Z0, (t0 < length) & (t0 + rows > length - TAP))):
            @pl.when(near)
            def _():
                at = lax.broadcasted_iota(jnp.int32, (rows, 1), 0) + t0
                edge = (at < TAP) if row == R_A0 else (at >= length - TAP)
                edge = edge.astype(f32)
                for q, ref in enumerate((f0_ref, f1_ref, f2_ref)):
                    acc[row + q] += fold(edge * ref[0, pl.ds(r0, rows), :])
        return 0

    lax.fori_loop(0, frames // rows, chunk, 0)
    y_ref[0] = yacc[...]
    sums = acc[...].sum(axis=1)
    point = acc[R_P, 0:1, :]
    ch_ref[0, 0:1, :] = point
    ch_ref[0, 1:ROWS, :] = sums[1:ROWS]

    def got(r):
        return sums[r : r + 1]

    n = jnp.clip(length - start, 0, frames).astype(f32)
    n_v = jnp.full((1, 1), n, f32)
    some = (n > 0).astype(f32)
    safe = jnp.maximum(n_v, 1.0)
    offset = got(R_S) / safe
    channel = point + offset
    mean2 = channel.sum(axis=1, keepdims=True) / width
    dev = channel - mean2
    spread = (got(R_SS) - safe * offset * offset + safe * dev * dev).sum(axis=1, keepdims=True)
    point = point - mean2
    gout = par(GAIN_OUT)
    wsum = taps[0] + taps[1] + taps[2]
    g1, sh1, cb = par(GAIN_IN), par(SHIFT_IN), par(BIAS_DW)

    def summed(x):
        return x.sum(axis=1, keepdims=True)

    s1 = summed(gout * got(R_GS))
    s2 = summed(gout * (got(R_GD) + point * got(R_GS)))
    t1, t2 = [], []
    for q in range(3):
        h, hf = got(R_H0 + q), got(R_HF0 + q)
        kh = wsum * h - taps[0] * got(R_A0 + q) - taps[2] * got(R_Z0 + q)
        if q == 0:
            h, hf, kh = gout * h, gout * hf, gout * kh
        if q == 2:
            h1, hf1 = got(R_H1), got(R_HF1)
            kh1 = wsum * h1 - taps[0] * got(R_A1) - taps[2] * got(R_Z1)
            h, hf, kh = h + point * h1, hf + point * hf1, kh + point * kh1
        t1.append(summed(g1 * kh))
        t2.append(summed(hf - cb * h - sh1 * kh))
    row = lane_put([mean2 * some, spread * some, n_v, s1, s2] + t1 + t2)
    st_ref[:, pl.ds(i, 1), :] = jnp.broadcast_to(row[None], (st_ref.shape[0], 1, LANES))


def third_kernel(
    rows, len_ref, tm_ref, v_ref, xb_ref, x_ref, xa_ref, f0_ref, f1_ref, f2_ref, gr_ref, z_ref, y_ref,
    ch_ref, bias_ref, w_ref, wr_ref, ws_ref, br_ref, pc_ref, ga1_ref, ga2_ref,
    res_ref, skip_ref, gin_ref, side_ref, sum_ref,
    w3, wt3, stat, coef, chan, zc, ext, vext, gw, gwt, acc,
):
    i = pl.program_id(0)
    items = pl.num_programs(0)
    frames, width = v_ref.shape[1:]
    base = gr_ref.shape[2]

    def par(k):
        return pc_ref[k : k + 1]

    def put(k, x):
        stat[k] = jnp.broadcast_to(x, stat.shape[1:])

    @pl.when(i == 0)
    def _():
        w3[...] = stacked3(w_ref[...])
        wt3[...] = stacked3(w_ref[...].T)
        mean1, scale1, count = merged(ga1_ref[...], width)
        mean2, scale2, _ = merged(ga2_ref[...], width)
        g = ga2_ref[...]

        def lane(k):
            return g[:, :, k : k + 1]

        dev = lane(0) - mean2[None]
        s1 = lane(3).sum(axis=0)
        s2 = (lane(4) + dev * lane(3)).sum(axis=0)
        alpha = scale2 * s1 / count
        beta = scale2 * scale2 * scale2 * s2 / count
        t1 = scale2 * lane(5).sum(axis=0) - alpha * lane(6).sum(axis=0) - beta * (lane(7) + dev * lane(6)).sum(axis=0)
        t2 = scale2 * lane(8).sum(axis=0) - alpha * lane(9).sum(axis=0) - beta * (lane(10) + dev * lane(9)).sum(axis=0)
        put(0, mean1)
        put(1, scale1)
        put(2, scale2)
        put(3, beta)
        put(4, scale1 * t1 / count)
        put(5, scale1 * scale1 * t2 / count)
        delta = ch_ref[:, R_P, :] - mean2
        coef[0] = scale2 * par(GAIN_OUT)
        coef[1] = alpha + beta * delta
        coef[2] = scale2 * par(GAIN_OUT) * delta + par(SHIFT_OUT)
        both = jnp.concatenate([wr_ref[...], ws_ref[...]], axis=1)
        zc[...] = lax.dot_general(
            coef[2], both, (((1,), (0,)), ((), ())), precision=lax.Precision.HIGHEST, preferred_element_type=f32
        )

        def row(r):
            return ch_ref[:, r, :]

        c0, c1 = coef[0], coef[1]

        def comb(r):
            return c0 * row(r) - c1 * row(r + 1) - beta * row(r + 2)

        h, hf, h_a, h_z = comb(R_H0), comb(R_HF0), comb(R_A0), comb(R_Z0)
        kh = (par(TAP0) + par(TAP1) + par(TAP2)) * h - par(TAP0) * h_a - par(TAP2) * h_z
        n = ga2_ref[pl.ds(tm_ref[0], 1), :, 2:3][0]
        total = c0 * row(R_GS) - c1 * n - beta * row(R_S)
        total_d = c0 * row(R_GD) - c1 * row(R_S) - beta * row(R_SS)
        total_f = c0 * row(R_PF0) - c1 * row(R_PF1) - beta * row(R_PF2)
        slope = (total_d + row(R_P) * total - total_f) / (1.0 - par(SLOPE_OUT))

        def over(x):
            return x.sum(axis=0, keepdims=True)

        gain_out = over(scale2 * row(R_GD) + (scale2 * delta) * row(R_GS))
        gain_in = over(hf - par(BIAS_DW) * h - par(SHIFT_IN) * kh) / par(GAIN_IN)
        shift = par(SHIFT_IN) - par(GAIN_IN) * scale1 * mean1
        chan[...] = jnp.concatenate(
            [jnp.zeros((2, width), f32), gain_in, over(kh), over(shift * (h - h_a)), over(shift * h),
             over(shift * (h - h_z)), over(h), -over(slope), gain_out, over(row(R_GS)), jnp.zeros((5, width), f32)],
            axis=0,
        )
        gw[...] = jnp.zeros_like(gw)
        gwt[...] = jnp.zeros_like(gwt)
        acc[...] = jnp.zeros_like(acc)

    length = len_ref[i]
    start = tm_ref[0] * frames

    def st(k):
        return wide(stat[k, pl.ds(i, 1), :], width)

    mean1, scale1, scale2, beta, cut, cut_v = [st(k) for k in range(6)]
    c0, c1 = coef[0, pl.ds(i, 1), :], coef[1, pl.ds(i, 1), :]
    gwt[...] += coef[0, pl.ds(i, 1), :] * y_ref[0]
    gain1 = par(GAIN_IN) * scale1
    taps = [par(TAP0), par(TAP1), par(TAP2)]
    a1 = par(SLOPE_IN)
    lead = TAP

    zeros = jnp.zeros((2 * TAP, width), f32)
    ext[0 : 2 * TAP, :] = zeros
    ext[frames + 2 * TAP : frames + 4 * TAP, :] = zeros

    def lift(k, _):
        r0 = pl.multiple_of(k * rows, rows)
        at = pl.ds(r0, rows)
        ext[pl.ds(2 * TAP + r0, rows), :] = c0 * f0_ref[0, at, :] - c1 * f1_ref[0, at, :] - beta * f2_ref[0, at, :]
        return 0

    lax.fori_loop(0, frames // rows, lift, 0)

    def part(x, at, rows, own, v_own):
        h = product3(x, w3[...]) + par(BIAS_IN)
        m = mask_rows(start + at - TAP, rows, length)
        xhi, xlo = split(x)
        his, los = [], []
        for j in range(width // LANES):
            s = slice(j * LANES, (j + 1) * LANES)
            hj, a = h[:, s], a1[:, s]
            t = jnp.tanh(0.5 * hj)
            logs = ((1.0 - a) * LN2) * jnp.log2(0.5 + 0.5 * jnp.abs(t))
            v = jnp.maximum(hj, a * hj) - logs
            later = ext[pl.ds(at + 2 * TAP, rows), s]
            here = ext[pl.ds(at + TAP, rows), s]
            before = ext[pl.ds(at, rows), s]
            vm = v * m
            acc[2, :, s] += gain1[:, s] * fold(later * vm)
            acc[3, :, s] += gain1[:, s] * fold(here * vm)
            acc[4, :, s] += gain1[:, s] * fold(before * vm)
            u = taps[0][:, s] * later + taps[1][:, s] * here + taps[2][:, s] * before
            u = gain1[:, s] * u
            if own:
                u = u - cut[:, s] - cut_v[:, s] * (v - mean1[:, s])
            u = u * m
            acc[1, :, s] += fold(u * (v - hj))
            gh = u * ((0.5 + 0.5 * a) + (0.5 - 0.5 * a) * t)
            acc[0, :, s] += fold(gh)
            hi, lo = split(gh)
            his.append(hi)
            los.append(lo)
        hi, lo = jnp.concatenate(his, axis=1), jnp.concatenate(los, axis=1)
        gw[...] += dot0(jnp.concatenate([xhi, xhi, xlo], axis=0), jnp.concatenate([hi, lo, hi], axis=0))
        return dot(jnp.concatenate([hi, hi, lo], axis=1), wt3[...])

    side_ref[0, 0] = part(xb_ref[0], 0, TAP, False, None)
    side_ref[1, 0] = part(xa_ref[0], frames + TAP, TAP, False, None)

    scale_c = stat[2, pl.ds(i, 1), :]

    def chunk(k, _):
        r0 = pl.multiple_of(k * rows, rows)
        at = pl.ds(r0, rows)
        x = x_ref[0, at, :]
        back = part(x, r0 + TAP, rows, True, None)
        gin_ref[0, at, :] = gr_ref[0, at, :] + back
        m = mask_rows(start + r0, rows, length)
        z = z_ref[0, at, :]
        zi = zc[pl.ds(i, 1), :]
        res_ref[0, at, :] = x + m * (scale_c * z[:, 0:base] + zi[:, 0:base]) + br_ref[0:1, :]
        skip_ref[0, at, :] = m * (scale_c * z[:, base:] + zi[:, base:]) + br_ref[1:2, :]
        return 0

    lax.fori_loop(0, frames // rows, chunk, 0)

    @pl.when(i == items - 1)
    def _():
        outer = lax.dot_general(
            ch_ref[:, R_GM, 0 : 2 * base], coef[2], (((0,), (0,)), ((), ())),
            precision=lax.Precision.HIGHEST, preferred_element_type=f32,
        )
        both = (gwt[...] + outer).T
        sum_ref[0:width, :] = both[:, 0:base]
        sum_ref[width : 2 * width, :] = both[:, base:]
        for j in range(width // LANES):
            sum_ref[2 * width + j * base : 2 * width + (j + 1) * base, :] = gw[:, j * LANES : (j + 1) * LANES]
        done = acc[...].sum(axis=1)
        rows_ = chan[...]
        extra = jnp.concatenate(
            [done[0:1], -done[1:2] / (1.0 - par(SLOPE_IN)), jnp.zeros((2, width), f32), done[2:5],
             jnp.zeros((9, width), f32)], axis=0)
        rows_ = rows_ + extra
        at0 = 2 * width + 4 * base
        for j in range(width // LANES):
            sum_ref[at0 + j * 16 : at0 + (j + 1) * 16, :] = rows_[:, j * LANES : (j + 1) * LANES]
        at1 = at0 + 64
        bias = bias_ref[...].sum(axis=0, keepdims=True)
        tail = jnp.concatenate([bias[:, 0:base], bias[:, base:], jnp.zeros((6, base), f32)], axis=0)
        sum_ref[at1 : at1 + 8, :] = tail
        sum_ref[at1 + 8 :, :] = jnp.zeros((sum_ref.shape[0] - at1 - 8, LANES), f32)


def sum_rows(size):
    return -(-size // 256) * 256


def exchange(x, axis):
    return lax.all_to_all(x, axis, 0, 0)


def reduce_all(x, sizes):
    steps = []
    for axis in ("item", "tm"):
        by = 1
        while by < sizes[axis]:
            steps.append((axis, by))
            by *= 2
    order = sorted(steps, key=lambda s: (s[1], s[0]))

    def swap(y, axis, by):
        return lax.ppermute(y, axis, [(d, d ^ by) for d in range(sizes[axis])])

    for axis, by in order:
        half = x.shape[0] // 2
        mine = (lax.axis_index(axis) // by) % 2
        keep = lax.dynamic_slice_in_dim(x, mine * half, half)
        send = lax.dynamic_slice_in_dim(x, (1 - mine) * half, half)
        x = keep + swap(send, axis, by)
    for axis, by in order[::-1]:
        mine = (lax.axis_index(axis) // by) % 2
        other = swap(x, axis, by)
        x = jnp.where(mine == 0, jnp.concatenate([x, other]), jnp.concatenate([other, x]))
    return x


def whole(shape):
    return pl.BlockSpec(shape, lambda i: (0,) * len(shape))


def per_item(shape):
    return pl.BlockSpec((1,) + shape, lambda i: (i,) + (0,) * len(shape))


SMEM = pl.BlockSpec(memory_space=pltpu.SMEM)


def body(
    inputs, lengths, counts, weight_in, bias_in, slope_in, gain_in, shift_in, channelwise_taps, channelwise_bias,
    slope_out, gain_out, shift_out, weight_res, bias_res, weight_skip, bias_skip, grad_residual, grad_skip,
):
    items, frames, base = inputs.shape
    width = weight_in.shape[1]
    sources = grad_skip.shape[1]
    tm, across = lax.axis_size("tm"), lax.axis_size("item")
    place = lax.axis_index("tm").astype(jnp.int32).reshape(1)
    up = [(d, d + 1) for d in range(tm - 1)]
    down = [(d + 1, d) for d in range(tm - 1)]
    x_before = lax.ppermute(inputs[:, frames - TAP :], "tm", up)
    x_after = lax.ppermute(inputs[:, :TAP], "tm", down)

    table = jnp.concatenate(
        [jnp.stack([bias_in, slope_in, gain_in, shift_in]), channelwise_taps,
         jnp.stack([channelwise_bias, slope_out, gain_out, shift_out]), jnp.zeros((5, width), f32)], axis=0)
    params = pltpu.CompilerParams(vmem_limit_bytes=VMEM)

    v1, st1 = pl.pallas_call(
        functools.partial(first_kernel, min(512, frames)),
        grid=(items,),
        in_specs=[SMEM, SMEM, per_item((frames, base)), whole((base, width)), whole((16, width))],
        out_specs=[per_item((frames, width)), whole((tm, items, LANES))],
        out_shape=[jax.ShapeDtypeStruct((items, frames, width), f32), jax.ShapeDtypeStruct((tm, items, LANES), f32)],
        scratch_shapes=[pltpu.VMEM((3 * base, width), bf16)],
        compiler_params=params,
        name="first",
    )(lengths, place, inputs, weight_in, table)
    ga1 = exchange(st1, "tm")

    rows = 256
    big = jax.ShapeDtypeStruct((items, frames, width), f32)
    f0, f1, f2, z, y, ch, st2, bias = pl.pallas_call(
        functools.partial(second_kernel, rows),
        grid=(items,),
        in_specs=[SMEM, SMEM, SMEM, per_item((frames, width)), per_item((TAP, base)), per_item((TAP, base)),
                  per_item((frames, base)), per_item((sources, frames, base)), whole((base, width)),
                  whole((width, base)), whole((width, base)), whole((16, width)), whole((tm, items, LANES))],
        out_specs=[per_item((frames, width))] * 3 + [per_item((frames, 2 * base)), per_item((2 * base, width)),
                   per_item((ROWS, width)), whole((tm, items, LANES)), whole((8, 2 * base))],
        out_shape=[big, big, big, jax.ShapeDtypeStruct((items, frames, 2 * base), f32),
                   jax.ShapeDtypeStruct((items, 2 * base, width), f32), jax.ShapeDtypeStruct((items, ROWS, width), f32),
                   jax.ShapeDtypeStruct((tm, items, LANES), f32), jax.ShapeDtypeStruct((8, 2 * base), f32)],
        scratch_shapes=[pltpu.VMEM((3 * base, width), bf16), pltpu.VMEM((6 * base, width), bf16),
                        pltpu.VMEM((3 * width, 2 * base), bf16), pltpu.VMEM((2, items, LANES), f32),
                        pltpu.VMEM((frames + 2 * TAP, width), f32), pltpu.VMEM((8, LANES), f32),
                        pltpu.VMEM((8, LANES), f32), pltpu.VMEM((ROWS, 8, width), f32),
                        pltpu.VMEM((2 * base, width), f32)],
        compiler_params=params,
        name="second",
    )(lengths, counts, place, v1, x_before, x_after, grad_residual, grad_skip, weight_in, weight_res, weight_skip,
      table, ga1)
    ga2 = exchange(st2, "tm")

    n_sum = sum_rows(2 * width + 4 * base + 64 + 8)
    out = jax.ShapeDtypeStruct((items, frames, base), f32)
    biases = jnp.stack([bias_res, bias_skip])
    res, skip, gin, side, sums = pl.pallas_call(
        functools.partial(third_kernel, rows),
        grid=(items,),
        in_specs=[SMEM, SMEM, per_item((frames, width)), per_item((TAP, base)), per_item((frames, base)),
                  per_item((TAP, base)), per_item((frames, width)), per_item((frames, width)),
                  per_item((frames, width)), per_item((frames, base)), per_item((frames, 2 * base)),
                  per_item((2 * base, width)), whole((items, ROWS, width)), whole((8, 2 * base)),
                  whole((base, width)), whole((width, base)), whole((width, base)), whole((2, base)),
                  whole((16, width)), whole((tm, items, LANES)), whole((tm, items, LANES))],
        out_specs=[per_item((frames, base))] * 3 + [pl.BlockSpec((2, 1, TAP, base), lambda i: (0, i, 0, 0)),
                   whole((n_sum, base))],
        out_shape=[out, out, out, jax.ShapeDtypeStruct((2, items, TAP, base), f32),
                   jax.ShapeDtypeStruct((n_sum, base), f32)],
        scratch_shapes=[pltpu.VMEM((3 * base, width), bf16), pltpu.VMEM((3 * width, base), bf16),
                        pltpu.VMEM((6, items, LANES), f32), pltpu.VMEM((3, items, width), f32),
                        pltpu.VMEM((16, width), f32), pltpu.VMEM((items, 2 * base), f32),
                        pltpu.VMEM((frames + 4 * TAP, width), f32), pltpu.VMEM((8, LANES), f32),
                        pltpu.VMEM((base, width), f32), pltpu.VMEM((2 * base, width), f32),
                        pltpu.VMEM((8, 8, width), f32)],
        compiler_params=params,
        name="third",
    )(lengths, place, v1, x_before, inputs, x_after, f0, f1, f2, grad_residual, z, y, ch, bias, weight_in, weight_res,
      weight_skip, biases, table, ga1, ga2)

    from_next = lax.ppermute(side[0], "tm", down)
    from_last = lax.ppermute(side[1], "tm", up)
    total = reduce_all(sums, {"tm": tm, "item": across})
    gin = gin.at[:, frames - TAP :].add(from_next)
    gin = gin.at[:, :TAP].add(from_last)

    g_res, g_skip = total[0:width], total[width : 2 * width]
    at0 = 2 * width + 4 * base
    g_in = total[2 * width : at0].reshape(4, base, LANES).transpose(1, 0, 2).reshape(base, width)
    vec = total[at0 : at0 + 64].reshape(4, 16, LANES).transpose(1, 0, 2).reshape(16, width)
    return (
        res, skip, gin, g_in, vec[0], vec[1], vec[2], vec[3], vec[4:7], vec[7], vec[8], vec[9], vec[10],
        g_res, total[at0 + 64], g_skip, total[at0 + 65],
    )


def solution(mesh):
    spread = P("item", "tm", None)
    return jax.shard_map(
        body,
        mesh=mesh,
        in_specs=(spread, P("item"), P("item")) + (P(),) * 14 + (spread, P("item", None, "tm", None)),
        out_specs=(spread,) * 3 + (P(),) * 14,
        check_vma=False,
    )
```

time: 836 us -> 276 us (0.33)
  other arithmetic: 242 us -> 5.61 us
  matrix products: 206 us -> 0 us
  Pallas kernels: 0 us -> 172 us
  blocking collectives: 154 us -> 0 us
  waiting for transfers between devices: 180 us -> 59 us
  starting transfers between devices: 11.5 us -> 27.7 us
  between operations: 14.8 us -> 0.92 us
  local copies, waits for them, and re-layouts: 20.8 us -> 10.2 us
    reduce_sum x10 -> x0, other arithmetic: 211 us -> none  [the longest x2 59.1 us: norm_forward(): total = jnp.sum(value * mask, axis=(1, 2))]
    dot_general x9 -> x0, matrix products: 206 us -> none  [the longest x6 121 us: project(): jnp.dot(left, right, precision=highest, preferred_element_type=jnp.float32)]
    pallas_call x0 -> x3, Pallas kernels: none -> 172 us  [the longest x1 81.7 us: body(): pl.pallas_call(functools.partial(second_kernel, rows), grid=(items,), in_...]
    psum x7 -> x0, blocking collectives: 154 us -> none  [the longest x2 42.8 us: norm_forward(): mean = lax.psum(total, 'tm') / count]
    psum x1 -> x0, waiting for transfers between devices: 71.7 us -> none  [body(): lax.psum((grad_weight_in, grad_bias_in, grad_slope_in, grad_gain_in, grad...]
    ppermute x4 -> x14, waiting for transfers between devices: 108 us -> 46.3 us  [the longest x10 38.7 us: swap(): return lax.ppermute(y, axis, [(d, d ^ by) for d in range(sizes[axis])])]
    mul x4 -> x0, other arithmetic: 29.7 us -> none  [the longest x1 19.3 us: body(): channelwise_taps[0] * grad_convolved[:, TAP_SPACING:]]
    unnamed x91 -> x14, local copies, waits for them, and re-layouts: 18 us -> 1.58 us
  transfers between devices with their start and end apart: 5 -> 16, of which waited for: 4 -> 12; matrix products, arithmetic and copies ran while one was open for 8% -> 3% of each run, Pallas kernels for 0% -> 6%
where the time goes in v1:
time: 276 us; the launch traced here: 275 us
  Pallas kernels  172 us (62%)
  waiting for transfers between devices  59 us (21%)
  starting transfers between devices  27.7 us (10%)
  local copies, waits for them, and re-layouts  10.2 us (4%)
  other arithmetic  5.61 us (2%)
    pallas_call x1, Pallas kernels, body(): pl.pallas_call(functools.partial(second_kernel, rows), grid=(items,), in_...  81.7 us
    pallas_call x1, Pallas kernels, body(): pl.pallas_call(functools.partial(third_kernel, rows), grid=(items,), in_s...  72 us
    ppermute x10, waiting for transfers between devices, swap(): return lax.ppermute(y, axis, [(d, d ^ by) for d in range(sizes[axis])])  38.7 us
    pallas_call x1, Pallas kernels, body(): pl.pallas_call(functools.partial(first_kernel, min(512, frames)), grid=(i...  17.9 us
    all_to_all x2, waiting for transfers between devices, exchange(): return lax.all_to_all(x, axis, 0, 0)  12.7 us
    all_to_all x2, starting transfers between devices, exchange(): return lax.all_to_all(x, axis, 0, 0)  10.3 us
    ppermute x1, waiting for transfers between devices, body(): from_last = lax.ppermute(side[1], 'tm', up)  7.56 us
    ppermute x10, starting transfers between devices, swap(): return lax.ppermute(y, axis, [(d, d ^ by) for d in range(sizes[axis])])  7.29 us
  transfers between devices with their start and end apart: 16, of which 12 were waited for; matrix products, arithmetic and copies ran while one was open for 3% of the time, Pallas kernels for 6%

profile of v1, /device:TPU:0, one launch (start us, length us, event | category | flops | bytes accessed | tf_op | source)
XLA Modules:
  0.0 275.0 jit_solution(5703781213626311668)
XLA Ops:
  0.7 1.3 fusion.1
  2.0 4.9 %collective-permute-start = (f32[8,128,128]{2,1,0:T(8,128)S(1)}, f32[8,128,128]{2,1,0:T(8,128)S(1)}, u32[]{:S(2)}, u32[]{:S(2)}) collective-permute-start(f32[8,128,128]{2,1,0:T(8,128)S(1)} %get-tuple-element.72), channel_id=1, source_target_pairs={{0,4},{4,8},{8,12},{12,16},{16,20},{20,24},{24,28},{1,5},{5,9},{9,... | collective-permute-start | bytes 1572872 | tf_op jit(solution)/shard_map/ppermute | solution.py:538
  6.8 1.3 collective-permute-start.1
  8.2 2.7 concatenate.37.pc_ref
  10.9 17.9 %first.1 = (f32[8,1024,512]{2,1,0:T(8,128)}, f32[8,8,128]{2,1,0:T(8,128)}) custom-call(s32[8]{0:T(128)} %len_ref.5, s32[1]{0:T(128)} %bitcast.tm_ref, f32[8,1024,128]{2,1,0:T(8,128)} %x_ref.3, f32[128,512]{1,0:T(8,128)} %w_ref.5, f32[16,512]{1,0:T(8,128)} %concatenate.37.pc_ref), custom_call_target="tpu_custom_call" | custom-call | tf_op jit(solution)/shard_map/first/pallas_call | solution.py:546
  28.7 7.0 %all-to-all-start = ((f32[8,8,128]{2,1,0:T(8,128)}), f32[8,8,128]{2,1,0:T(8,128)S(1)}, u32[]{:S(2)}, u32[]{:S(2)}) async-start(f32[8,8,128]{2,1,0:T(8,128)} %get-tuple-element.57), calls=%async_computation | async-start | bytes 65536 | tf_op jit(solution)/shard_map/all_to_all | solution.py:488
  35.7 6.7 %all-to-all-done.ga_ref.ga1_ref = f32[8,8,128]{2,1,0:T(8,128)S(1)} async-done(((f32[8,8,128]{2,1,0:T(8,128)}), f32[8,8,128]{2,1,0:T(8,128)S(1)}, u32[]{:S(2)}, u32[]{:S(2)}) %all-to-all-start) | async-done | bytes 32800 | tf_op jit(solution)/shard_map/all_to_all | solution.py:488
  42.4 0.0 copy-start.3
  42.4 0.0 collective-permute-done.xb_ref
  42.4 0.0 copy-start
  42.4 0.0 collective-permute-done.1.xa_ref
  42.4 0.0 copy-start.1
  42.4 0.6 copy-done.3
  43.0 0.2 copy-done
  43.2 0.2 copy-done.1
  43.3 0.0 copy-start.5
  43.3 0.0 copy-start.6
  43.4 81.7 %second.1 = (f32[8,1024,512]{2,1,0:T(8,128)}, f32[8,1024,512]{2,1,0:T(8,128)}, f32[8,1024,512]{2,1,0:T(8,128)}, f32[8,1024,256]{2,1,0:T(8,128)}, f32[8,256,512]{...) custom-call(s32[8]{0:T(128)} %len_ref.5, s32[8]{0:T(128)} %cnt_ref.1, ...), custom_call_target="tpu_custom_call" | custom-call | tf_op jit(solution)/shard_map/second/pallas_call | solution.py:560
  125.0 3.4 %all-to-all-start.1 = ((f32[8,8,128]{2,1,0:T(8,128)}), f32[8,8,128]{2,1,0:T(8,128)S(1)}, u32[]{:S(2)}, u32[]{:S(2)}) async-start(f32[8,8,128]{2,1,0:T(8,128)} %get-tuple-element.65), calls=%async_computation.1 | async-start | bytes 65536 | tf_op jit(solution)/shard_map/all_to_all | solution.py:488
  128.4 0.0 copy-done.5
  128.4 0.0 copy-done.6
  128.4 0.6 pad_maximum_fusion.br_ref
  129.0 6.0 %all-to-all-done.1.ga2_ref = f32[8,8,128]{2,1,0:T(8,128)S(1)} async-done(((f32[8,8,128]{2,1,0:T(8,128)}), f32[8,8,128]{2,1,0:T(8,128)S(1)}, u32[]{:S(2)}, u32[]{:S(2)}) %all-to-all-start.1) | async-done | bytes 32800 | tf_op jit(solution)/shard_map/all_to_all | solution.py:488
  135.0 0.0 copy-start.4
  135.0 0.6 copy-done.4
  135.6 72.0 %third.1 = (f32[8,1024,128]{2,1,0:T(8,128)}, f32[8,1024,128]{2,1,0:T(8,128)}, f32[8,1024,128]{2,1,0:T(8,128)}, f32[2,8,128,128]{3,2,1,0:T(8,128)}, f32[1792,128]{1,0:T(8,128)}) custom-call(s32[8]{0:T(128)} %len_ref.5, s32[1]{0:T(128)} %bitcast.tm_ref, f32[8,1024,512]{2,1,0:T(8,128)} %get-tuple-element.56.v_ref, f32[8,128,128]{2,1,0:T(8,128)} %copy-done, ...), custom_call_target="tpu_custom_call" | custom-call | tf_op jit(solution)/shard_map/third/pallas_call | solution.py:585
  207.7 0.0 copy-start.2
  207.7 1.1 constant_dynamic-slice_fusion.4
  208.8 0.1 collective-permute-start.4
  208.9 1.8 collective-permute-done.4
  210.7 1.1 dynamic-slice_add_fusion
  211.8 0.5 collective-permute-start.5
  212.3 7.2 %collective-permute-done.5 = f32[448,128]{1,0:T(8,128)S(1)} collective-permute-done((f32[448,128]{1,0:T(8,128)S(1)}, f32[448,128]{1,0:T(8,128)S(1)}, u32[]{:S(2)}, u32[]{:S(2)}) %collective-permute-start.5) | collective-permute-done | bytes 229408 | tf_op jit(solution)/shard_map/ppermute | solution.py:501
  219.6 1.6 collective-permute-start.6
  221.2 3.3 %collective-permute-done.6 = f32[224,128]{1,0:T(8,128)S(1)} collective-permute-done((f32[224,128]{1,0:T(8,128)S(1)}, f32[224,128]{1,0:T(8,128)S(1)}, u32[]{:S(2)}, u32[]{:S(2)}) %collective-permute-start.6) | collective-permute-done | bytes 114720 | tf_op jit(solution)/shard_map/ppermute | solution.py:501
  224.5 0.5 collective-permute-start.7
  224.9 3.8 %collective-permute-done.7 = f32[112,128]{1,0:T(8,128)S(1)} collective-permute-done((f32[112,128]{1,0:T(8,128)S(1)}, f32[112,128]{1,0:T(8,128)S(1)}, u32[]{:S(2)}, u32[]{:S(2)}) %collective-permute-start.7) | collective-permute-done | bytes 57376 | tf_op jit(solution)/shard_map/ppermute | solution.py:501
  228.7 0.6 collective-permute-start.8
  229.3 4.7 %collective-permute-done.8 = f32[56,128]{1,0:T(8,128)S(1)} collective-permute-done((f32[56,128]{1,0:T(8,128)S(1)}, f32[56,128]{1,0:T(8,128)S(1)}, u32[]{:S(2)}, u32[]{:S(2)}) %collective-permute-start.8) | collective-permute-done | bytes 28704 | tf_op jit(solution)/shard_map/ppermute | solution.py:501
  234.0 0.2 collective-permute-start.9
  234.2 4.6 %collective-permute-done.9 = f32[56,128]{1,0:T(8,128)S(1)} collective-permute-done((f32[56,128]{1,0:T(8,128)S(1)}, f32[56,128]{1,0:T(8,128)S(1)}, u32[]{:S(2)}, u32[]{:S(2)}) %collective-permute-start.9) | collective-permute-done | bytes 28704 | tf_op jit(solution)/shard_map/ppermute | solution.py:501
  238.8 0.2 collective-permute-start.10
  239.1 4.0 %collective-permute-done.10 = f32[112,128]{1,0:T(8,128)S(1)} collective-permute-done((f32[112,128]{1,0:T(8,128)S(1)}, f32[112,128]{1,0:T(8,128)S(1)}, u32[]{:S(2)}, u32[]{:S(2)}) %collective-permute-start.10) | collective-permute-done | bytes 57376 | tf_op jit(solution)/shard_map/ppermute | solution.py:501
  243.1 2.2 collective-permute-start.11
  245.3 0.0 copy-done.2
  245.3 0.1 slice_bitcast_fusion
  245.3 1.3 collective-permute-start.2
  246.6 1.4 collective-permute-done.11
  248.1 1.3 collective-permute-start.12
  249.4 2.7 collective-permute-start.3
  252.1 8.1 %collective-permute-done.12 = f32[448,128]{1,0:T(8,128)S(1)} collective-permute-done((f32[448,128]{1,0:T(8,128)S(1)}, f32[448,128]{1,0:T(8,128)S(1)}, u32[]{:S(2)}, u32[]{:S(2)}) %collective-permute-start.12) | collective-permute-done | bytes 229408 | tf_op jit(solution)/shard_map/ppermute | solution.py:501
  260.2 0.1 collective-permute-start.13
  260.3 0.0 collective-permute-done.2
  260.3 1.9 add_dynamic-update-slice_fusion
  262.2 7.6 %collective-permute-done.3 = f32[8,128,128]{2,1,0:T(8,128)S(1)} collective-permute-done((f32[8,128,128]{2,1,0:T(8,128)S(1)}, f32[8,128,128]{2,1,0:T(8,128)S(1)}, u32[]{:S(2)}, u32[]{:S(2)}) %collective-permute-start.3) | collective-permute-done | bytes 524320 | tf_op jit(solution)/shard_map/ppermute | solution.py:610
  269.7 1.9 fusion
  271.6 0.0 collective-permute-done.13
  271.6 0.1 maximum_select_fusion
  271.7 0.8 fusion.2
  272.5 0.6 fusion.3
  273.2 0.6 slice_bitcast_fusion.2
  273.8 0.5 slice_bitcast_fusion.3
  274.3 0.7 copy.40
  (14 shorter events, 0.2 us)
Async XLA Ops:
  2.0 40.4 %collective-permute-start = (f32[8,128,128]{2,1,0:T(8,128)S(1)}, f32[8,128,128]{2,1,0:T(8,128)S(1)}, u32[]{:S(2)}, u32[]{:S(2)}) collective-permute-start(f32[8,128,128]{2,1,0:T(8,128)S(1)} %get-tuple-element.72), channel_id=1, source_target_pairs={{0,4},{4,8},{8,12},{12,16},{16,20},{20,24},{24,28},{1,5},{5,9},{9,... | collective-permute-start | bytes 1572872 | tf_op jit(solution)/shard_map/ppermute | solution.py:538
  6.8 35.5 %collective-permute-start.1 = (f32[8,128,128]{2,1,0:T(8,128)S(1)}, f32[8,128,128]{2,1,0:T(8,128)S(1)}, u32[]{:S(2)}, u32[]{:S(2)}) collective-permute-start(f32[8,128,128]{2,1,0:T(8,128)S(1)} %get-tuple-element.71), channel_id=1, source_target_pairs={{4,0},{8,4},{12,8},{16,12},{20,16},{24,20},{28,24},{5,1},{9,5},{13... | collective-permute-start | bytes 1572872 | tf_op jit(solution)/shard_map/ppermute | solution.py:539
  28.7 13.6 %all-to-all-start = ((f32[8,8,128]{2,1,0:T(8,128)}), f32[8,8,128]{2,1,0:T(8,128)S(1)}, u32[]{:S(2)}, u32[]{:S(2)}) async-start(f32[8,8,128]{2,1,0:T(8,128)} %get-tuple-element.57), calls=%async_computation | async-start | bytes 65536 | tf_op jit(solution)/shard_map/all_to_all | solution.py:488
  42.4 0.6 copy-start.3
  42.4 0.8 copy-start
  42.4 1.0 copy-start.1
  43.3 85.0 %copy-start.5 = (f32[128]{0:T(128)S(1)}, f32[128]{0:T(128)}, u32[]{:S(2)}) copy-start(f32[128]{0:T(128)} %param.39) | copy-start | bytes 1540
  43.3 85.0 %copy-start.6 = (f32[128]{0:T(128)S(1)}, f32[128]{0:T(128)}, u32[]{:S(2)}) copy-start(f32[128]{0:T(128)} %param.37) | copy-start | bytes 1540
  125.0 10.0 %all-to-all-start.1 = ((f32[8,8,128]{2,1,0:T(8,128)}), f32[8,8,128]{2,1,0:T(8,128)S(1)}, u32[]{:S(2)}, u32[]{:S(2)}) async-start(f32[8,8,128]{2,1,0:T(8,128)} %get-tuple-element.65), calls=%async_computation.1 | async-start | bytes 65536 | tf_op jit(solution)/shard_map/all_to_all | solution.py:488
  135.0 0.6 copy-start.4
  207.7 37.6 %copy-start.2 = (f32[2,8,128,128]{3,2,1,0:T(8,128)S(1)}, f32[2,8,128,128]{3,2,1,0:T(8,128)}, u32[]{:S(2)}) copy-start(f32[2,8,128,128]{3,2,1,0:T(8,128)} %get-tuple-element.69) | copy-start | bytes 3145732
  208.8 1.9 collective-permute-start.4
  211.8 7.7 %collective-permute-start.5 = (f32[448,128]{1,0:T(8,128)S(1)}, f32[448,128]{1,0:T(8,128)S(1)}, u32[]{:S(2)}, u32[]{:S(2)}) collective-permute-start(f32[448,128]{1,0:T(8,128)S(1)} %constant_dynamic-slice_fusion.3), channel_id=1, source_target_pairs={{0,4},{4,0},{8,12},{12,8},{16,20},{20,16},{24,28},{28,24},{1,5},{5... | collective-permute-start | bytes 688136 | tf_op jit(solution)/shard_map/ppermute | solution.py:501
  219.6 4.9 %collective-permute-start.6 = (f32[224,128]{1,0:T(8,128)S(1)}, f32[224,128]{1,0:T(8,128)S(1)}, u32[]{:S(2)}, u32[]{:S(2)}) collective-permute-start(f32[224,128]{1,0:T(8,128)S(1)} %constant_dynamic-slice_fusion.2), channel_id=1, source_target_pairs={{0,2},{1,3},{2,0},{3,1},{4,6},{5,7},{6,4},{7,5},{8,10},{9,11},{10,... | collective-permute-start | bytes 344072 | tf_op jit(solution)/shard_map/ppermute | solution.py:501
  224.5 4.2 %collective-permute-start.7 = (f32[112,128]{1,0:T(8,128)S(1)}, f32[112,128]{1,0:T(8,128)S(1)}, u32[]{:S(2)}, u32[]{:S(2)}) collective-permute-start(f32[112,128]{1,0:T(8,128)S(1)} %constant_dynamic-slice_fusion.1), channel_id=1, source_target_pairs={{0,8},{4,12},{8,0},{12,4},{16,24},{20,28},{24,16},{28,20},{1,9},{5... | collective-permute-start | bytes 172040 | tf_op jit(solution)/shard_map/ppermute | solution.py:501
  228.7 5.3 %collective-permute-start.8 = (f32[56,128]{1,0:T(8,128)S(1)}, f32[56,128]{1,0:T(8,128)S(1)}, u32[]{:S(2)}, u32[]{:S(2)}) collective-permute-start(f32[56,128]{1,0:T(8,128)S(1)} %constant_dynamic-slice_fusion), channel_id=1, source_target_pairs={{0,16},{4,20},{8,24},{12,28},{16,0},{20,4},{24,8},{28,12},{1,17},{... | collective-permute-start | bytes 86024 | tf_op jit(solution)/shard_map/ppermute | solution.py:501
  234.0 4.8 %collective-permute-start.9 = (f32[56,128]{1,0:T(8,128)S(1)}, f32[56,128]{1,0:T(8,128)S(1)}, u32[]{:S(2)}, u32[]{:S(2)}) collective-permute-start(f32[56,128]{1,0:T(8,128)S(1)} %dynamic-slice_add_fusion.4), channel_id=1, source_target_pairs={{0,16},{4,20},{8,24},{12,28},{16,0},{20,4},{24,8},{28,12},{1,17},{... | collective-permute-start | bytes 86024 | tf_op jit(solution)/shard_map/ppermute | solution.py:501
  238.8 4.2 %collective-permute-start.10 = (f32[112,128]{1,0:T(8,128)S(1)}, f32[112,128]{1,0:T(8,128)S(1)}, u32[]{:S(2)}, u32[]{:S(2)}) collective-permute-start(f32[112,128]{1,0:T(8,128)S(1)} %maximum_select_fusion.4), channel_id=1, source_target_pairs={{0,8},{4,12},{8,0},{12,4},{16,24},{20,28},{24,16},{28,20},{1,9},{5... | collective-permute-start | bytes 172040 | tf_op jit(solution)/shard_map/ppermute | solution.py:501
  243.1 5.0 %collective-permute-start.11 = (f32[224,128]{1,0:T(8,128)S(1)}, f32[224,128]{1,0:T(8,128)S(1)}, u32[]{:S(2)}, u32[]{:S(2)}) collective-permute-start(f32[224,128]{1,0:T(8,128)S(1)} %maximum_select_fusion.3), channel_id=1, source_target_pairs={{0,2},{1,3},{2,0},{3,1},{4,6},{5,7},{6,4},{7,5},{8,10},{9,11},{10,... | collective-permute-start | bytes 344072 | tf_op jit(solution)/shard_map/ppermute | solution.py:501
  245.3 14.9 %collective-permute-start.2 = (f32[8,128,128]{2,1,0:T(8,128)S(1)}, f32[8,128,128]{2,1,0:T(8,128)S(1)}, u32[]{:S(2)}, u32[]{:S(2)}) collective-permute-start(f32[8,128,128]{2,1,0:T(8,128)S(1)} %get-tuple-element.74), channel_id=1, source_target_pairs={{4,0},{8,4},{12,8},{16,12},{20,16},{24,20},{28,24},{5,1},{9,5},{13... | collective-permute-start | bytes 1572872 | tf_op jit(solution)/shard_map/ppermute | solution.py:609
  248.1 12.1 %collective-permute-start.12 = (f32[448,128]{1,0:T(8,128)S(1)}, f32[448,128]{1,0:T(8,128)S(1)}, u32[]{:S(2)}, u32[]{:S(2)}) collective-permute-start(f32[448,128]{1,0:T(8,128)S(1)} %maximum_select_fusion.2), channel_id=1, source_target_pairs={{0,4},{4,0},{8,12},{12,8},{16,20},{20,16},{24,28},{28,24},{1,5},{5... | collective-permute-start | bytes 688136 | tf_op jit(solution)/shard_map/ppermute | solution.py:501
  249.4 20.4 %collective-permute-start.3 = (f32[8,128,128]{2,1,0:T(8,128)S(1)}, f32[8,128,128]{2,1,0:T(8,128)S(1)}, u32[]{:S(2)}, u32[]{:S(2)}) collective-permute-start(f32[8,128,128]{2,1,0:T(8,128)S(1)} %get-tuple-element.73), channel_id=1, source_target_pairs={{0,4},{4,8},{8,12},{12,16},{16,20},{20,24},{24,28},{1,5},{5,9},{9,... | collective-permute-start | bytes 1572872 | tf_op jit(solution)/shard_map/ppermute | solution.py:610
  260.2 11.4 %collective-permute-start.13 = (f32[896,128]{1,0:T(8,128)S(1)}, f32[896,128]{1,0:T(8,128)S(1)}, u32[]{:S(2)}, u32[]{:S(2)}) collective-permute-start(f32[896,128]{1,0:T(8,128)S(1)} %maximum_select_fusion.1), channel_id=1, source_target_pairs={{0,1},{1,0},{2,3},{3,2},{4,5},{5,4},{6,7},{7,6},{8,9},{9,8},{10,11... | collective-permute-start | bytes 1376264 | tf_op jit(solution)/shard_map/ppermute | solution.py:501

commit v2 on v1

v2 whole, which is shorter than its diff:
```python
import functools

import jax
import jax.numpy as jnp
from jax import lax
from jax.experimental import pallas as pl
from jax.experimental.pallas import tpu as pltpu
from jax.sharding import PartitionSpec as P

TAP = 128
LANES = 128
EPSILON = 1e-05
LN2 = 0.6931471805599453
f32 = jnp.float32
bf16 = jnp.bfloat16

PARAMS = ("bias_in", "slope_in", "gain_in", "shift_in", "taps", "bias_dw", "slope_out", "gain_out", "shift_out")
(R_P, R_S, R_SS, R_GD, R_GS, R_H0, R_H1, R_H2, R_HF0, R_HF1, R_HF2, R_PF0, R_PF1, R_PF2,
 R_A0, R_A1, R_A2, R_Z0, R_Z1, R_Z2, R_GM) = range(21)
ROWS = 24
SUB = 32
HALF = 128
CHUNK1, CHUNK2, CHUNK3 = 256, 256, 256


def split(x):
    hi = x.astype(bf16)
    lo = (x - hi.astype(f32)).astype(bf16)
    return hi, lo


def dot(a, b):
    return jnp.dot(a, b, preferred_element_type=f32)


def dot0(a, b):
    return lax.dot_general(a, b, (((0,), (0,)), ((), ())), preferred_element_type=f32)


def product3(x, w3):
    hi, lo = split(x)
    return dot(jnp.concatenate([hi, hi, lo], axis=1), w3)


def stacked3(w):
    hi, lo = split(w)
    return jnp.concatenate([hi, lo, hi], axis=0)


def half_act(h, a, c):
    t = jnp.tanh(h)
    return jnp.maximum(h, a * h) - c * jnp.log2(1.0 + jnp.abs(t)), t


def fold(x):
    rows, cols = x.shape
    return x.reshape(rows // 8, 8, cols).sum(axis=0)


def mask_rows(first, rows, length):
    row = lax.broadcasted_iota(jnp.int32, (rows, 1), 0) + first
    return ((row >= 0) & (row < length)).astype(f32)


def lane_put(values):
    shape = values[0].shape[:-1] + (LANES,)
    lane = lax.broadcasted_iota(jnp.int32, shape, len(shape) - 1)
    out = jnp.zeros(shape, f32)
    for k, v in enumerate(values):
        out = jnp.where(lane == k, jnp.broadcast_to(v, shape), out)
    return out


def channel(ref):
    def get(name):
        if name.startswith("tap"):
            k = int(name[3])
            return ref["taps"][k : k + 1]
        return ref[name][...]

    return get


def interleave(first, second):
    done = 0
    for n, piece in enumerate(first):
        piece()
        upto = (n + 1) * len(second) // len(first)
        for other in second[done:upto]:
            other()
        done = upto
    for other in second[done:]:
        other()


def blocks(width):
    return [slice(j * LANES, (j + 1) * LANES) for j in range(width // LANES)]


def per_item_column(values):
    row = lax.broadcasted_iota(jnp.int32, (len(values), 1), 0)
    out = jnp.zeros((len(values), 1), f32)
    for k, v in enumerate(values):
        out = jnp.where(row == k, v, out)
    return out


def frames_here(len_ref, start, frames, items):
    return per_item_column([jnp.clip(len_ref[k] - start, 0, frames).astype(f32) for k in range(items)])


def first_kernel(rows, len_ref, tm_ref, x_ref, xn_ref, w_ref, b_ref, a_ref, v_ref, st_ref, ch_ref, w3, acc, hb0, hb1):
    i = pl.program_id(0)
    items = ch_ref.shape[0]
    frames, width = v_ref.shape[1:]
    slots = (hb0, hb1)

    @pl.when(i == 0)
    def _():
        w3[...] = stacked3(0.5 * w_ref[...])
        hb0[...] = product3(x_ref[0, 0:rows, :], w3[...])

    length = len_ref[i]
    start = tm_ref[0] * frames
    b, a = 0.5 * b_ref[...], a_ref[...]
    c = (1.0 - a) * (0.5 * LN2)
    centre = half_act(hb0[0:8, :] + b, a, c)[0][0:1]
    parts = frames // rows

    for k in range(parts):
        def step(masked, k=k):
            h, then = slots[k % 2], slots[(k + 1) % 2]
            if masked:
                m = mask_rows(start + k * rows, rows, length)

            def ahead(q):
                x = x_ref[0, (k + 1) * rows + q : (k + 1) * rows + q + HALF, :] if k < parts - 1 else xn_ref[0, q : q + HALF, :]
                then[q : q + HALF, :] = product3(x, w3[...])

            def unit(s):
                total = square = jnp.zeros((8, LANES), f32)
                for q in range(0, rows, SUB):
                    v, _ = half_act(h[q : q + SUB, s] + b[:, s], a[:, s], c[:, s])
                    v_ref[0, k * rows + q : k * rows + q + SUB, s] = v
                    d = v - centre[:, s]
                    dm = d * m[q : q + SUB] if masked else d
                    total = total + fold(dm)
                    square = square + fold(dm * d)
                acc[0, :, s] = total if k == 0 else acc[0, :, s] + total
                acc[1, :, s] = square if k == 0 else acc[1, :, s] + square

            interleave([functools.partial(ahead, q) for q in range(0, rows, HALF)],
                       [functools.partial(unit, s) for s in blocks(width)])

        full = start + (k + 1) * rows <= length
        pl.when(full)(functools.partial(step, False))
        pl.when(jnp.logical_not(full))(functools.partial(step, True))

    ch_ref[pl.ds(i, 1), 0, :] = acc[0].sum(axis=0, keepdims=True)
    ch_ref[pl.ds(i, 1), 1, :] = acc[1].sum(axis=0, keepdims=True)
    ch_ref[pl.ds(i, 1), 2, :] = centre

    @pl.when(i == items - 1)
    def _():
        n = frames_here(len_ref, start, frames, items)
        safe = jnp.maximum(n, 1.0)
        total, square, centre = ch_ref[:, 0, :], ch_ref[:, 1, :], ch_ref[:, 2, :]
        ch_ref[:, 0, :] = total + n * centre
        ch_ref[:, 1, :] = square + 2.0 * centre * total + n * centre * centre
        total = total / safe
        level = centre + c + total
        mean = level.sum(axis=1, keepdims=True) / width
        dev = level - mean
        spread = (square - safe * total * total + safe * dev * dev).sum(axis=1, keepdims=True)
        some = (n > 0).astype(f32)
        st_ref[...] = jnp.broadcast_to(lane_put([2.0 * mean * some, 4.0 * spread * some, n])[None], st_ref.shape)


def merged(gathered, width):
    mean_d, spread_d, n_d = gathered[:, :, 0:1], gathered[:, :, 1:2], gathered[:, :, 2:3]
    n = n_d.sum(axis=0)
    mean = (n_d * mean_d).sum(axis=0) / n
    dev = mean_d - mean[None]
    spread = (spread_d + n_d * width * dev * dev).sum(axis=0)
    count = n * width
    return mean, lax.rsqrt(spread / count + EPSILON), count


def wide(x, width):
    return jnp.broadcast_to(x[:, 0:1], (x.shape[0], width))


def second_kernel(
    rows, len_ref, cnt_ref, tm_ref, v_ref, xb_ref, xa_ref, gr_ref, gk_ref, w_ref, wr_ref, ws_ref, *rest
):
    params, rest = rest[: len(PARAMS)], rest[len(PARAMS) :]
    ga_ref, f0_ref, f1_ref, f2_ref, z_ref, y_ref, ch_ref, st_ref, bias_ref, *rest = rest
    w3, wt3, wg3, stat, fst, acc, gacc, yacc, gs0, gs1, hl0, hl1, gb = rest
    par = channel(dict(zip(PARAMS, params)))
    i = pl.program_id(0)
    items = ch_ref.shape[0]
    frames, width = v_ref.shape[1:]
    base = gr_ref.shape[2]
    parts = frames // rows
    gs_slots, hl_slots = (gs0, gs1), (hl0, hl1)

    @pl.when(i == 0)
    def _():
        w3[...] = stacked3(0.5 * w_ref[...])
        both = jnp.concatenate([wr_ref[...], ws_ref[...]], axis=1)
        wt3[...] = stacked3(both.T)
        gain = 2.0 * par("gain_out")
        wg3[...] = stacked3((both.T * gain).T)
        mean, scale, _ = merged(ga_ref[...], width)
        stat[0] = jnp.broadcast_to(mean, stat.shape[1:])
        stat[1] = jnp.broadcast_to(scale, stat.shape[1:])
        bias_ref[...] = jnp.zeros_like(bias_ref)
        ch_ref[...] = jnp.zeros_like(ch_ref)

    length = len_ref[i]
    start = tm_ref[0] * frames
    mean = wide(stat[0, pl.ds(i, 1), :], width)
    scale = wide(stat[1, pl.ds(i, 1), :], width)
    a1 = par("slope_in")
    c1 = (1.0 - a1) * (0.5 * LN2)
    gain = 2.0 * par("gain_in") * scale
    shift = par("shift_in") + gain * (c1 - 0.5 * mean)
    b1 = 0.5 * par("bias_in")
    alive = [(s < cnt_ref[i]).astype(f32) for s in range(gk_ref.shape[1])]
    taps = [0.5 * par(f"tap{k}") for k in range(3)]
    bias = 0.5 * par("bias_dw")
    a2 = par("slope_out")
    c2 = (1.0 - a2) * (0.5 * LN2)
    d_base, d_gain = 0.5 + 0.5 * a2, 0.5 - 0.5 * a2

    def cotangents(k):
        at = slice(k * rows, (k + 1) * rows)
        g_res = gr_ref[0, at, :]
        g_skip = alive[0] * gk_ref[0, 0, at, :]
        for s in range(1, len(alive)):
            g_skip = g_skip + alive[s] * gk_ref[0, s, at, :]
        return jnp.concatenate([g_res, g_skip], axis=1)

    def spread(k):
        def prepare():
            both = cotangents(k)
            bias_ref[...] += fold(both)
            row = lax.broadcasted_iota(jnp.int32, (rows, 1), 0)
            both = jnp.where(row < length - start - k * rows, both, 0.0)
            gacc[...] = fold(both) if k == 0 else gacc[...] + fold(both)
            ghi, glo = split(both)
            gb[k, 0], gb[k, 1] = ghi, glo

        def multiply(q):
            if q == 0:
                prepare()
            ghi, glo = gb[k, 0, q : q + HALF, :], gb[k, 1, q : q + HALF, :]
            gs_slots[k % 2][q : q + HALF, :] = dot(jnp.concatenate([ghi, ghi, glo], axis=1), wt3[...])

        return [functools.partial(multiply, q) for q in range(0, rows, HALF)]

    def products(k):
        hl = hl_slots[k % 2]

        def out(q):
            hi, lo = hl[0, q : q + HALF, :], hl[1, q : q + HALF, :]
            z_ref[0, k * rows + q : k * rows + q + HALF, :] = dot(jnp.concatenate([hi, hi, lo], axis=1), wg3[...])

        def weights(q):
            at = slice(q, q + base)
            ghi, glo = gb[k, 0, :, at], gb[k, 1, :, at]
            y = dot0(jnp.concatenate([ghi, ghi, glo], axis=0), jnp.concatenate([hl[0], hl[1], hl[0]], axis=0))
            if k == parts - 1:
                y_ref[0, at, :] = yacc[at, :] + y if k else y
            else:
                yacc[at, :] = yacc[at, :] + y if k else y

        return [functools.partial(out, q) for q in range(0, rows, HALF)] + [
            functools.partial(weights, q) for q in (0, base)]

    h = product3(jnp.concatenate([xb_ref[0], xa_ref[0]], axis=0), w3[...])
    for piece in spread(0):
        piece()
    for side, at in ((0, 0), (1, frames + TAP)):
        m = mask_rows(start + at - TAP, TAP, length)
        for s in blocks(width):
            for q in range(0, TAP, SUB):
                v, _ = half_act(h[side * TAP + q : side * TAP + q + SUB, s] + b1[:, s], a1[:, s], c1[:, s])
                fst[at + q : at + q + SUB, s] = m[q : q + SUB] * (gain[:, s] * v + shift[:, s])

    def lift(k, _):
        r0 = pl.multiple_of(k * TAP, TAP)
        full = start + r0 + TAP <= length

        @pl.when(full)
        def _():
            fst[pl.ds(TAP + r0, TAP), :] = gain * v_ref[0, pl.ds(r0, TAP), :] + shift

        @pl.when(jnp.logical_not(full))
        def _():
            m = mask_rows(start + r0, TAP, length)
            fst[pl.ds(TAP + r0, TAP), :] = m * (gain * v_ref[0, pl.ds(r0, TAP), :] + shift)

        return 0

    lax.fori_loop(0, frames // TAP, lift, 0)

    def halved(r, size, s):
        return (
            taps[0][:, s] * fst[r : r + size, s]
            + taps[1][:, s] * fst[r + TAP : r + TAP + size, s]
            + taps[2][:, s] * fst[r + 2 * TAP : r + 2 * TAP + size, s]
            + bias[:, s]
        )

    point = jnp.concatenate(
        [half_act(halved(0, 8, s), a2[:, s], c2[:, s])[0][0:1] for s in blocks(width)], axis=1
    )
    tracked = [r for r in range(R_S, R_A0) if r != R_GS]

    def elementwise(k, masked):
        gs, hl = gs_slots[k % 2], hl_slots[k % 2]
        if masked:
            m = mask_rows(start + k * rows, rows, length)

        def unit(s, begin):
            zero = jnp.zeros((8, LANES), f32)
            sums = {r: zero for r in tracked}
            for q in range(begin, begin + HALF, SUB):
                at = slice(k * rows + q, k * rows + q + SUB)
                f = halved(k * rows + q, SUB, s)
                v, t = half_act(f, a2[:, s], c2[:, s])
                dm = d_base[:, s] + d_gain[:, s] * t
                d = v - point[:, s]
                g = gs[q : q + SUB, s]
                dd, fm = d, f
                if masked:
                    mq = m[q : q + SUB]
                    dm, dd, fm = dm * mq, d * mq, f * mq
                f0 = g * dm
                f2 = d * dm
                f0_ref[0, at, s] = f0
                f1_ref[0, at, s] = dm
                f2_ref[0, at, s] = f2
                for r, x in (
                    (R_S, dd), (R_SS, dd * d), (R_GD, g * d), (R_H0, f0), (R_H1, dm), (R_H2, f2), (R_HF0, f0 * f),
                    (R_HF1, dm * f), (R_HF2, f2 * f), (R_PF0, g * f), (R_PF1, fm), (R_PF2, dd * f),
                ):
                    sums[r] = sums[r] + fold(x)
                hi, lo = split(d)
                hl[0, q : q + SUB, s] = hi
                hl[1, q : q + SUB, s] = lo
            for r, x in sums.items():
                acc[r, :, s] = x if k == 0 and begin == 0 else acc[r, :, s] + x

        return [functools.partial(unit, s, q) for q in range(0, rows, HALF) for s in blocks(width)]

    def nothing(k):
        at = slice(k * rows, (k + 1) * rows)
        zero = jnp.zeros((rows, width), f32)
        for ref in (f0_ref, f1_ref, f2_ref):
            ref[0, at, :] = zero
        hl_slots[k % 2][...] = jnp.zeros_like(hl0)
        if k == 0:
            for r in tracked:
                acc[r] = jnp.zeros((8, width), f32)

    for k in range(parts):
        def step(kind, k=k):
            matrix = (spread(k + 1) if k + 1 < parts else []) + (products(k - 1) if k > 0 else [])
            interleave(matrix, [functools.partial(nothing, k)] if kind == "none" else elementwise(k, kind == "some"))

        t0 = start + k * rows
        full, none = t0 + rows <= length, t0 >= length
        pl.when(full)(functools.partial(step, "full"))
        pl.when(jnp.logical_not(full | none))(functools.partial(step, "some"))
        pl.when(none)(functools.partial(step, "none"))
    for piece in products(parts - 1):
        piece()

    edges = acc.at[pl.ds(R_A0, 6)]
    edges[...] = jnp.zeros(edges.shape, f32)

    def edge(k, _):
        r0 = pl.multiple_of(k * TAP, TAP)
        t0 = start + r0
        for row, near in ((R_A0, t0 < TAP), (R_Z0, (t0 < length) & (t0 + TAP > length - TAP))):
            @pl.when(near)
            def _():
                at = lax.broadcasted_iota(jnp.int32, (TAP, 1), 0) + t0
                there = ((at < TAP) if row == R_A0 else (at >= length - TAP)).astype(f32)
                for q, ref in enumerate((f0_ref, f1_ref, f2_ref)):
                    acc[row + q] += fold(there * ref[0, pl.ds(r0, TAP), :])
        return 0

    lax.fori_loop(0, frames // TAP, edge, 0)

    ch_ref[pl.ds(i, 1), R_GM, 0 : 2 * base] = gacc[...].sum(axis=0, keepdims=True)
    ch_ref[pl.ds(i, 1), R_P, :] = 2.0 * (point + c2)
    for r in range(R_S, R_GM):
        if r != R_GS:
            total = acc[r].sum(axis=0, keepdims=True)
            if r in (R_S, R_GD, R_H2, R_HF0, R_HF1, R_PF0, R_PF1, R_A2, R_Z2):
                total = 2.0 * total
            if r in (R_SS, R_HF2, R_PF2):
                total = 4.0 * total
            ch_ref[pl.ds(i, 1), r, :] = total

    @pl.when(i == items - 1)
    def _():
        gm = jnp.concatenate([ch_ref[:, R_GM, 0 : 2 * base]] * 2, axis=0)
        ch_ref[:, R_GS, :] = product3(gm, wt3[...])[0:items]

        def got(r):
            return ch_ref[:, r, :]

        n = frames_here(len_ref, start, frames, items)
        some = (n > 0).astype(f32)
        safe = jnp.maximum(n, 1.0)
        point, offset = got(R_P), got(R_S) / safe
        level = point + offset
        mean2 = level.sum(axis=1, keepdims=True) / width
        dev = level - mean2
        spread2 = (got(R_SS) - safe * offset * offset + safe * dev * dev).sum(axis=1, keepdims=True)
        point = point - mean2
        gout = par("gain_out")
        tap0, tap1, tap2 = par("tap0"), par("tap1"), par("tap2")
        g1, sh1, cb = par("gain_in"), par("shift_in"), par("bias_dw")

        def summed(x):
            return x.sum(axis=1, keepdims=True)

        s1 = summed(gout * got(R_GS))
        s2 = summed(gout * (got(R_GD) + point * got(R_GS)))
        t1, t2 = [], []
        for q in range(3):
            h, hf, h_a, h_z = got(R_H0 + q), got(R_HF0 + q), got(R_A0 + q), got(R_Z0 + q)
            if q == 0:
                h, hf, h_a, h_z = gout * h, gout * hf, gout * h_a, gout * h_z
            if q == 2:
                h, hf = h + point * got(R_H1), hf + point * got(R_HF1)
                h_a, h_z = h_a + point * got(R_A1), h_z + point * got(R_Z1)
            kh = (tap0 + tap1 + tap2) * h - tap0 * h_a - tap2 * h_z
            t1.append(summed(g1 * kh))
            t2.append(summed(hf - cb * h - sh1 * kh))
        row = lane_put([mean2 * some, spread2 * some, n, s1, s2] + t1 + t2)
        st_ref[...] = jnp.broadcast_to(row[None], st_ref.shape)


def edge_kernel(
    frames, len_ref, tm_ref, xb_ref, xa_ref, f0a_ref, f0z_ref, f1a_ref, f1z_ref, f2a_ref, f2z_ref,
    ch1_ref, ch_ref, w_ref, wr_ref, ws_ref, *rest
):
    params, rest = rest[: len(PARAMS)], rest[len(PARAMS) :]
    ga1_ref, ga2_ref, before_ref, after_ref, stat_ref, coef_ref, chan_ref, zc_ref, gw, acc, w3, wt3 = rest
    par = channel(dict(zip(PARAMS, params)))
    i = pl.program_id(0)
    width = f0a_ref.shape[2]
    tap0, tap1, tap2 = par("tap0"), par("tap1"), par("tap2")
    a1 = par("slope_in")
    c1 = (1.0 - a1) * (0.5 * LN2)

    def put(k, x):
        stat_ref[k] = jnp.broadcast_to(x, stat_ref.shape[1:])

    @pl.when(i == 0)
    def _():
        w3[...] = stacked3(0.5 * w_ref[...])
        wt3[...] = stacked3(w_ref[...].T)
        mean1, scale1, count = merged(ga1_ref[...], width)
        mean2, scale2, _ = merged(ga2_ref[...], width)
        g = ga2_ref[...]

        def lane(k):
            return g[:, :, k : k + 1]

        dev = lane(0) - mean2[None]
        s1 = lane(3).sum(axis=0)
        s2 = (lane(4) + dev * lane(3)).sum(axis=0)
        alpha = scale2 * s1 / count
        beta = scale2 * scale2 * scale2 * s2 / count
        t1 = scale2 * lane(5).sum(axis=0) - alpha * lane(6).sum(axis=0) - beta * (lane(7) + dev * lane(6)).sum(axis=0)
        t2 = scale2 * lane(8).sum(axis=0) - alpha * lane(9).sum(axis=0) - beta * (lane(10) + dev * lane(9)).sum(axis=0)
        cut = scale1 * t1 / count
        cut_v = scale1 * scale1 * t2 / count
        put(0, scale1)
        put(1, scale2)
        put(2, 2.0 * beta)
        put(3, cut - cut_v * mean1)
        put(4, 2.0 * cut_v)
        delta = ch_ref[:, R_P, :] - mean2
        coef_ref[0] = scale2 * par("gain_out")
        coef_ref[1] = alpha + beta * delta
        coef_ref[2] = scale2 * par("gain_out") * delta + par("shift_out")
        both = jnp.concatenate([wr_ref[...], ws_ref[...]], axis=1)
        zc_ref[...] = lax.dot_general(
            coef_ref[2], both, (((1,), (0,)), ((), ())), precision=lax.Precision.HIGHEST, preferred_element_type=f32
        )

        def row(r):
            return ch_ref[:, r, :]

        c0, cc = coef_ref[0], coef_ref[1]

        def comb(r):
            return c0 * row(r) - cc * row(r + 1) - beta * row(r + 2)

        h, hf, h_a, h_z = comb(R_H0), comb(R_HF0), comb(R_A0), comb(R_Z0)
        kh = (tap0 + tap1 + tap2) * h - tap0 * h_a - tap2 * h_z
        n = ga2_ref[pl.ds(tm_ref[0], 1), :, 2:3][0]
        total = c0 * row(R_GS) - cc * n - beta * row(R_S)
        total_d = c0 * row(R_GD) - cc * row(R_S) - beta * row(R_SS)
        total_f = c0 * row(R_PF0) - cc * row(R_PF1) - beta * row(R_PF2)
        slope = (total_d + row(R_P) * total - total_f) / (1.0 - par("slope_out"))

        def over(x):
            return x.sum(axis=0, keepdims=True)

        gain_out = over(scale2 * row(R_GD) + (scale2 * delta) * row(R_GS))
        gain_in = over(hf - par("bias_dw") * h - par("shift_in") * kh) / par("gain_in")
        gain1 = par("gain_in") * scale1
        shift = par("shift_in") + gain1 * (2.0 * c1 - mean1)
        m1, m2 = ch1_ref[:, 0, :], ch1_ref[:, 1, :]
        k0 = cut - cut_v * mean1 + 2.0 * cut_v * c1
        k1 = 2.0 * cut_v
        act_sum = gain1 * kh - k0 * n - k1 * m1
        act_v = -(k0 * m1 + k1 * m2)
        zero = jnp.zeros((1, width), f32)
        chan_ref[...] = jnp.concatenate(
            [zero, over(c1 * act_sum + act_v), gain_in, over(kh), over(shift * (h - h_a)), over(shift * h),
             over(shift * (h - h_z)), over(h), -over(slope), gain_out, over(row(R_GS)), jnp.zeros((5, width), f32)],
            axis=0,
        )
        gw[...] = jnp.zeros_like(gw)
        acc[...] = jnp.zeros_like(acc)

    length = len_ref[i]
    start = tm_ref[0] * frames

    def st(k):
        return wide(stat_ref[k, pl.ds(i, 1), :], width)

    gain1, beta = par("gain_in") * st(0), st(2)
    c0, cc = coef_ref[0, pl.ds(i, 1), :], coef_ref[1, pl.ds(i, 1), :]
    b1 = 0.5 * par("bias_in")
    d_base, d_gain = 0.5 + 0.5 * a1, 0.5 - 0.5 * a1
    x = jnp.concatenate([xb_ref[0], xa_ref[0]], axis=0)
    xhi, xlo = split(x)
    h = dot(jnp.concatenate([xhi, xhi, xlo], axis=1), w3[...])
    masks = (mask_rows(start - TAP, TAP, length), mask_rows(start + frames, TAP, length))
    taps = (gain1 * tap0, gain1 * tap2)
    grads = ((f0a_ref, f1a_ref, f2a_ref), (f0z_ref, f1z_ref, f2z_ref))
    his, los = [], []
    for side in range(2):
        f0, f1, f2 = grads[side]
        m = masks[side]
        hi_s, lo_s = [], []
        for s in blocks(width):
            sums = [jnp.zeros((8, LANES), f32)] * 3
            hi_q, lo_q = [], []
            for q in range(0, TAP, SUB):
                at = slice(q, q + SUB)
                hq = h[side * TAP + q : side * TAP + q + SUB, s] + b1[:, s]
                v, t = half_act(hq, a1[:, s], c1[:, s])
                grad = m[at] * (c0[:, s] * f0[0, at, s] - cc[:, s] * f1[0, at, s] - beta[:, s] * f2[0, at, s])
                u = taps[side][:, s] * grad
                gh = u * (d_base[:, s] + d_gain[:, s] * t)
                for k, x_ in enumerate((gh, u * hq, grad * v)):
                    sums[k] = sums[k] + fold(x_)
                hi, lo = split(gh)
                hi_q.append(hi)
                lo_q.append(lo)
            acc[0, :, s] += sums[0]
            acc[1, :, s] += sums[1]
            acc[2 + 2 * side, :, s] += gain1[:, s] * sums[2]
            hi_s.append(jnp.concatenate(hi_q, axis=0))
            lo_s.append(jnp.concatenate(lo_q, axis=0))
        his.append(jnp.concatenate(hi_s, axis=1))
        los.append(jnp.concatenate(lo_s, axis=1))
    hi, lo = jnp.concatenate(his, axis=0), jnp.concatenate(los, axis=0)
    gw[...] += dot0(jnp.concatenate([xhi, xhi, xlo], axis=0), jnp.concatenate([hi, lo, hi], axis=0))
    back = dot(jnp.concatenate([hi, hi, lo], axis=1), wt3[...])
    before_ref[0], after_ref[0] = back[0:TAP], back[TAP:]


def third_kernel(
    rows, len_ref, tm_ref, mine_ref, v_ref, x_ref, f0_ref, f1_ref, f2_ref, gr_ref, z_ref, y_ref,
    ch_ref, bias_ref, w_ref, br_ref, bs_ref, stat, coef, chan, zc, gw0_ref, acc0_ref, *rest
):
    params, rest = rest[: len(PARAMS)], rest[len(PARAMS) :]
    res_ref, skip_ref, gin_ref, keep_ref, send_ref, *rest = rest
    w3, wt, ext, gw, gwt, acc, hb0, hb1, hl0, hl1 = rest
    par = channel(dict(zip(PARAMS, params)))
    i = pl.program_id(0)
    items = ch_ref.shape[0]
    frames, width = v_ref.shape[1:]
    base = gr_ref.shape[2]
    tap0, tap1, tap2 = par("tap0"), par("tap1"), par("tap2")
    a1 = par("slope_in")
    c1 = (1.0 - a1) * (0.5 * LN2)

    @pl.when(i == 0)
    def _():
        w3[...] = stacked3(0.5 * w_ref[...])
        wt[...] = jnp.concatenate(split(w_ref[...].T), axis=1)
        zeros = jnp.zeros((2 * TAP, width), f32)
        ext[0 : 2 * TAP, :] = zeros
        ext[frames + 2 * TAP : frames + 4 * TAP, :] = zeros
        gw[...] = gw0_ref[...]
        gwt[...] = jnp.zeros_like(gwt)
        acc[...] = acc0_ref[...]

    length = len_ref[i]
    start = tm_ref[0] * frames

    def st(k):
        return wide(stat[k, pl.ds(i, 1), :], width)

    scale1, scale2, beta, cut, cut_v = [st(k) for k in range(5)]
    c0, cc = coef[0, pl.ds(i, 1), :], coef[1, pl.ds(i, 1), :]
    gwt[...] += (2.0 * c0) * y_ref[0]
    gain1 = par("gain_in") * scale1
    cut = cut + cut_v * c1
    taps = [gain1 * tap0, gain1 * tap1, gain1 * tap2]
    b1 = 0.5 * par("bias_in")
    d_base, d_gain = 0.5 + 0.5 * a1, 0.5 - 0.5 * a1

    parts = frames // rows
    h_slots, hl_slots = (hb0, hb1), (hl0, hl1)

    def spread(n):
        def multiply(q):
            h_slots[n % 2][q : q + HALF, :] = product3(x_ref[0, n * rows + q : n * rows + q + HALF, :], w3[...])

        return [functools.partial(multiply, q) for q in range(0, rows, HALF)]

    def elementwise(n, masked):
        hb, hl = h_slots[n % 2], hl_slots[n % 2]
        if masked:
            m = mask_rows(start + n * rows, rows, length)

        def unit(s, begin):
            sums = [jnp.zeros((8, LANES), f32)] * 5
            for q in range(begin, begin + HALF, SUB):
                hq = hb[q : q + SUB, s] + b1[:, s]
                r = n * rows + q
                t = jnp.tanh(hq)
                v = v_ref[0, r : r + SUB, s]
                later = ext[r + 3 * TAP : r + 3 * TAP + SUB, s]
                here = ext[r + 2 * TAP : r + 2 * TAP + SUB, s]
                before = ext[r + TAP : r + TAP + SUB, s]
                u = taps[0][:, s] * later + taps[1][:, s] * here + taps[2][:, s] * before
                u = u - cut[:, s] - cut_v[:, s] * v
                vm = v
                if masked:
                    u, vm = u * m[q : q + SUB], v * m[q : q + SUB]
                gh = u * (d_base[:, s] + d_gain[:, s] * t)
                for k, x_ in enumerate((gh, u * hq, later * vm, here * vm, before * vm)):
                    sums[k] = sums[k] + fold(x_)
                hi, lo = split(gh)
                hl[0, q : q + SUB, s] = hi
                hl[1, q : q + SUB, s] = lo
            for k, x_ in enumerate(sums):
                acc[k, :, s] += x_ if k < 2 else gain1[:, s] * x_

        return [functools.partial(unit, s, q) for q in range(0, rows, HALF) for s in blocks(width)]

    def products(n):
        hl = hl_slots[n % 2]

        def weights():
            xhi, xlo = split(x_ref[0, n * rows : (n + 1) * rows, :])
            gw[...] += dot0(jnp.concatenate([xhi, xhi, xlo], axis=0), jnp.concatenate([hl[0], hl[1], hl[0]], axis=0))

        def out(q):
            hi, lo = hl[0, q : q + HALF, :], hl[1, q : q + HALF, :]
            at = slice(n * rows + q, n * rows + q + HALF)
            by_hi = dot(hi, wt[...])
            by_lo = dot(lo, wt[:, 0:base])
            gin_ref[0, at, :] = gr_ref[0, at, :] + (by_hi[:, 0:base] + (by_hi[:, base:] + by_lo))

        return [weights] + [functools.partial(out, q) for q in range(0, rows, HALF)]

    scale_c = stat[1, pl.ds(i, 1), :]
    br, bs = br_ref[...], bs_ref[...]
    zi = zc[pl.ds(i, 1), :]

    def outputs(n, kind):
        at = slice(n * rows, (n + 1) * rows)
        x = x_ref[0, at, :]
        if kind == "none":
            res_ref[0, at, :] = x + br
            skip_ref[0, at, :] = jnp.broadcast_to(bs, (rows, base))
            gin_ref[0, at, :] = gr_ref[0, at, :]
            return
        z = z_ref[0, at, :]
        to_res = scale_c * z[:, 0:base] + zi[:, 0:base]
        to_skip = scale_c * z[:, base:] + zi[:, base:]
        if kind == "some":
            m = mask_rows(start + n * rows, rows, length)
            to_res, to_skip = to_res * m, to_skip * m
        res_ref[0, at, :] = (x + to_res) + br
        skip_ref[0, at, :] = to_skip + bs

    def lift(k):
        for s in blocks(width):
            for q in range(k * rows, (k + 1) * rows, SUB):
                at = slice(q, q + SUB)
                ext[2 * TAP + q : 2 * TAP + q + SUB, s] = (
                    c0[:, s] * f0_ref[0, at, s] - cc[:, s] * f1_ref[0, at, s] - beta[:, s] * f2_ref[0, at, s]
                )

    interleave(spread(0), [functools.partial(lift, k) for k in range(parts)])
    for n in range(parts):
        def step(kind, n=n):
            ahead = spread(n + 1) if n + 1 < parts else []
            if kind == "none":
                for piece in ahead + [functools.partial(outputs, n, kind)]:
                    piece()
                return
            vector = elementwise(n, kind == "some")
            weights, *outs = products(n)
            each = len(vector) // len(outs)
            for j, out in enumerate(outs):
                interleave(ahead[j : j + 1] or [lambda: None], vector[j * each : (j + 1) * each])
                out()
            outputs(n, kind)
            weights()

        t0 = start + n * rows
        full, none = t0 + rows <= length, t0 >= length
        pl.when(full)(functools.partial(step, "full"))
        pl.when(jnp.logical_not(full | none))(functools.partial(step, "some"))
        pl.when(none)(functools.partial(step, "none"))

    @pl.when(i == items - 1)
    def _():
        outer = lax.dot_general(
            ch_ref[:, R_GM, 0 : 2 * base], coef[2], (((0,), (0,)), ((), ())),
            precision=lax.Precision.HIGHEST, preferred_element_type=f32,
        )
        both = (gwt[...] + outer).T
        done = acc[...].sum(axis=1)
        tap_sums = 2.0 * done[2:5]
        by_v = 0.5 * (tap0 * tap_sums[0:1] + tap1 * tap_sums[1:2] + tap2 * tap_sums[2:3])
        slope = (-2.0 / (1.0 - a1)) * (chan[1:2, :] + by_v - done[1:2])
        table = jnp.concatenate([done[0:1], slope, chan[2:4, :], chan[4:7, :] + tap_sums, chan[7:16, :]], axis=0)
        bias = bias_ref[...].sum(axis=0, keepdims=True)
        tail = jnp.concatenate([bias[:, 0:base], bias[:, base:], jnp.zeros((6, base), f32)], axis=0)
        pieces = [both[:, 0:base], both[:, base:]] + [gw[:, s] for s in blocks(width)]
        pieces += [table[:, s] for s in blocks(width)] + [tail]
        half = keep_ref.shape[0]
        pieces.append(jnp.zeros((2 * half - sum(p.shape[0] for p in pieces), LANES), f32))

        def store(first, second):
            at = 0
            for piece in pieces:
                end = at + piece.shape[0]
                for side, ref in enumerate((first, second)):
                    a, b = max(at, side * half), min(end, (side + 1) * half)
                    if a < b:
                        ref[a - side * half : b - side * half, :] = piece[a - at : b - at]
                at = end

        pl.when(mine_ref[0] == 0)(functools.partial(store, keep_ref, send_ref))
        pl.when(mine_ref[0] == 1)(functools.partial(store, send_ref, keep_ref))


def sum_rows(size):
    return -(-size // 256) * 256


def exchange(x, axis):
    return lax.all_to_all(x, axis, 0, 0)


def halves(n_item):
    return [1 << k for k in range(n_item.bit_length() - 1)]


def reduce_all(x, sizes, beside):
    n_tm, n_item = sizes["tm"], sizes["item"]
    keep, send = x

    def swap(y, by):
        return lax.ppermute(y, "item", [(d, d ^ by) for d in range(n_item)])

    for by in halves(n_item):
        if by > 1:
            half = x.shape[0] // 2
            mine = (lax.axis_index("item") // by) % 2
            keep = lax.dynamic_slice_in_dim(x, mine * half, half)
            send = lax.dynamic_slice_in_dim(x, (1 - mine) * half, half)
        x = keep + swap(send, by)
    if n_item == 1:
        x = jnp.concatenate([keep, send])
    parts = exchange(x.reshape((n_tm, x.shape[0] // n_tm) + x.shape[1:]), "tm")
    x = jnp.sum(parts, axis=0)
    x = exchange(jnp.broadcast_to(x[None], (n_tm,) + x.shape), "tm").reshape((-1,) + x.shape[1:])
    for by in halves(n_item)[::-1]:
        if by == 1:
            x, beside = lax.optimization_barrier((x, beside))
        mine = (lax.axis_index("item") // by) % 2
        other = swap(x, by)
        x = jnp.where(mine == 0, jnp.concatenate([x, other]), jnp.concatenate([other, x]))
    return x, beside


def whole(shape):
    return pl.BlockSpec(shape, lambda i: (0,) * len(shape))


def per_item(shape):
    return pl.BlockSpec((1,) + shape, lambda i: (i,) + (0,) * len(shape))


SMEM = pl.BlockSpec(memory_space=pltpu.SMEM)


def body(
    inputs, lengths, counts, weight_in, bias_in, slope_in, gain_in, shift_in, channelwise_taps, channelwise_bias,
    slope_out, gain_out, shift_out, weight_res, bias_res, weight_skip, bias_skip, grad_residual, grad_skip,
):
    items, frames, base = inputs.shape
    width = weight_in.shape[1]
    sources = grad_skip.shape[1]
    tm, across = lax.axis_size("tm"), lax.axis_size("item")
    place = lax.axis_index("tm").astype(jnp.int32).reshape(1)
    mine = (lax.axis_index("item") % 2).astype(jnp.int32).reshape(1)
    up = [(d, d + 1) for d in range(tm - 1)]
    down = [(d + 1, d) for d in range(tm - 1)]
    x_before = lax.ppermute(inputs[:, frames - TAP :], "tm", up)
    x_after = lax.ppermute(inputs[:, :TAP], "tm", down)

    def row(v):
        return v.reshape(1, -1)

    table = [row(bias_in), row(slope_in), row(gain_in), row(shift_in), channelwise_taps, row(channelwise_bias),
             row(slope_out), row(gain_out), row(shift_out)]
    table_specs = [whole(t.shape) for t in table]
    vmem = lambda mib: pltpu.CompilerParams(vmem_limit_bytes=mib * 2**20)

    rows1, rows2, rows3 = (min(c, frames) for c in (CHUNK1, CHUNK2, CHUNK3))
    v1, st1, ch1 = pl.pallas_call(
        functools.partial(first_kernel, rows1),
        grid=(items,),
        in_specs=[SMEM, SMEM, per_item((frames, base)),
                  pl.BlockSpec((1, rows1, base), lambda i: (jnp.minimum(i + 1, items - 1), 0, 0)),
                  whole((base, width)), whole((1, width)), whole((1, width))],
        out_specs=[per_item((frames, width)), whole((tm, items, LANES)), whole((items, 8, width))],
        out_shape=[jax.ShapeDtypeStruct((items, frames, width), f32), jax.ShapeDtypeStruct((tm, items, LANES), f32),
                   jax.ShapeDtypeStruct((items, 8, width), f32)],
        scratch_shapes=[pltpu.VMEM((3 * base, width), bf16), pltpu.VMEM((2, 8, width), f32)]
        + [pltpu.VMEM((rows1, width), f32)] * 2,
        compiler_params=vmem(48),
        name="first",
    )(lengths, place, inputs, inputs, weight_in, table[0], table[1])
    ga1 = exchange(st1, "tm")

    big = jax.ShapeDtypeStruct((items, frames, width), f32)
    f0, f1, f2, z, y, ch, st2, bias = pl.pallas_call(
        functools.partial(second_kernel, rows2),
        grid=(items,),
        in_specs=[SMEM, SMEM, SMEM, per_item((frames, width)), per_item((TAP, base)), per_item((TAP, base)),
                  per_item((frames, base)), per_item((sources, frames, base)), whole((base, width)),
                  whole((width, base)), whole((width, base))] + table_specs + [whole((tm, items, LANES))],
        out_specs=[per_item((frames, width))] * 3 + [per_item((frames, 2 * base)), per_item((2 * base, width)),
                   whole((items, ROWS, width)), whole((tm, items, LANES)), whole((8, 2 * base))],
        out_shape=[big, big, big, jax.ShapeDtypeStruct((items, frames, 2 * base), f32),
                   jax.ShapeDtypeStruct((items, 2 * base, width), f32), jax.ShapeDtypeStruct((items, ROWS, width), f32),
                   jax.ShapeDtypeStruct((tm, items, LANES), f32), jax.ShapeDtypeStruct((8, 2 * base), f32)],
        scratch_shapes=[pltpu.VMEM((3 * base, width), bf16), pltpu.VMEM((6 * base, width), bf16),
                        pltpu.VMEM((3 * width, 2 * base), bf16), pltpu.VMEM((2, items, LANES), f32),
                        pltpu.VMEM((frames + 2 * TAP, width), f32), pltpu.VMEM((ROWS, 8, width), f32),
                        pltpu.VMEM((8, 2 * base), f32), pltpu.VMEM((2 * base, width), f32)]
        + [pltpu.VMEM((rows2, width), f32)] * 2 + [pltpu.VMEM((2, rows2, width), bf16)] * 2
        + [pltpu.VMEM((frames // rows2, 2, rows2, 2 * base), bf16)],
        compiler_params=vmem(48),
        name="second",
    )(lengths, counts, place, v1, x_before, x_after, grad_residual, grad_skip, weight_in, weight_res, weight_skip,
      *table, ga1)
    ga2 = exchange(st2, "tm")

    n_sum = sum_rows(2 * width + 4 * base + 64 + 8)
    out = jax.ShapeDtypeStruct((items, frames, base), f32)
    strip = lambda k: pl.BlockSpec((1, TAP, width), lambda i: (i, k, 0))
    last = frames // TAP - 1
    small = [((5, items, LANES), f32), ((3, items, width), f32), ((16, width), f32), ((items, 2 * base), f32),
             ((base, width), f32), ((8, 8, width), f32)]
    to_last, to_next, *given = pl.pallas_call(
        functools.partial(edge_kernel, frames),
        grid=(items,),
        in_specs=[SMEM, SMEM, per_item((TAP, base)), per_item((TAP, base))] + [strip(0), strip(last)] * 3
        + [whole((items, 8, width)), whole((items, ROWS, width)), whole((base, width)), whole((width, base)),
           whole((width, base))] + table_specs + [whole((tm, items, LANES))] * 2,
        out_specs=[per_item((TAP, base))] * 2 + [whole(shape) for shape, _ in small],
        out_shape=[jax.ShapeDtypeStruct((items, TAP, base), f32)] * 2
        + [jax.ShapeDtypeStruct(shape, dtype) for shape, dtype in small],
        scratch_shapes=[pltpu.VMEM((3 * base, width), bf16), pltpu.VMEM((3 * width, base), bf16)],
        compiler_params=vmem(48),
        name="edge",
    )(lengths, place, x_before, x_after, f0, f0, f1, f1, f2, f2, ch1, ch, weight_in, weight_res, weight_skip, *table,
      ga1, ga2)
    from_next = lax.ppermute(to_last, "tm", down)
    from_last = lax.ppermute(to_next, "tm", up)

    res, skip, gin, *sums = pl.pallas_call(
        functools.partial(third_kernel, rows3),
        grid=(items,),
        in_specs=[SMEM, SMEM, SMEM, per_item((frames, width)), per_item((frames, base)), per_item((frames, width)),
                  per_item((frames, width)), per_item((frames, width)), per_item((frames, base)),
                  per_item((frames, 2 * base)), per_item((2 * base, width)), whole((items, ROWS, width)),
                  whole((8, 2 * base)), whole((base, width)), whole((1, base)), whole((1, base))]
        + [whole(shape) for shape, _ in small] + table_specs,
        out_specs=[per_item((frames, base))] * 3 + [whole((n_sum // 2, base))] * 2,
        out_shape=[out, out, out] + [jax.ShapeDtypeStruct((n_sum // 2, base), f32)] * 2,
        scratch_shapes=[pltpu.VMEM((3 * base, width), bf16), pltpu.VMEM((width, 2 * base), bf16),
                        pltpu.VMEM((frames + 4 * TAP, width), f32),
                        pltpu.VMEM((base, width), f32), pltpu.VMEM((2 * base, width), f32),
                        pltpu.VMEM((8, 8, width), f32)]
        + [pltpu.VMEM((rows3, width), f32)] * 2 + [pltpu.VMEM((2, rows3, width), bf16)] * 2,
        compiler_params=vmem(48),
        cost_estimate=pl.CostEstimate(flops=items * frames * width * base * 30, transcendentals=items * frames * width,
                                      bytes_accessed=items * frames * (5 * width + 7 * base) * 4),
        name="third",
    )(lengths, place, mine, v1, inputs, f0, f1, f2, grad_residual, z, y, ch, bias, weight_in, row(bias_res), row(bias_skip),
      *given, *table)

    sums, from_next, from_last = lax.optimization_barrier((sums, from_next, from_last))
    gin = gin.at[:, frames - TAP :].add(from_next)
    gin = gin.at[:, :TAP].add(from_last)
    total, gin = reduce_all(sums, {"tm": tm, "item": across}, gin)

    g_res, g_skip = total[0:width], total[width : 2 * width]
    at0 = 2 * width + 4 * base
    g_in = total[2 * width : at0].reshape(4, base, LANES).transpose(1, 0, 2).reshape(base, width)
    vec = total[at0 : at0 + 64].reshape(4, 16, LANES).transpose(1, 0, 2).reshape(16, width)
    return (
        res, skip, gin, g_in, vec[0], vec[1], vec[2], vec[3], vec[4:7], vec[7], vec[8], vec[9], vec[10],
        g_res, total[at0 + 64], g_skip, total[at0 + 65],
    )


def solution(mesh):
    spread = P("item", "tm", None)
    return jax.shard_map(
        body,
        mesh=mesh,
        in_specs=(spread, P("item"), P("item")) + (P(),) * 14 + (spread, P("item", None, "tm", None)),
        out_specs=(spread,) * 3 + (P(),) * 14,
        check_vma=False,
    )
```

time: 276 us -> 219 us (0.79)
  Pallas kernels: 172 us -> 131 us
  waiting for transfers between devices: 59 us -> 24.6 us
  blocking collectives: 0 us -> 23.4 us
  starting transfers between devices: 27.7 us -> 23 us
    pallas_call x3 -> x4, Pallas kernels: 172 us -> 131 us  [the longest x1 58.6 us: body(): pl.pallas_call(functools.partial(second_kernel, rows2), grid=(items,), in...]
    ppermute x12 -> x6, waiting for transfers between devices: 46.3 us -> 12 us  [the longest x4 12 us: swap(): return lax.ppermute(y, 'item', [(d, d ^ by) for d in range(n_item)])]
    all_to_all x0 -> x2, blocking collectives: none -> 23.4 us  [exchange(): return lax.all_to_all(x, axis, 0, 0)]
    unnamed x14 -> x42, local copies, waits for them, and re-layouts: 1.58 us -> 5.24 us
    all_to_all x2, starting transfers between devices: 10.3 us -> 6.76 us  [exchange(): return lax.all_to_all(x, axis, 0, 0)]
    ppermute x12 -> x6, starting transfers between devices: 11.3 us -> 9.46 us  [the longest x1 4.58 us: body(): from_last = lax.ppermute(to_next, 'tm', up)]
  transfers between devices with their start and end apart: 16 -> 10, of which waited for: 12 -> 6; matrix products, arithmetic and copies ran while one was open for 3% -> 2% of each run, Pallas kernels for 6% -> 28%
where the time goes in v2:
time: 219 us; the launch traced here: 218 us
  Pallas kernels  131 us (60%)
  waiting for transfers between devices  24.6 us (11%)
  blocking collectives  23.4 us (11%)
  starting transfers between devices  23 us (11%)
  local copies, waits for them, and re-layouts  10.6 us (5%)
  other arithmetic  3.97 us (2%)
    pallas_call x1, Pallas kernels, body(): pl.pallas_call(functools.partial(second_kernel, rows2), grid=(items,), in...  58.6 us
    pallas_call x1, Pallas kernels, body(): pl.pallas_call(functools.partial(third_kernel, rows3), grid=(items,), in_...  44.8 us
    all_to_all x2, blocking collectives, exchange(): return lax.all_to_all(x, axis, 0, 0)  23.4 us
    pallas_call x1, Pallas kernels, body(): pl.pallas_call(functools.partial(first_kernel, rows1), grid=(items,), in_...  15.6 us
    all_to_all x2, waiting for transfers between devices, exchange(): return lax.all_to_all(x, axis, 0, 0)  12.7 us
    pallas_call x1, Pallas kernels, body(): pl.pallas_call(functools.partial(edge_kernel, frames), grid=(items,), in_...  12.3 us
    ppermute x4, waiting for transfers between devices, swap(): return lax.ppermute(y, 'item', [(d, d ^ by) for d in range(n_item)])  12 us
    all_to_all x2, starting transfers between devices, exchange(): return lax.all_to_all(x, axis, 0, 0)  6.76 us
  transfers between devices with their start and end apart: 10, of which 6 were waited for; matrix products, arithmetic and copies ran while one was open for 2% of the time, Pallas kernels for 28%

profile of v2, /device:TPU:0, one launch (start us, length us, event | category | flops | bytes accessed | tf_op | source)
XLA Modules:
  0.0 218.0 jit_solution(335581357253230948)
XLA Ops:
  0.7 1.3 fusion.1
  1.9 1.3 collective-permute-start.1
  3.2 5.5 %collective-permute-start = (f32[8,128,128]{2,1,0:T(8,128)S(1)}, f32[8,128,128]{2,1,0:T(8,128)S(1)}, u32[]{:S(2)}, u32[]{:S(2)}) collective-permute-start(f32[8,128,128]{2,1,0:T(8,128)S(1)} %get-tuple-element.102), channel_id=1, source_target_pairs={{0,4},{4,8},{8,12},{12,16},{16,20},{20,24},{24,28},{1,5},{5,9},{9,... | collective-permute-start | bytes 1572872 | tf_op jit(solution)/shard_map/ppermute | solution.py:832
  8.8 0.0 copy-start
  8.8 2.2 copy-done
  10.9 0.9 copy-done.1
  11.9 0.7 copy-done.6
  12.6 0.7 copy-done.8
  13.3 0.7 copy-done.16
  13.9 0.0 copy-start.11
  13.9 0.0 copy-start.12
  13.9 0.0 copy-start.13
  14.0 0.0 copy-start.14
  14.0 0.0 copy-start.15
  14.0 0.0 copy-start.20
  14.0 15.6 %first.1 = (f32[8,1024,512]{2,1,0:T(8,128)}, f32[8,8,128]{2,1,0:T(8,128)S(1)}, f32[8,8,512]{2,1,0:T(8,128)S(1)}) custom-call(s32[8]{0:T(128)S(1)} %copy-done.16, s32[1]{0:T(128)} %bitcast.tm_ref, f32[8,1024,128]{2,1,0:T(8,128)S(1)} %copy-done, f32[8,1024,128]{2,1,0:T(8,128)S(1)} %copy-done, f32[128,512]{1,0:T(8,128)S(1)} %copy-done.1, ...), custom_call_target="tpu_custom_call" | custom-call | tf_op jit(solution)/shard_map/first/pallas_call | solution.py:844
  29.6 12.7 %all_to_all.20.rest_9_ = f32[8,8,128]{2,1,0:T(8,128)S(1)} all-to-all(f32[8,8,128]{2,1,0:T(8,128)S(1)} %get-tuple-element.72), channel_id=1, replica_groups=mesh['tm'=8,'item'=4] {'tm'}, dimensions={0} | all-to-all | bytes 65536 | tf_op jit(solution)/shard_map/all_to_all | solution.py:774
  42.4 0.0 collective-permute-done.1.xa_ref
  42.4 0.0 collective-permute-done.xb_ref
  42.4 0.0 copy-done.3
  42.4 0.0 copy-done.4
  42.4 0.0 copy-done.5
  42.4 0.0 copy-done.10
  42.4 0.0 copy-done.11
  42.4 0.0 copy-done.12
  42.4 0.0 copy-done.13
  42.5 0.0 copy-start.2
  42.5 0.0 copy-start.7
  42.5 0.0 copy-start.9
  42.5 0.0 copy-start.17
  42.5 58.6 %second.1 = (f32[8,1024,512]{2,1,0:T(8,128)}, f32[8,1024,512]{2,1,0:T(8,128)}, f32[8,1024,512]{2,1,0:T(8,128)}, f32[8,1024,256]{2,1,0:T(8,128)}, f32[8,256,512]{...) custom-call(s32[8]{0:T(128)S(1)} %copy-done.16, s32[8]{0:T(128)S(1)} %copy-done.20, ...), custom_call_target="tpu_custom_call" | custom-call | tf_op jit(solution)/shard_map/second/pallas_call | solution.py:861
  101.1 3.4 %all-to-all-start.1 = ((f32[8,8,128]{2,1,0:T(8,128)}), f32[8,8,128]{2,1,0:T(8,128)S(1)}, u32[]{:S(2)}, u32[]{:S(2)}) async-start(f32[8,8,128]{2,1,0:T(8,128)} %get-tuple-element.81), calls=%async_computation.1 | async-start | bytes 65536 | tf_op jit(solution)/shard_map/all_to_all | solution.py:774
  104.5 6.6 %all-to-all-done.1.rest_10_ = f32[8,8,128]{2,1,0:T(8,128)S(1)} async-done(((f32[8,8,128]{2,1,0:T(8,128)}), f32[8,8,128]{2,1,0:T(8,128)S(1)}, u32[]{:S(2)}, u32[]{:S(2)}) %all-to-all-start.1) | async-done | bytes 32800 | tf_op jit(solution)/shard_map/all_to_all | solution.py:774
  111.1 0.0 copy-done.7
  111.2 0.0 copy-start.18
  111.2 0.0 copy-start.19
  111.2 12.3 %edge.1 = (f32[8,128,128]{2,1,0:T(8,128)S(1)}, f32[8,128,128]{2,1,0:T(8,128)S(1)}, f32[5,8,128]{2,1,0:T(8,128)S(1)}, f32[3,8,512]{2,1,0:T(8,128)S(1)}, f32[16,51...) custom-call(s32[8]{0:T(128)S(1)} %copy-done.17, s32[1]{0:T(128)} %bitcast.tm_ref, ...), custom_call_target="tpu_custom_call" | custom-call | tf_op jit(solution)/shard_map/edge/pallas_call | solution.py:890
  123.5 1.3 collective-permute-start.2
  124.8 4.6 %collective-permute-start.3 = (f32[8,128,128]{2,1,0:T(8,128)S(1)}, f32[8,128,128]{2,1,0:T(8,128)S(1)}, u32[]{:S(2)}, u32[]{:S(2)}) collective-permute-start(f32[8,128,128]{2,1,0:T(8,128)S(1)} %get-tuple-element.93), channel_id=1, source_target_pairs={{0,4},{4,8},{8,12},{12,16},{16,20},{20,24},{24,28},{1,5},{5,9},{9,... | collective-permute-start | bytes 1572872 | tf_op jit(solution)/shard_map/ppermute | solution.py:905
  129.4 0.0 copy-done.18
  129.4 0.0 copy-done.19
  129.4 44.8 %third.1 = (f32[8,1024,128]{2,1,0:T(8,128)}, f32[8,1024,128]{2,1,0:T(8,128)}, f32[8,1024,128]{2,1,0:T(8,128)}, f32[896,128]{1,0:T(8,128)S(1)}, f32[896,128]{1,0:T(8,128)S(1)}) custom-call(s32[8]{0:T(128)S(1)} %copy-done.17, s32[1]{0:T(128)} %bitcast.tm_ref, s32[1]{0:T(128)} %bitcast.1.mine_ref, f32[8,1024,512]{2,1,0:T(8,128)} %get-tuple-element.71.v_ref, ...), custom_call_target="tpu_custom_call" | custom-call | flops 16106127360 | bytes 113246208 | tf_op jit(solution)/shard_map/third/pallas_call | solution.py:907
  174.2 0.0 collective-permute-done.2
  174.2 0.0 collective-permute-done.3
  174.2 0.1 collective-permute-start.4
  174.4 1.8 collective-permute-done.4
  176.2 1.7 collective-permute-start.5
  178.0 6.0 %collective-permute-done.5 = f32[448,128]{1,0:T(8,128)S(1)} collective-permute-done((f32[448,128]{1,0:T(8,128)S(1)}, f32[448,128]{1,0:T(8,128)S(1)}, u32[]{:S(2)}, u32[]{:S(2)}) %collective-permute-start.5) | collective-permute-done | bytes 229408 | tf_op jit(solution)/shard_map/ppermute | solution.py:786
  183.9 10.6 %all_to_all.21 = f32[8,56,128]{2,1,0:T(8,128)S(1)} all-to-all(f32[8,56,128]{2,1,0:T(8,128)S(1)} %bitcast.69), channel_id=1, replica_groups=mesh['tm'=8,'item'=4] {'tm'}, dimensions={0} | all-to-all | bytes 458752 | tf_op jit(solution)/shard_map/all_to_all | solution.py:774
  194.6 0.7 broadcast_in_dim.2
  195.3 3.4 %all-to-all-start.3 = ((f32[8,56,128]{2,1,0:T(8,128)}), f32[8,56,128]{2,1,0:T(8,128)S(1)}, u32[]{:S(2)}, u32[]{:S(2)}) async-start(f32[8,56,128]{2,1,0:T(8,128)} %broadcast_in_dim.2), calls=%async_computation.3 | async-start | bytes 458752 | tf_op jit(solution)/shard_map/all_to_all | solution.py:774
  198.7 1.9 add_dynamic-update-slice_fusion
  200.6 6.1 %all-to-all-done.3 = f32[8,56,128]{2,1,0:T(8,128)S(1)} async-done(((f32[8,56,128]{2,1,0:T(8,128)}), f32[8,56,128]{2,1,0:T(8,128)S(1)}, u32[]{:S(2)}, u32[]{:S(2)}) %all-to-all-start.3) | async-done | bytes 229408 | tf_op jit(solution)/shard_map/all_to_all | solution.py:774
  206.7 1.7 collective-permute-start.6
  208.4 1.9 fusion
  210.2 2.4 %collective-permute-done.6 = f32[448,128]{1,0:T(8,128)S(1)} collective-permute-done((f32[448,128]{1,0:T(8,128)S(1)}, f32[448,128]{1,0:T(8,128)S(1)}, u32[]{:S(2)}, u32[]{:S(2)}) %collective-permute-start.6) | collective-permute-done | bytes 229408 | tf_op jit(solution)/shard_map/ppermute | solution.py:786
  212.7 0.1 collective-permute-start.7
  212.8 1.8 collective-permute-done.7
  214.6 0.1 maximum_select_fusion
  214.7 0.5 slice_bitcast_fusion.1
  215.2 0.8 fusion.2
  216.0 0.6 slice_bitcast_fusion
  216.6 0.6 fusion.3
  217.2 0.7 copy.40
  (20 shorter events, 0.2 us)
Async XLA Ops:
  1.9 40.4 %collective-permute-start.1 = (f32[8,128,128]{2,1,0:T(8,128)S(1)}, f32[8,128,128]{2,1,0:T(8,128)S(1)}, u32[]{:S(2)}, u32[]{:S(2)}) collective-permute-start(f32[8,128,128]{2,1,0:T(8,128)S(1)} %get-tuple-element.101), channel_id=1, source_target_pairs={{4,0},{8,4},{12,8},{16,12},{20,16},{24,20},{28,24},{5,1},{9,5},{13... | collective-permute-start | bytes 1572872 | tf_op jit(solution)/shard_map/ppermute | solution.py:833
  3.2 39.1 %collective-permute-start = (f32[8,128,128]{2,1,0:T(8,128)S(1)}, f32[8,128,128]{2,1,0:T(8,128)S(1)}, u32[]{:S(2)}, u32[]{:S(2)}) collective-permute-start(f32[8,128,128]{2,1,0:T(8,128)S(1)} %get-tuple-element.102), channel_id=1, source_target_pairs={{0,4},{4,8},{8,12},{12,16},{16,20},{20,24},{24,28},{1,5},{5,9},{9,... | collective-permute-start | bytes 1572872 | tf_op jit(solution)/shard_map/ppermute | solution.py:832
  8.8 2.2 %copy-start = (f32[8,1024,128]{2,1,0:T(8,128)S(1)}, f32[8,1024,128]{2,1,0:T(8,128)}, u32[]{:S(2)}) copy-start(f32[8,1024,128]{2,1,0:T(8,128)} %x_ref.3) | copy-start | bytes 12582916
  10.9 0.9 copy-start.1
  11.9 0.7 copy-start.6
  12.6 0.7 copy-start.8
  13.3 0.7 copy-start.16
  13.9 28.4 %copy-start.3 = (f32[512,128]{1,0:T(8,128)S(1)}, f32[512,128]{1,0:T(8,128)}, u32[]{:S(2)}) copy-start(f32[512,128]{1,0:T(8,128)} %wr_ref.3) | copy-start | bytes 786436
  13.9 28.4 %copy-start.4 = (f32[512,128]{1,0:T(8,128)S(1)}, f32[512,128]{1,0:T(8,128)}, u32[]{:S(2)}) copy-start(f32[512,128]{1,0:T(8,128)} %ws_ref.3) | copy-start | bytes 786436
  13.9 28.5 %copy-start.5 = (f32[3,512]{1,0:T(4,128)S(1)}, f32[3,512]{1,0:T(4,128)}, u32[]{:S(2)}) copy-start(f32[3,512]{1,0:T(4,128)} %rest_4_.5) | copy-start | bytes 18436
  13.9 28.5 %copy-start.10 = (f32[512]{0:T(512)S(1)}, f32[512]{0:T(512)}, u32[]{:S(2)}) copy-start(f32[512]{0:T(512)} %param.29) | copy-start | bytes 6148
  13.9 28.5 %copy-start.11 = (f32[512]{0:T(512)S(1)}, f32[512]{0:T(512)}, u32[]{:S(2)}) copy-start(f32[512]{0:T(512)} %param.30) | copy-start | bytes 6148
  13.9 28.5 %copy-start.12 = (f32[512]{0:T(512)S(1)}, f32[512]{0:T(512)}, u32[]{:S(2)}) copy-start(f32[512]{0:T(512)} %param.32) | copy-start | bytes 6148
  13.9 28.5 %copy-start.13 = (f32[512]{0:T(512)S(1)}, f32[512]{0:T(512)}, u32[]{:S(2)}) copy-start(f32[512]{0:T(512)} %param.33) | copy-start | bytes 6148
  14.0 28.5 %copy-start.14 = (f32[512]{0:T(512)S(1)}, f32[512]{0:T(512)}, u32[]{:S(2)}) copy-start(f32[512]{0:T(512)} %param.34) | copy-start | bytes 6148
  14.0 28.5 %copy-start.15 = (f32[512]{0:T(512)S(1)}, f32[512]{0:T(512)}, u32[]{:S(2)}) copy-start(f32[512]{0:T(512)} %param.35) | copy-start | bytes 6148
  14.0 28.5 %copy-start.20 = (s32[8]{0:T(128)S(1)}, s32[8]{0:T(128)}, u32[]{:S(2)}) copy-start(s32[8]{0:T(128)} %cnt_ref.1) | copy-start | bytes 100
  42.5 68.7 %copy-start.2 = (f32[128,512]{1,0:T(8,128)S(1)}, f32[128,512]{1,0:T(8,128)}, u32[]{:S(2)}) copy-start(f32[128,512]{1,0:T(8,128)} %w_ref.7) | copy-start | bytes 786436
  42.5 68.7 %copy-start.7 = (f32[512]{0:T(512)S(1)}, f32[512]{0:T(512)}, u32[]{:S(2)}) copy-start(f32[512]{0:T(512)} %param.27) | copy-start | bytes 6148
  42.5 68.7 %copy-start.9 = (f32[512]{0:T(512)S(1)}, f32[512]{0:T(512)}, u32[]{:S(2)}) copy-start(f32[512]{0:T(512)} %param.28) | copy-start | bytes 6148
  42.5 68.7 %copy-start.17 = (s32[8]{0:T(128)S(1)}, s32[8]{0:T(128)}, u32[]{:S(2)}) copy-start(s32[8]{0:T(128)} %len_ref.7) | copy-start | bytes 100
  101.1 10.0 %all-to-all-start.1 = ((f32[8,8,128]{2,1,0:T(8,128)}), f32[8,8,128]{2,1,0:T(8,128)S(1)}, u32[]{:S(2)}, u32[]{:S(2)}) async-start(f32[8,8,128]{2,1,0:T(8,128)} %get-tuple-element.81), calls=%async_computation.1 | async-start | bytes 65536 | tf_op jit(solution)/shard_map/all_to_all | solution.py:774
  111.2 18.2 %copy-start.18 = (f32[128]{0:T(128)S(1)}, f32[128]{0:T(128)}, u32[]{:S(2)}) copy-start(f32[128]{0:T(128)} %param.37) | copy-start | bytes 1540
  111.2 18.2 %copy-start.19 = (f32[128]{0:T(128)S(1)}, f32[128]{0:T(128)}, u32[]{:S(2)}) copy-start(f32[128]{0:T(128)} %param.39) | copy-start | bytes 1540
  123.5 50.7 %collective-permute-start.2 = (f32[8,128,128]{2,1,0:T(8,128)S(1)}, f32[8,128,128]{2,1,0:T(8,128)S(1)}, u32[]{:S(2)}, u32[]{:S(2)}) collective-permute-start(f32[8,128,128]{2,1,0:T(8,128)S(1)} %get-tuple-element.92), channel_id=1, source_target_pairs={{4,0},{8,4},{12,8},{16,12},{20,16},{24,20},{28,24},{5,1},{9,5},{13... | collective-permute-start | bytes 1572872 | tf_op jit(solution)/shard_map/ppermute | solution.py:904
  124.8 49.4 %collective-permute-start.3 = (f32[8,128,128]{2,1,0:T(8,128)S(1)}, f32[8,128,128]{2,1,0:T(8,128)S(1)}, u32[]{:S(2)}, u32[]{:S(2)}) collective-permute-start(f32[8,128,128]{2,1,0:T(8,128)S(1)} %get-tuple-element.93), channel_id=1, source_target_pairs={{0,4},{4,8},{8,12},{12,16},{16,20},{20,24},{24,28},{1,5},{5,9},{9,... | collective-permute-start | bytes 1572872 | tf_op jit(solution)/shard_map/ppermute | solution.py:905
  174.2 1.9 collective-permute-start.4
  176.2 7.7 %collective-permute-start.5 = (f32[448,128]{1,0:T(8,128)S(1)}, f32[448,128]{1,0:T(8,128)S(1)}, u32[]{:S(2)}, u32[]{:S(2)}) collective-permute-start(f32[448,128]{1,0:T(8,128)S(1)} %constant_dynamic-slice_fusion), channel_id=1, source_target_pairs={{0,2},{1,3},{2,0},{3,1},{4,6},{5,7},{6,4},{7,5},{8,10},{9,11},{10,... | collective-permute-start | bytes 688136 | tf_op jit(solution)/shard_map/ppermute | solution.py:786
  195.3 11.4 %all-to-all-start.3 = ((f32[8,56,128]{2,1,0:T(8,128)}), f32[8,56,128]{2,1,0:T(8,128)S(1)}, u32[]{:S(2)}, u32[]{:S(2)}) async-start(f32[8,56,128]{2,1,0:T(8,128)} %broadcast_in_dim.2), calls=%async_computation.3 | async-start | bytes 458752 | tf_op jit(solution)/shard_map/all_to_all | solution.py:774
  206.7 6.0 %collective-permute-start.6 = (f32[448,128]{1,0:T(8,128)S(1)}, f32[448,128]{1,0:T(8,128)S(1)}, u32[]{:S(2)}, u32[]{:S(2)}) collective-permute-start(f32[448,128]{1,0:T(8,128)S(1)} %bitcast.67), channel_id=1, source_target_pairs={{0,2},{1,3},{2,0},{3,1},{4,6},{5,7},{6,4},{7,5},{8,10},{9,11},{10,... | collective-permute-start | bytes 688136 | tf_op jit(solution)/shard_map/ppermute | solution.py:786
  212.7 1.9 collective-permute-start.7

commit v3 on v2

--- a/solution.py
+++ b/solution.py
@@ -194,8 +194,8 @@
     rows, len_ref, cnt_ref, tm_ref, v_ref, xb_ref, xa_ref, gr_ref, gk_ref, w_ref, wr_ref, ws_ref, *rest
 ):
     params, rest = rest[: len(PARAMS)], rest[len(PARAMS) :]
-    ga_ref, f0_ref, f1_ref, f2_ref, z_ref, y_ref, ch_ref, st_ref, bias_ref, *rest = rest
-    w3, wt3, wg3, stat, fst, acc, gacc, yacc, gs0, gs1, hl0, hl1, gb = rest
+    ga_ref, f0_ref, f1_ref, d_ref, y_ref, ch_ref, st_ref, bias_ref, *rest = rest
+    w3, wt3, stat, fst, acc, gacc, yacc, gs0, gs1, hl0, hl1, gb = rest
     par = channel(dict(zip(PARAMS, params)))
     i = pl.program_id(0)
     items = ch_ref.shape[0]
@@ -209,8 +209,6 @@
         w3[...] = stacked3(0.5 * w_ref[...])
         both = jnp.concatenate([wr_ref[...], ws_ref[...]], axis=1)
         wt3[...] = stacked3(both.T)
-        gain = 2.0 * par("gain_out")
-        wg3[...] = stacked3((both.T * gain).T)
         mean, scale, _ = merged(ga_ref[...], width)
         stat[0] = jnp.broadcast_to(mean, stat.shape[1:])
         stat[1] = jnp.broadcast_to(scale, stat.shape[1:])
@@ -262,10 +260,6 @@
     def products(k):
         hl = hl_slots[k % 2]
 
-        def out(q):
-            hi, lo = hl[0, q : q + HALF, :], hl[1, q : q + HALF, :]
-            z_ref[0, k * rows + q : k * rows + q + HALF, :] = dot(jnp.concatenate([hi, hi, lo], axis=1), wg3[...])
-
         def weights(q):
             at = slice(q, q + base)
             ghi, glo = gb[k, 0, :, at], gb[k, 1, :, at]
@@ -275,8 +269,7 @@
             else:
                 yacc[at, :] = yacc[at, :] + y if k else y
 
-        return [functools.partial(out, q) for q in range(0, rows, HALF)] + [
-            functools.partial(weights, q) for q in (0, base)]
+        return [functools.partial(weights, q) for q in (0, base)]
 
     h = product3(jnp.concatenate([xb_ref[0], xa_ref[0]], axis=0), w3[...])
     for piece in spread(0):
@@ -341,7 +334,7 @@
                 f2 = d * dm
                 f0_ref[0, at, s] = f0
                 f1_ref[0, at, s] = dm
-                f2_ref[0, at, s] = f2
+                d_ref[0, at, s] = d
                 for r, x in (
                     (R_S, dd), (R_SS, dd * d), (R_GD, g * d), (R_H0, f0), (R_H1, dm), (R_H2, f2), (R_HF0, f0 * f),
                     (R_HF1, dm * f), (R_HF2, f2 * f), (R_PF0, g * f), (R_PF1, fm), (R_PF2, dd * f),
@@ -358,7 +351,7 @@
     def nothing(k):
         at = slice(k * rows, (k + 1) * rows)
         zero = jnp.zeros((rows, width), f32)
-        for ref in (f0_ref, f1_ref, f2_ref):
+        for ref in (f0_ref, f1_ref, d_ref):
             ref[0, at, :] = zero
         hl_slots[k % 2][...] = jnp.zeros_like(hl0)
         if k == 0:
@@ -389,8 +382,10 @@
             def _():
                 at = lax.broadcasted_iota(jnp.int32, (TAP, 1), 0) + t0
                 there = ((at < TAP) if row == R_A0 else (at >= length - TAP)).astype(f32)
-                for q, ref in enumerate((f0_ref, f1_ref, f2_ref)):
-                    acc[row + q] += fold(there * ref[0, pl.ds(r0, TAP), :])
+                f1 = there * f1_ref[0, pl.ds(r0, TAP), :]
+                acc[row] += fold(there * f0_ref[0, pl.ds(r0, TAP), :])
+                acc[row + 1] += fold(f1)
+                acc[row + 2] += fold(f1 * d_ref[0, pl.ds(r0, TAP), :])
         return 0
 
     lax.fori_loop(0, frames // TAP, edge, 0)
@@ -448,7 +443,7 @@
 
 
 def edge_kernel(
-    frames, len_ref, tm_ref, xb_ref, xa_ref, f0a_ref, f0z_ref, f1a_ref, f1z_ref, f2a_ref, f2z_ref,
+    frames, len_ref, tm_ref, xb_ref, xa_ref, f0a_ref, f0z_ref, f1a_ref, f1z_ref, da_ref, dz_ref,
     ch1_ref, ch_ref, w_ref, wr_ref, ws_ref, *rest
 ):
     params, rest = rest[: len(PARAMS)], rest[len(PARAMS) :]
@@ -549,10 +544,10 @@
     h = dot(jnp.concatenate([xhi, xhi, xlo], axis=1), w3[...])
     masks = (mask_rows(start - TAP, TAP, length), mask_rows(start + frames, TAP, length))
     taps = (gain1 * tap0, gain1 * tap2)
-    grads = ((f0a_ref, f1a_ref, f2a_ref), (f0z_ref, f1z_ref, f2z_ref))
+    grads = ((f0a_ref, f1a_ref, da_ref), (f0z_ref, f1z_ref, dz_ref))
     his, los = [], []
     for side in range(2):
-        f0, f1, f2 = grads[side]
+        f0, f1, d = grads[side]
         m = masks[side]
         hi_s, lo_s = [], []
         for s in blocks(width):
@@ -562,7 +557,7 @@
                 at = slice(q, q + SUB)
                 hq = h[side * TAP + q : side * TAP + q + SUB, s] + b1[:, s]
                 v, t = half_act(hq, a1[:, s], c1[:, s])
-                grad = m[at] * (c0[:, s] * f0[0, at, s] - cc[:, s] * f1[0, at, s] - beta[:, s] * f2[0, at, s])
+                grad = m[at] * (c0[:, s] * f0[0, at, s] - f1[0, at, s] * (cc[:, s] + beta[:, s] * d[0, at, s]))
                 u = taps[side][:, s] * grad
                 gh = u * (d_base[:, s] + d_gain[:, s] * t)
                 for k, x_ in enumerate((gh, u * hq, grad * v)):
@@ -584,12 +579,12 @@
 
 
 def third_kernel(
-    rows, len_ref, tm_ref, mine_ref, v_ref, x_ref, f0_ref, f1_ref, f2_ref, gr_ref, z_ref, y_ref,
-    ch_ref, bias_ref, w_ref, br_ref, bs_ref, stat, coef, chan, zc, gw0_ref, acc0_ref, *rest
+    rows, len_ref, tm_ref, mine_ref, v_ref, x_ref, f0_ref, f1_ref, d_ref, gr_ref, y_ref,
+    ch_ref, bias_ref, w_ref, wr_ref, ws_ref, br_ref, bs_ref, stat, coef, chan, zc, gw0_ref, acc0_ref, *rest
 ):
     params, rest = rest[: len(PARAMS)], rest[len(PARAMS) :]
     res_ref, skip_ref, gin_ref, keep_ref, send_ref, *rest = rest
-    w3, wt, ext, gw, gwt, acc, hb0, hb1, hl0, hl1 = rest
+    w3, wt, wg3, ext, gw, gwt, acc, hb0, hb1, hl0, hl1 = rest
     par = channel(dict(zip(PARAMS, params)))
     i = pl.program_id(0)
     items = ch_ref.shape[0]
@@ -603,6 +598,8 @@
     def _():
         w3[...] = stacked3(0.5 * w_ref[...])
         wt[...] = jnp.concatenate(split(w_ref[...].T), axis=1)
+        both = jnp.concatenate([wr_ref[...], ws_ref[...]], axis=1)
+        wg3[...] = stacked3((both.T * (2.0 * par("gain_out"))).T)
         zeros = jnp.zeros((2 * TAP, width), f32)
         ext[0 : 2 * TAP, :] = zeros
         ext[frames + 2 * TAP : frames + 4 * TAP, :] = zeros
@@ -685,19 +682,19 @@
     br, bs = br_ref[...], bs_ref[...]
     zi = zc[pl.ds(i, 1), :]
 
-    def outputs(n, kind):
-        at = slice(n * rows, (n + 1) * rows)
+    def outputs(n, kind, q):
+        at = slice(n * rows + q, n * rows + q + HALF)
         x = x_ref[0, at, :]
         if kind == "none":
             res_ref[0, at, :] = x + br
-            skip_ref[0, at, :] = jnp.broadcast_to(bs, (rows, base))
+            skip_ref[0, at, :] = jnp.broadcast_to(bs, (HALF, base))
             gin_ref[0, at, :] = gr_ref[0, at, :]
             return
-        z = z_ref[0, at, :]
+        z = product3(d_ref[0, at, :], wg3[...])
         to_res = scale_c * z[:, 0:base] + zi[:, 0:base]
         to_skip = scale_c * z[:, base:] + zi[:, base:]
         if kind == "some":
-            m = mask_rows(start + n * rows, rows, length)
+            m = mask_rows(start + n * rows + q, HALF, length)
             to_res, to_skip = to_res * m, to_skip * m
         res_ref[0, at, :] = (x + to_res) + br
         skip_ref[0, at, :] = to_skip + bs
@@ -707,24 +704,24 @@
             for q in range(k * rows, (k + 1) * rows, SUB):
                 at = slice(q, q + SUB)
                 ext[2 * TAP + q : 2 * TAP + q + SUB, s] = (
-                    c0[:, s] * f0_ref[0, at, s] - cc[:, s] * f1_ref[0, at, s] - beta[:, s] * f2_ref[0, at, s]
+                    c0[:, s] * f0_ref[0, at, s] - f1_ref[0, at, s] * (cc[:, s] + beta[:, s] * d_ref[0, at, s])
                 )
 
     interleave(spread(0), [functools.partial(lift, k) for k in range(parts)])
     for n in range(parts):
         def step(kind, n=n):
             ahead = spread(n + 1) if n + 1 < parts else []
+            shown = [functools.partial(outputs, n, kind, q) for q in range(0, rows, HALF)]
             if kind == "none":
-                for piece in ahead + [functools.partial(outputs, n, kind)]:
+                for piece in ahead + shown:
                     piece()
                 return
             vector = elementwise(n, kind == "some")
             weights, *outs = products(n)
             each = len(vector) // len(outs)
             for j, out in enumerate(outs):
-                interleave(ahead[j : j + 1] or [lambda: None], vector[j * each : (j + 1) * each])
+                interleave(ahead[j : j + 1] + shown[j : j + 1], vector[j * each : (j + 1) * each])
                 out()
-            outputs(n, kind)
             weights()
 
         t0 = start + n * rows
@@ -852,25 +849,24 @@
                    jax.ShapeDtypeStruct((items, 8, width), f32)],
         scratch_shapes=[pltpu.VMEM((3 * base, width), bf16), pltpu.VMEM((2, 8, width), f32)]
         + [pltpu.VMEM((rows1, width), f32)] * 2,
-        compiler_params=vmem(48),
+        compiler_params=vmem(58),
         name="first",
     )(lengths, place, inputs, inputs, weight_in, table[0], table[1])
     ga1 = exchange(st1, "tm")
 
     big = jax.ShapeDtypeStruct((items, frames, width), f32)
-    f0, f1, f2, z, y, ch, st2, bias = pl.pallas_call(
+    f0, f1, d2, y, ch, st2, bias = pl.pallas_call(
         functools.partial(second_kernel, rows2),
         grid=(items,),
         in_specs=[SMEM, SMEM, SMEM, per_item((frames, width)), per_item((TAP, base)), per_item((TAP, base)),
                   per_item((frames, base)), per_item((sources, frames, base)), whole((base, width)),
                   whole((width, base)), whole((width, base))] + table_specs + [whole((tm, items, LANES))],
-        out_specs=[per_item((frames, width))] * 3 + [per_item((frames, 2 * base)), per_item((2 * base, width)),
+        out_specs=[per_item((frames, width))] * 3 + [per_item((2 * base, width)),
                    whole((items, ROWS, width)), whole((tm, items, LANES)), whole((8, 2 * base))],
-        out_shape=[big, big, big, jax.ShapeDtypeStruct((items, frames, 2 * base), f32),
-                   jax.ShapeDtypeStruct((items, 2 * base, width), f32), jax.ShapeDtypeStruct((items, ROWS, width), f32),
+        out_shape=[big, big, big, jax.ShapeDtypeStruct((items, 2 * base, width), f32), jax.ShapeDtypeStruct((items, ROWS, width), f32),
                    jax.ShapeDtypeStruct((tm, items, LANES), f32), jax.ShapeDtypeStruct((8, 2 * base), f32)],
         scratch_shapes=[pltpu.VMEM((3 * base, width), bf16), pltpu.VMEM((6 * base, width), bf16),
-                        pltpu.VMEM((3 * width, 2 * base), bf16), pltpu.VMEM((2, items, LANES), f32),
+                        pltpu.VMEM((2, items, LANES), f32),
                         pltpu.VMEM((frames + 2 * TAP, width), f32), pltpu.VMEM((ROWS, 8, width), f32),
                         pltpu.VMEM((8, 2 * base), f32), pltpu.VMEM((2 * base, width), f32)]
         + [pltpu.VMEM((rows2, width), f32)] * 2 + [pltpu.VMEM((2, rows2, width), bf16)] * 2
@@ -899,7 +895,7 @@
         scratch_shapes=[pltpu.VMEM((3 * base, width), bf16), pltpu.VMEM((3 * width, base), bf16)],
         compiler_params=vmem(48),
         name="edge",
-    )(lengths, place, x_before, x_after, f0, f0, f1, f1, f2, f2, ch1, ch, weight_in, weight_res, weight_skip, *table,
+    )(lengths, place, x_before, x_after, f0, f0, f1, f1, d2, d2, ch1, ch, weight_in, weight_res, weight_skip, *table,
       ga1, ga2)
     from_next = lax.ppermute(to_last, "tm", down)
     from_last = lax.ppermute(to_next, "tm", up)
@@ -909,12 +905,14 @@
         grid=(items,),
         in_specs=[SMEM, SMEM, SMEM, per_item((frames, width)), per_item((frames, base)), per_item((frames, width)),
                   per_item((frames, width)), per_item((frames, width)), per_item((frames, base)),
-                  per_item((frames, 2 * base)), per_item((2 * base, width)), whole((items, ROWS, width)),
-                  whole((8, 2 * base)), whole((base, width)), whole((1, base)), whole((1, base))]
+                  per_item((2 * base, width)), whole((items, ROWS, width)),
+                  whole((8, 2 * base)), whole((base, width)), whole((width, base)), whole((width, base)),
+                  whole((1, base)), whole((1, base))]
         + [whole(shape) for shape, _ in small] + table_specs,
         out_specs=[per_item((frames, base))] * 3 + [whole((n_sum // 2, base))] * 2,
         out_shape=[out, out, out] + [jax.ShapeDtypeStruct((n_sum // 2, base), f32)] * 2,
         scratch_shapes=[pltpu.VMEM((3 * base, width), bf16), pltpu.VMEM((width, 2 * base), bf16),
+                        pltpu.VMEM((3 * width, 2 * base), bf16),
                         pltpu.VMEM((frames + 4 * TAP, width), f32),
                         pltpu.VMEM((base, width), f32), pltpu.VMEM((2 * base, width), f32),
                         pltpu.VMEM((8, 8, width), f32)]
@@ -923,7 +921,7 @@
         cost_estimate=pl.CostEstimate(flops=items * frames * width * base * 30, transcendentals=items * frames * width,
                                       bytes_accessed=items * frames * (5 * width + 7 * base) * 4),
         name="third",
-    )(lengths, place, mine, v1, inputs, f0, f1, f2, grad_residual, z, y, ch, bias, weight_in, row(bias_res), row(bias_skip),
+    )(lengths, place, mine, v1, inputs, f0, f1, d2, grad_residual, y, ch, bias, weight_in, weight_res, weight_skip, row(bias_res), row(bias_skip),
       *given, *table)
 
     sums, from_next, from_last = lax.optimization_barrier((sums, from_next, from_last))

time: 219 us -> 213 us (0.973)
  local copies, waits for them, and re-layouts: 10.6 us -> 5.43 us
    unnamed x42 -> x34, local copies, waits for them, and re-layouts: 5.24 us -> 0.1 us
    pallas_call x1, Pallas kernels: 58.6 us -> 54.1 us  [body(): pl.pallas_call(functools.partial(second_kernel, rows2), grid=(items,), in...]
    pallas_call x1, Pallas kernels: 44.8 us -> 47.2 us  [body(): pl.pallas_call(functools.partial(third_kernel, rows3), grid=(items,), in_...]
  transfers between devices with their start and end apart: 10 -> 10, of which waited for: 6 -> 6; matrix products, arithmetic and copies ran while one was open for 2% -> 2% of each run, Pallas kernels for 28% -> 30%
where the time goes in v3:
time: 213 us; the launch traced here: 212 us
  Pallas kernels  130 us (61%)
  waiting for transfers between devices  25 us (12%)
  blocking collectives  23.6 us (11%)
  starting transfers between devices  22.9 us (11%)
  local copies, waits for them, and re-layouts  5.43 us (3%)
  other arithmetic  3.97 us (2%)
    pallas_call x1, Pallas kernels, body(): pl.pallas_call(functools.partial(second_kernel, rows2), grid=(items,), in...  54.1 us
    pallas_call x1, Pallas kernels, body(): pl.pallas_call(functools.partial(third_kernel, rows3), grid=(items,), in_...  47.2 us
    all_to_all x2, blocking collectives, exchange(): return lax.all_to_all(x, axis, 0, 0)  23.6 us
    pallas_call x1, Pallas kernels, body(): pl.pallas_call(functools.partial(first_kernel, rows1), grid=(items,), in_...  16.5 us
    all_to_all x2, waiting for transfers between devices, exchange(): return lax.all_to_all(x, axis, 0, 0)  12.7 us
    ppermute x4, waiting for transfers between devices, swap(): return lax.ppermute(y, 'item', [(d, d ^ by) for d in range(n_item)])  12.3 us
    pallas_call x1, Pallas kernels, body(): pl.pallas_call(functools.partial(edge_kernel, frames), grid=(items,), in_...  12.2 us
    all_to_all x2, starting transfers between devices, exchange(): return lax.all_to_all(x, axis, 0, 0)  6.98 us
  transfers between devices with their start and end apart: 10, of which 6 were waited for; matrix products, arithmetic and copies ran while one was open for 2% of the time, Pallas kernels for 30%

profile of v3, /device:TPU:0, one launch (start us, length us, event | category | flops | bytes accessed | tf_op | source)
XLA Modules:
  0.0 211.9 jit_solution(4395334549567417256)
XLA Ops:
  0.7 1.3 fusion.1
  2.0 1.3 collective-permute-start.1
  3.3 5.5 %collective-permute-start = (f32[8,128,128]{2,1,0:T(8,128)S(1)}, f32[8,128,128]{2,1,0:T(8,128)S(1)}, u32[]{:S(2)}, u32[]{:S(2)}) collective-permute-start(f32[8,128,128]{2,1,0:T(8,128)S(1)} %get-tuple-element.100), channel_id=1, source_target_pairs={{0,4},{4,8},{8,12},{12,16},{16,20},{20,24},{24,28},{1,5},{5,9},{9,... | collective-permute-start | bytes 1572872 | tf_op jit(solution)/shard_map/ppermute | solution.py:829
  8.8 0.0 copy-start
  8.8 0.0 copy-start.1
  8.8 0.0 copy-start.2
  8.8 0.0 copy-start.4
  8.8 0.0 copy-start.5
  8.8 0.0 copy-start.6
  8.8 0.0 copy-start.7
  8.9 0.0 copy-start.8
  8.9 0.0 copy-start.9
  8.9 0.0 copy-start.10
  8.9 0.0 copy-start.11
  8.9 0.0 copy-start.12
  8.9 0.0 copy-start.13
  8.9 0.0 copy-start.14
  8.9 16.5 %first.1 = (f32[8,1024,512]{2,1,0:T(8,128)}, f32[8,8,128]{2,1,0:T(8,128)}, f32[8,8,512]{2,1,0:T(8,128)}) custom-call(s32[8]{0:T(128)} %len_ref.7, s32[1]{0:T(128)} %bitcast.tm_ref, f32[8,1024,128]{2,1,0:T(8,128)} %x_ref.3, f32[8,1024,128]{2,1,0:T(8,128)} %x_ref.3, f32[128,512]{1,0:T(8,128)} %w_ref.7, f32[1,512]{1,0:T(1,128)} %bitcast.38, f32[1,512]{1,0:T(1,128)} %bitcast.42), custom_call_target="tpu_custom_call" | custom-call | tf_op jit(solution)/shard_map/first/pallas_call | solution.py:841
  25.4 13.0 %all_to_all.20.rest_9_ = f32[8,8,128]{2,1,0:T(8,128)S(1)} all-to-all(f32[8,8,128]{2,1,0:T(8,128)} %get-tuple-element.71), channel_id=1, replica_groups=mesh['tm'=8,'item'=4] {'tm'}, dimensions={0} | all-to-all | bytes 65536 | tf_op jit(solution)/shard_map/all_to_all | solution.py:771
  38.4 0.0 collective-permute-done.1.xa_ref
  38.4 0.0 collective-permute-done.xb_ref
  38.4 0.0 copy-done
  38.4 0.0 copy-done.1
  38.4 0.0 copy-done.2
  38.5 0.0 copy-done.4
  38.5 0.0 copy-done.5
  38.5 0.0 copy-done.6
  38.5 0.0 copy-done.7
  38.5 0.0 copy-done.8
  38.5 0.0 copy-done.9
  38.5 0.0 copy-done.10
  38.5 0.0 copy-done.11
  38.5 0.0 copy-done.12
  38.5 0.0 copy-done.13
  38.6 0.0 copy-start.3
  38.6 54.1 %second.1 = (f32[8,1024,512]{2,1,0:T(8,128)}, f32[8,1024,512]{2,1,0:T(8,128)}, f32[8,1024,512]{2,1,0:T(8,128)}, f32[8,256,512]{2,1,0:T(8,128)}, f32[8,24,512]{2,...) custom-call(s32[8]{0:T(128)S(1)} %copy-done.13, s32[8]{0:T(128)S(1)} %copy-done.14, s32[1]{0:T(128)} %bitcast.tm_ref, ...), custom_call_target="tpu_custom_call" | custom-call | tf_op jit(solution)/shard_map/second/pallas_call | solution.py:858
  92.6 3.6 %all-to-all-start.1 = ((f32[8,8,128]{2,1,0:T(8,128)}), f32[8,8,128]{2,1,0:T(8,128)S(1)}, u32[]{:S(2)}, u32[]{:S(2)}) async-start(f32[8,8,128]{2,1,0:T(8,128)} %get-tuple-element.79), calls=%async_computation.1 | async-start | bytes 65536 | tf_op jit(solution)/shard_map/all_to_all | solution.py:771
  96.2 6.6 %all-to-all-done.1.rest_10_ = f32[8,8,128]{2,1,0:T(8,128)S(1)} async-done(((f32[8,8,128]{2,1,0:T(8,128)}), f32[8,8,128]{2,1,0:T(8,128)S(1)}, u32[]{:S(2)}, u32[]{:S(2)}) %all-to-all-start.1) | async-done | bytes 32800 | tf_op jit(solution)/shard_map/all_to_all | solution.py:771
  102.9 12.2 %edge.1 = (f32[8,128,128]{2,1,0:T(8,128)S(1)}, f32[8,128,128]{2,1,0:T(8,128)S(1)}, f32[5,8,128]{2,1,0:T(8,128)S(1)}, f32[3,8,512]{2,1,0:T(8,128)S(1)}, f32[16,51...) custom-call(s32[8]{0:T(128)S(1)} %copy-done.13, s32[1]{0:T(128)} %bitcast.tm_ref, ...), custom_call_target="tpu_custom_call" | custom-call | tf_op jit(solution)/shard_map/edge/pallas_call | solution.py:886
  115.1 1.3 collective-permute-start.2
  116.4 4.6 %collective-permute-start.3 = (f32[8,128,128]{2,1,0:T(8,128)S(1)}, f32[8,128,128]{2,1,0:T(8,128)S(1)}, u32[]{:S(2)}, u32[]{:S(2)}) collective-permute-start(f32[8,128,128]{2,1,0:T(8,128)S(1)} %get-tuple-element.91), channel_id=1, source_target_pairs={{0,4},{4,8},{8,12},{12,16},{16,20},{20,24},{24,28},{1,5},{5,9},{9,... | collective-permute-start | bytes 1572872 | tf_op jit(solution)/shard_map/ppermute | solution.py:901
  121.0 47.2 %third.1 = (f32[8,1024,128]{2,1,0:T(8,128)}, f32[8,1024,128]{2,1,0:T(8,128)}, f32[8,1024,128]{2,1,0:T(8,128)}, f32[896,128]{1,0:T(8,128)S(1)}, f32[896,128]{1,0:T(8,128)S(1)}) custom-call(s32[8]{0:T(128)S(1)} %copy-done.13, s32[1]{0:T(128)} %bitcast.tm_ref, s32[1]{0:T(128)} %bitcast.1.mine_ref, f32[8,1024,512]{2,1,0:T(8,128)} %get-tuple-element.70.v_ref, ...), custom_call_target="tpu_custom_call" | custom-call | flops 16106127360 | bytes 113246208 | tf_op jit(solution)/shard_map/third/pallas_call | solution.py:903
  168.2 0.0 collective-permute-done.2
  168.2 0.0 collective-permute-done.3
  168.2 0.1 collective-permute-start.4
  168.3 1.8 collective-permute-done.4
  170.2 1.6 collective-permute-start.5
  171.8 6.1 %collective-permute-done.5 = f32[448,128]{1,0:T(8,128)S(1)} collective-permute-done((f32[448,128]{1,0:T(8,128)S(1)}, f32[448,128]{1,0:T(8,128)S(1)}, u32[]{:S(2)}, u32[]{:S(2)}) %collective-permute-start.5) | collective-permute-done | bytes 229408 | tf_op jit(solution)/shard_map/ppermute | solution.py:783
  177.9 10.6 %all_to_all.21 = f32[8,56,128]{2,1,0:T(8,128)S(1)} all-to-all(f32[8,56,128]{2,1,0:T(8,128)S(1)} %bitcast.69), channel_id=1, replica_groups=mesh['tm'=8,'item'=4] {'tm'}, dimensions={0} | all-to-all | bytes 458752 | tf_op jit(solution)/shard_map/all_to_all | solution.py:771
  188.5 0.7 broadcast_in_dim.2
  189.2 3.4 %all-to-all-start.3 = ((f32[8,56,128]{2,1,0:T(8,128)}), f32[8,56,128]{2,1,0:T(8,128)S(1)}, u32[]{:S(2)}, u32[]{:S(2)}) async-start(f32[8,56,128]{2,1,0:T(8,128)} %broadcast_in_dim.2), calls=%async_computation.3 | async-start | bytes 458752 | tf_op jit(solution)/shard_map/all_to_all | solution.py:771
  192.7 1.9 add_dynamic-update-slice_fusion
  194.6 6.1 %all-to-all-done.3 = f32[8,56,128]{2,1,0:T(8,128)S(1)} async-done(((f32[8,56,128]{2,1,0:T(8,128)}), f32[8,56,128]{2,1,0:T(8,128)S(1)}, u32[]{:S(2)}, u32[]{:S(2)}) %all-to-all-start.3) | async-done | bytes 229408 | tf_op jit(solution)/shard_map/all_to_all | solution.py:771
  200.6 1.5 collective-permute-start.6
  202.2 1.9 fusion
  204.0 2.6 %collective-permute-done.6 = f32[448,128]{1,0:T(8,128)S(1)} collective-permute-done((f32[448,128]{1,0:T(8,128)S(1)}, f32[448,128]{1,0:T(8,128)S(1)}, u32[]{:S(2)}, u32[]{:S(2)}) %collective-permute-start.6) | collective-permute-done | bytes 229408 | tf_op jit(solution)/shard_map/ppermute | solution.py:783
  206.7 0.1 collective-permute-start.7
  206.8 1.8 collective-permute-done.7
  208.6 0.1 maximum_select_fusion
  208.6 0.5 slice_bitcast_fusion.1
  209.2 0.8 fusion.2
  210.0 0.6 slice_bitcast_fusion
  210.6 0.6 fusion.3
  211.2 0.7 copy.40
  (12 shorter events, 0.2 us)
Async XLA Ops:
  2.0 36.5 %collective-permute-start.1 = (f32[8,128,128]{2,1,0:T(8,128)S(1)}, f32[8,128,128]{2,1,0:T(8,128)S(1)}, u32[]{:S(2)}, u32[]{:S(2)}) collective-permute-start(f32[8,128,128]{2,1,0:T(8,128)S(1)} %get-tuple-element.99), channel_id=1, source_target_pairs={{4,0},{8,4},{12,8},{16,12},{20,16},{24,20},{28,24},{5,1},{9,5},{13... | collective-permute-start | bytes 1572872 | tf_op jit(solution)/shard_map/ppermute | solution.py:830
  3.3 35.2 %collective-permute-start = (f32[8,128,128]{2,1,0:T(8,128)S(1)}, f32[8,128,128]{2,1,0:T(8,128)S(1)}, u32[]{:S(2)}, u32[]{:S(2)}) collective-permute-start(f32[8,128,128]{2,1,0:T(8,128)S(1)} %get-tuple-element.100), channel_id=1, source_target_pairs={{0,4},{4,8},{8,12},{12,16},{16,20},{20,24},{24,28},{1,5},{5,9},{9,... | collective-permute-start | bytes 1572872 | tf_op jit(solution)/shard_map/ppermute | solution.py:829
  8.8 29.7 %copy-start = (f32[128,512]{1,0:T(8,128)S(1)}, f32[128,512]{1,0:T(8,128)}, u32[]{:S(2)}) copy-start(f32[128,512]{1,0:T(8,128)} %w_ref.7) | copy-start | bytes 786436
  8.8 29.7 %copy-start.1 = (f32[512,128]{1,0:T(8,128)S(1)}, f32[512,128]{1,0:T(8,128)}, u32[]{:S(2)}) copy-start(f32[512,128]{1,0:T(8,128)} %wr_ref.5) | copy-start | bytes 786436
  8.8 29.6 %copy-start.2 = (f32[512,128]{1,0:T(8,128)S(1)}, f32[512,128]{1,0:T(8,128)}, u32[]{:S(2)}) copy-start(f32[512,128]{1,0:T(8,128)} %ws_ref.5) | copy-start | bytes 786436
  8.8 29.6 %copy-start.4 = (f32[3,512]{1,0:T(4,128)S(1)}, f32[3,512]{1,0:T(4,128)}, u32[]{:S(2)}) copy-start(f32[3,512]{1,0:T(4,128)} %rest_4_.5) | copy-start | bytes 18436
  8.8 29.6 %copy-start.5 = (f32[512]{0:T(512)S(1)}, f32[512]{0:T(512)}, u32[]{:S(2)}) copy-start(f32[512]{0:T(512)} %param.27) | copy-start | bytes 6148
  8.8 29.6 %copy-start.6 = (f32[512]{0:T(512)S(1)}, f32[512]{0:T(512)}, u32[]{:S(2)}) copy-start(f32[512]{0:T(512)} %param.28) | copy-start | bytes 6148
  8.8 29.6 %copy-start.7 = (f32[512]{0:T(512)S(1)}, f32[512]{0:T(512)}, u32[]{:S(2)}) copy-start(f32[512]{0:T(512)} %param.29) | copy-start | bytes 6148
  8.9 29.6 %copy-start.8 = (f32[512]{0:T(512)S(1)}, f32[512]{0:T(512)}, u32[]{:S(2)}) copy-start(f32[512]{0:T(512)} %param.30) | copy-start | bytes 6148
  8.9 29.6 %copy-start.9 = (f32[512]{0:T(512)S(1)}, f32[512]{0:T(512)}, u32[]{:S(2)}) copy-start(f32[512]{0:T(512)} %param.32) | copy-start | bytes 6148
  8.9 29.6 %copy-start.10 = (f32[512]{0:T(512)S(1)}, f32[512]{0:T(512)}, u32[]{:S(2)}) copy-start(f32[512]{0:T(512)} %param.33) | copy-start | bytes 6148
  8.9 29.6 %copy-start.11 = (f32[512]{0:T(512)S(1)}, f32[512]{0:T(512)}, u32[]{:S(2)}) copy-start(f32[512]{0:T(512)} %param.34) | copy-start | bytes 6148
  8.9 29.6 %copy-start.12 = (f32[512]{0:T(512)S(1)}, f32[512]{0:T(512)}, u32[]{:S(2)}) copy-start(f32[512]{0:T(512)} %param.35) | copy-start | bytes 6148
  8.9 29.6 %copy-start.13 = (s32[8]{0:T(128)S(1)}, s32[8]{0:T(128)}, u32[]{:S(2)}) copy-start(s32[8]{0:T(128)} %len_ref.7) | copy-start | bytes 100
  8.9 29.6 %copy-start.14 = (s32[8]{0:T(128)S(1)}, s32[8]{0:T(128)}, u32[]{:S(2)}) copy-start(s32[8]{0:T(128)} %cnt_ref.1) | copy-start | bytes 100
  38.6 64.3 %copy-start.3 = (f32[8,8,512]{2,1,0:T(8,128)S(1)}, f32[8,8,512]{2,1,0:T(8,128)}, u32[]{:S(2)}) copy-start(f32[8,8,512]{2,1,0:T(8,128)} %get-tuple-element.78.ch1_ref) | copy-start | bytes 393220
  92.6 10.2 %all-to-all-start.1 = ((f32[8,8,128]{2,1,0:T(8,128)}), f32[8,8,128]{2,1,0:T(8,128)S(1)}, u32[]{:S(2)}, u32[]{:S(2)}) async-start(f32[8,8,128]{2,1,0:T(8,128)} %get-tuple-element.79), calls=%async_computation.1 | async-start | bytes 65536 | tf_op jit(solution)/shard_map/all_to_all | solution.py:771
  102.9 18.1 %copy-start.15 = (f32[128]{0:T(128)S(1)}, f32[128]{0:T(128)}, u32[]{:S(2)}) copy-start(f32[128]{0:T(128)} %param.37) | copy-start | bytes 1540
  102.9 18.1 %copy-start.16 = (f32[128]{0:T(128)S(1)}, f32[128]{0:T(128)}, u32[]{:S(2)}) copy-start(f32[128]{0:T(128)} %param.39) | copy-start | bytes 1540
  115.1 53.1 %collective-permute-start.2 = (f32[8,128,128]{2,1,0:T(8,128)S(1)}, f32[8,128,128]{2,1,0:T(8,128)S(1)}, u32[]{:S(2)}, u32[]{:S(2)}) collective-permute-start(f32[8,128,128]{2,1,0:T(8,128)S(1)} %get-tuple-element.90), channel_id=1, source_target_pairs={{4,0},{8,4},{12,8},{16,12},{20,16},{24,20},{28,24},{5,1},{9,5},{13... | collective-permute-start | bytes 1572872 | tf_op jit(solution)/shard_map/ppermute | solution.py:900
  116.4 51.8 %collective-permute-start.3 = (f32[8,128,128]{2,1,0:T(8,128)S(1)}, f32[8,128,128]{2,1,0:T(8,128)S(1)}, u32[]{:S(2)}, u32[]{:S(2)}) collective-permute-start(f32[8,128,128]{2,1,0:T(8,128)S(1)} %get-tuple-element.91), channel_id=1, source_target_pairs={{0,4},{4,8},{8,12},{12,16},{16,20},{20,24},{24,28},{1,5},{5,9},{9,... | collective-permute-start | bytes 1572872 | tf_op jit(solution)/shard_map/ppermute | solution.py:901
  168.2 1.9 collective-permute-start.4
  170.2 7.7 %collective-permute-start.5 = (f32[448,128]{1,0:T(8,128)S(1)}, f32[448,128]{1,0:T(8,128)S(1)}, u32[]{:S(2)}, u32[]{:S(2)}) collective-permute-start(f32[448,128]{1,0:T(8,128)S(1)} %constant_dynamic-slice_fusion), channel_id=1, source_target_pairs={{0,2},{1,3},{2,0},{3,1},{4,6},{5,7},{6,4},{7,5},{8,10},{9,11},{10,... | collective-permute-start | bytes 688136 | tf_op jit(solution)/shard_map/ppermute | solution.py:783
  189.2 11.4 %all-to-all-start.3 = ((f32[8,56,128]{2,1,0:T(8,128)}), f32[8,56,128]{2,1,0:T(8,128)S(1)}, u32[]{:S(2)}, u32[]{:S(2)}) async-start(f32[8,56,128]{2,1,0:T(8,128)} %broadcast_in_dim.2), calls=%async_computation.3 | async-start | bytes 458752 | tf_op jit(solution)/shard_map/all_to_all | solution.py:771
  200.6 6.0 %collective-permute-start.6 = (f32[448,128]{1,0:T(8,128)S(1)}, f32[448,128]{1,0:T(8,128)S(1)}, u32[]{:S(2)}, u32[]{:S(2)}) collective-permute-start(f32[448,128]{1,0:T(8,128)S(1)} %bitcast.67), channel_id=1, source_target_pairs={{0,2},{1,3},{2,0},{3,1},{4,6},{5,7},{6,4},{7,5},{8,10},{9,11},{10,... | collective-permute-start | bytes 688136 | tf_op jit(solution)/shard_map/ppermute | solution.py:783
  206.7 1.9 collective-permute-start.7

commit v4 on v3

--- a/solution.py
+++ b/solution.py
@@ -20,7 +20,7 @@
 ROWS = 24
 SUB = 32
 HALF = 128
-CHUNK1, CHUNK2, CHUNK3 = 256, 256, 256
+CHUNK1, CHUNK2, CHUNK3 = 512, 256, 256
 
 
 def split(x):

time: 213 us -> 212 us (level)
  no operation moved by 1% of the time
where the time goes in v4:
time: 212 us; the launch traced here: 211 us
  Pallas kernels  129 us (61%)
  waiting for transfers between devices  24.7 us (12%)
  blocking collectives  23.6 us (11%)
  starting transfers between devices  23.3 us (11%)
  local copies, waits for them, and re-layouts  5.43 us (3%)
  other arithmetic  3.97 us (2%)
    pallas_call x1, Pallas kernels, body(): pl.pallas_call(functools.partial(second_kernel, rows2), grid=(items,), in...  54.1 us
    pallas_call x1, Pallas kernels, body(): pl.pallas_call(functools.partial(third_kernel, rows3), grid=(items,), in_...  47.2 us
    all_to_all x2, blocking collectives, exchange(): return lax.all_to_all(x, axis, 0, 0)  23.6 us
    pallas_call x1, Pallas kernels, body(): pl.pallas_call(functools.partial(first_kernel, rows1), grid=(items,), in_...  15.8 us
    all_to_all x2, waiting for transfers between devices, exchange(): return lax.all_to_all(x, axis, 0, 0)  12.7 us
    pallas_call x1, Pallas kernels, body(): pl.pallas_call(functools.partial(edge_kernel, frames), grid=(items,), in_...  12.2 us
    ppermute x4, waiting for transfers between devices, swap(): return lax.ppermute(y, 'item', [(d, d ^ by) for d in range(n_item)])  12 us
    all_to_all x2, starting transfers between devices, exchange(): return lax.all_to_all(x, axis, 0, 0)  6.98 us
  transfers between devices with their start and end apart: 10, of which 6 were waited for; matrix products, arithmetic and copies ran while one was open for 2% of the time, Pallas kernels for 30%

profile of v4, /device:TPU:0, one launch (start us, length us, event | category | flops | bytes accessed | tf_op | source)
XLA Modules:
  0.0 211.3 jit_solution(5580219685422791169)
XLA Ops:
  0.7 1.3 fusion.1
  2.0 1.3 collective-permute-start.1
  3.3 5.5 %collective-permute-start = (f32[8,128,128]{2,1,0:T(8,128)S(1)}, f32[8,128,128]{2,1,0:T(8,128)S(1)}, u32[]{:S(2)}, u32[]{:S(2)}) collective-permute-start(f32[8,128,128]{2,1,0:T(8,128)S(1)} %get-tuple-element.100), channel_id=1, source_target_pairs={{0,4},{4,8},{8,12},{12,16},{16,20},{20,24},{24,28},{1,5},{5,9},{9,... | collective-permute-start | bytes 1572872 | tf_op jit(solution)/shard_map/ppermute | solution.py:829
  8.8 0.0 copy-start
  8.8 0.0 copy-start.1
  8.8 0.0 copy-start.2
  8.8 0.0 copy-start.4
  8.8 0.0 copy-start.5
  8.8 0.0 copy-start.6
  8.8 0.0 copy-start.7
  8.9 0.0 copy-start.8
  8.9 0.0 copy-start.9
  8.9 0.0 copy-start.10
  8.9 0.0 copy-start.11
  8.9 0.0 copy-start.12
  8.9 0.0 copy-start.13
  8.9 0.0 copy-start.14
  8.9 15.8 %first.1 = (f32[8,1024,512]{2,1,0:T(8,128)}, f32[8,8,128]{2,1,0:T(8,128)}, f32[8,8,512]{2,1,0:T(8,128)}) custom-call(s32[8]{0:T(128)} %len_ref.7, s32[1]{0:T(128)} %bitcast.tm_ref, f32[8,1024,128]{2,1,0:T(8,128)} %x_ref.3, f32[8,1024,128]{2,1,0:T(8,128)} %x_ref.3, f32[128,512]{1,0:T(8,128)} %w_ref.7, f32[1,512]{1,0:T(1,128)} %bitcast.38, f32[1,512]{1,0:T(1,128)} %bitcast.42), custom_call_target="tpu_custom_call" | custom-call | tf_op jit(solution)/shard_map/first/pallas_call | solution.py:841
  24.7 12.9 %all_to_all.20.rest_9_ = f32[8,8,128]{2,1,0:T(8,128)S(1)} all-to-all(f32[8,8,128]{2,1,0:T(8,128)} %get-tuple-element.71), channel_id=1, replica_groups=mesh['tm'=8,'item'=4] {'tm'}, dimensions={0} | all-to-all | bytes 65536 | tf_op jit(solution)/shard_map/all_to_all | solution.py:771
  37.6 0.0 collective-permute-done.1.xa_ref
  37.6 0.0 collective-permute-done.xb_ref
  37.6 0.0 copy-done
  37.6 0.0 copy-done.1
  37.6 0.0 copy-done.2
  37.6 0.0 copy-done.4
  37.6 0.0 copy-done.5
  37.6 0.0 copy-done.6
  37.7 0.0 copy-done.7
  37.7 0.0 copy-done.8
  37.7 0.0 copy-done.9
  37.7 0.0 copy-done.10
  37.7 0.0 copy-done.11
  37.7 0.0 copy-done.12
  37.7 0.0 copy-start.3
  37.7 54.1 %second.1 = (f32[8,1024,512]{2,1,0:T(8,128)}, f32[8,1024,512]{2,1,0:T(8,128)}, f32[8,1024,512]{2,1,0:T(8,128)}, f32[8,256,512]{2,1,0:T(8,128)}, f32[8,24,512]{2,...) custom-call(s32[8]{0:T(128)S(1)} %copy-done.13, s32[8]{0:T(128)S(1)} %copy-done.14, s32[1]{0:T(128)} %bitcast.tm_ref, ...), custom_call_target="tpu_custom_call" | custom-call | tf_op jit(solution)/shard_map/second/pallas_call | solution.py:858
  91.8 3.6 %all-to-all-start.1 = ((f32[8,8,128]{2,1,0:T(8,128)}), f32[8,8,128]{2,1,0:T(8,128)S(1)}, u32[]{:S(2)}, u32[]{:S(2)}) async-start(f32[8,8,128]{2,1,0:T(8,128)} %get-tuple-element.79), calls=%async_computation.1 | async-start | bytes 65536 | tf_op jit(solution)/shard_map/all_to_all | solution.py:771
  95.4 6.6 %all-to-all-done.1.rest_10_ = f32[8,8,128]{2,1,0:T(8,128)S(1)} async-done(((f32[8,8,128]{2,1,0:T(8,128)}), f32[8,8,128]{2,1,0:T(8,128)S(1)}, u32[]{:S(2)}, u32[]{:S(2)}) %all-to-all-start.1) | async-done | bytes 32800 | tf_op jit(solution)/shard_map/all_to_all | solution.py:771
  102.0 0.0 copy-done.3
  102.0 12.2 %edge.1 = (f32[8,128,128]{2,1,0:T(8,128)S(1)}, f32[8,128,128]{2,1,0:T(8,128)S(1)}, f32[5,8,128]{2,1,0:T(8,128)S(1)}, f32[3,8,512]{2,1,0:T(8,128)S(1)}, f32[16,51...) custom-call(s32[8]{0:T(128)S(1)} %copy-done.13, s32[1]{0:T(128)} %bitcast.tm_ref, ...), custom_call_target="tpu_custom_call" | custom-call | tf_op jit(solution)/shard_map/edge/pallas_call | solution.py:886
  114.2 1.3 collective-permute-start.2
  115.5 4.6 %collective-permute-start.3 = (f32[8,128,128]{2,1,0:T(8,128)S(1)}, f32[8,128,128]{2,1,0:T(8,128)S(1)}, u32[]{:S(2)}, u32[]{:S(2)}) collective-permute-start(f32[8,128,128]{2,1,0:T(8,128)S(1)} %get-tuple-element.91), channel_id=1, source_target_pairs={{0,4},{4,8},{8,12},{12,16},{16,20},{20,24},{24,28},{1,5},{5,9},{9,... | collective-permute-start | bytes 1572872 | tf_op jit(solution)/shard_map/ppermute | solution.py:901
  120.2 47.2 %third.1 = (f32[8,1024,128]{2,1,0:T(8,128)}, f32[8,1024,128]{2,1,0:T(8,128)}, f32[8,1024,128]{2,1,0:T(8,128)}, f32[896,128]{1,0:T(8,128)S(1)}, f32[896,128]{1,0:T(8,128)S(1)}) custom-call(s32[8]{0:T(128)S(1)} %copy-done.13, s32[1]{0:T(128)} %bitcast.tm_ref, s32[1]{0:T(128)} %bitcast.1.mine_ref, f32[8,1024,512]{2,1,0:T(8,128)} %get-tuple-element.70.v_ref, ...), custom_call_target="tpu_custom_call" | custom-call | flops 16106127360 | bytes 113246208 | tf_op jit(solution)/shard_map/third/pallas_call | solution.py:903
  167.4 0.0 collective-permute-done.2
  167.4 0.0 collective-permute-done.3
  167.4 0.1 collective-permute-start.4
  167.5 1.8 collective-permute-done.4
  169.3 1.9 collective-permute-start.5
  171.3 5.9 %collective-permute-done.5 = f32[448,128]{1,0:T(8,128)S(1)} collective-permute-done((f32[448,128]{1,0:T(8,128)S(1)}, f32[448,128]{1,0:T(8,128)S(1)}, u32[]{:S(2)}, u32[]{:S(2)}) %collective-permute-start.5) | collective-permute-done | bytes 229408 | tf_op jit(solution)/shard_map/ppermute | solution.py:783
  177.2 10.7 %all_to_all.21 = f32[8,56,128]{2,1,0:T(8,128)S(1)} all-to-all(f32[8,56,128]{2,1,0:T(8,128)S(1)} %bitcast.69), channel_id=1, replica_groups=mesh['tm'=8,'item'=4] {'tm'}, dimensions={0} | all-to-all | bytes 458752 | tf_op jit(solution)/shard_map/all_to_all | solution.py:771
  187.9 0.7 broadcast_in_dim.2
  188.6 3.4 %all-to-all-start.3 = ((f32[8,56,128]{2,1,0:T(8,128)}), f32[8,56,128]{2,1,0:T(8,128)S(1)}, u32[]{:S(2)}, u32[]{:S(2)}) async-start(f32[8,56,128]{2,1,0:T(8,128)} %broadcast_in_dim.2), calls=%async_computation.3 | async-start | bytes 458752 | tf_op jit(solution)/shard_map/all_to_all | solution.py:771
  192.0 1.9 add_dynamic-update-slice_fusion
  193.9 6.1 %all-to-all-done.3 = f32[8,56,128]{2,1,0:T(8,128)S(1)} async-done(((f32[8,56,128]{2,1,0:T(8,128)}), f32[8,56,128]{2,1,0:T(8,128)S(1)}, u32[]{:S(2)}, u32[]{:S(2)}) %all-to-all-start.3) | async-done | bytes 229408 | tf_op jit(solution)/shard_map/all_to_all | solution.py:771
  200.0 1.6 collective-permute-start.6
  201.7 1.9 fusion
  203.5 2.5 %collective-permute-done.6 = f32[448,128]{1,0:T(8,128)S(1)} collective-permute-done((f32[448,128]{1,0:T(8,128)S(1)}, f32[448,128]{1,0:T(8,128)S(1)}, u32[]{:S(2)}, u32[]{:S(2)}) %collective-permute-start.6) | collective-permute-done | bytes 229408 | tf_op jit(solution)/shard_map/ppermute | solution.py:783
  206.1 0.1 collective-permute-start.7
  206.2 1.8 collective-permute-done.7
  208.0 0.1 maximum_select_fusion
  208.0 0.5 slice_bitcast_fusion.1
  208.6 0.8 fusion.2
  209.4 0.6 slice_bitcast_fusion
  210.0 0.6 fusion.3
  210.6 0.7 copy.40
  (12 shorter events, 0.2 us)
Async XLA Ops:
  2.0 35.6 %collective-permute-start.1 = (f32[8,128,128]{2,1,0:T(8,128)S(1)}, f32[8,128,128]{2,1,0:T(8,128)S(1)}, u32[]{:S(2)}, u32[]{:S(2)}) collective-permute-start(f32[8,128,128]{2,1,0:T(8,128)S(1)} %get-tuple-element.99), channel_id=1, source_target_pairs={{4,0},{8,4},{12,8},{16,12},{20,16},{24,20},{28,24},{5,1},{9,5},{13... | collective-permute-start | bytes 1572872 | tf_op jit(solution)/shard_map/ppermute | solution.py:830
  3.3 34.3 %collective-permute-start = (f32[8,128,128]{2,1,0:T(8,128)S(1)}, f32[8,128,128]{2,1,0:T(8,128)S(1)}, u32[]{:S(2)}, u32[]{:S(2)}) collective-permute-start(f32[8,128,128]{2,1,0:T(8,128)S(1)} %get-tuple-element.100), channel_id=1, source_target_pairs={{0,4},{4,8},{8,12},{12,16},{16,20},{20,24},{24,28},{1,5},{5,9},{9,... | collective-permute-start | bytes 1572872 | tf_op jit(solution)/shard_map/ppermute | solution.py:829
  8.8 28.8 %copy-start = (f32[128,512]{1,0:T(8,128)S(1)}, f32[128,512]{1,0:T(8,128)}, u32[]{:S(2)}) copy-start(f32[128,512]{1,0:T(8,128)} %w_ref.7) | copy-start | bytes 786436
  8.8 28.8 %copy-start.1 = (f32[512,128]{1,0:T(8,128)S(1)}, f32[512,128]{1,0:T(8,128)}, u32[]{:S(2)}) copy-start(f32[512,128]{1,0:T(8,128)} %wr_ref.5) | copy-start | bytes 786436
  8.8 28.8 %copy-start.2 = (f32[512,128]{1,0:T(8,128)S(1)}, f32[512,128]{1,0:T(8,128)}, u32[]{:S(2)}) copy-start(f32[512,128]{1,0:T(8,128)} %ws_ref.5) | copy-start | bytes 786436
  8.8 28.8 %copy-start.4 = (f32[3,512]{1,0:T(4,128)S(1)}, f32[3,512]{1,0:T(4,128)}, u32[]{:S(2)}) copy-start(f32[3,512]{1,0:T(4,128)} %rest_4_.5) | copy-start | bytes 18436
  8.8 28.8 %copy-start.5 = (f32[512]{0:T(512)S(1)}, f32[512]{0:T(512)}, u32[]{:S(2)}) copy-start(f32[512]{0:T(512)} %param.27) | copy-start | bytes 6148
  8.8 28.8 %copy-start.6 = (f32[512]{0:T(512)S(1)}, f32[512]{0:T(512)}, u32[]{:S(2)}) copy-start(f32[512]{0:T(512)} %param.28) | copy-start | bytes 6148
  8.8 28.8 %copy-start.7 = (f32[512]{0:T(512)S(1)}, f32[512]{0:T(512)}, u32[]{:S(2)}) copy-start(f32[512]{0:T(512)} %param.29) | copy-start | bytes 6148
  8.9 28.8 %copy-start.8 = (f32[512]{0:T(512)S(1)}, f32[512]{0:T(512)}, u32[]{:S(2)}) copy-start(f32[512]{0:T(512)} %param.30) | copy-start | bytes 6148
  8.9 28.8 %copy-start.9 = (f32[512]{0:T(512)S(1)}, f32[512]{0:T(512)}, u32[]{:S(2)}) copy-start(f32[512]{0:T(512)} %param.32) | copy-start | bytes 6148
  8.9 28.8 %copy-start.10 = (f32[512]{0:T(512)S(1)}, f32[512]{0:T(512)}, u32[]{:S(2)}) copy-start(f32[512]{0:T(512)} %param.33) | copy-start | bytes 6148
  8.9 28.8 %copy-start.11 = (f32[512]{0:T(512)S(1)}, f32[512]{0:T(512)}, u32[]{:S(2)}) copy-start(f32[512]{0:T(512)} %param.34) | copy-start | bytes 6148
  8.9 28.8 %copy-start.12 = (f32[512]{0:T(512)S(1)}, f32[512]{0:T(512)}, u32[]{:S(2)}) copy-start(f32[512]{0:T(512)} %param.35) | copy-start | bytes 6148
  8.9 28.8 %copy-start.13 = (s32[8]{0:T(128)S(1)}, s32[8]{0:T(128)}, u32[]{:S(2)}) copy-start(s32[8]{0:T(128)} %len_ref.7) | copy-start | bytes 100
  8.9 28.8 %copy-start.14 = (s32[8]{0:T(128)S(1)}, s32[8]{0:T(128)}, u32[]{:S(2)}) copy-start(s32[8]{0:T(128)} %cnt_ref.1) | copy-start | bytes 100
  37.7 64.3 %copy-start.3 = (f32[8,8,512]{2,1,0:T(8,128)S(1)}, f32[8,8,512]{2,1,0:T(8,128)}, u32[]{:S(2)}) copy-start(f32[8,8,512]{2,1,0:T(8,128)} %get-tuple-element.78.ch1_ref) | copy-start | bytes 393220
  91.8 10.2 %all-to-all-start.1 = ((f32[8,8,128]{2,1,0:T(8,128)}), f32[8,8,128]{2,1,0:T(8,128)S(1)}, u32[]{:S(2)}, u32[]{:S(2)}) async-start(f32[8,8,128]{2,1,0:T(8,128)} %get-tuple-element.79), calls=%async_computation.1 | async-start | bytes 65536 | tf_op jit(solution)/shard_map/all_to_all | solution.py:771
  102.0 18.1 %copy-start.15 = (f32[128]{0:T(128)S(1)}, f32[128]{0:T(128)}, u32[]{:S(2)}) copy-start(f32[128]{0:T(128)} %param.37) | copy-start | bytes 1540
  102.0 18.1 %copy-start.16 = (f32[128]{0:T(128)S(1)}, f32[128]{0:T(128)}, u32[]{:S(2)}) copy-start(f32[128]{0:T(128)} %param.39) | copy-start | bytes 1540
  114.2 53.1 %collective-permute-start.2 = (f32[8,128,128]{2,1,0:T(8,128)S(1)}, f32[8,128,128]{2,1,0:T(8,128)S(1)}, u32[]{:S(2)}, u32[]{:S(2)}) collective-permute-start(f32[8,128,128]{2,1,0:T(8,128)S(1)} %get-tuple-element.90), channel_id=1, source_target_pairs={{4,0},{8,4},{12,8},{16,12},{20,16},{24,20},{28,24},{5,1},{9,5},{13... | collective-permute-start | bytes 1572872 | tf_op jit(solution)/shard_map/ppermute | solution.py:900
  115.5 51.8 %collective-permute-start.3 = (f32[8,128,128]{2,1,0:T(8,128)S(1)}, f32[8,128,128]{2,1,0:T(8,128)S(1)}, u32[]{:S(2)}, u32[]{:S(2)}) collective-permute-start(f32[8,128,128]{2,1,0:T(8,128)S(1)} %get-tuple-element.91), channel_id=1, source_target_pairs={{0,4},{4,8},{8,12},{12,16},{16,20},{20,24},{24,28},{1,5},{5,9},{9,... | collective-permute-start | bytes 1572872 | tf_op jit(solution)/shard_map/ppermute | solution.py:901
  167.4 1.9 collective-permute-start.4
  169.3 7.8 %collective-permute-start.5 = (f32[448,128]{1,0:T(8,128)S(1)}, f32[448,128]{1,0:T(8,128)S(1)}, u32[]{:S(2)}, u32[]{:S(2)}) collective-permute-start(f32[448,128]{1,0:T(8,128)S(1)} %constant_dynamic-slice_fusion), channel_id=1, source_target_pairs={{0,2},{1,3},{2,0},{3,1},{4,6},{5,7},{6,4},{7,5},{8,10},{9,11},{10,... | collective-permute-start | bytes 688136 | tf_op jit(solution)/shard_map/ppermute | solution.py:783
  188.6 11.4 %all-to-all-start.3 = ((f32[8,56,128]{2,1,0:T(8,128)}), f32[8,56,128]{2,1,0:T(8,128)S(1)}, u32[]{:S(2)}, u32[]{:S(2)}) async-start(f32[8,56,128]{2,1,0:T(8,128)} %broadcast_in_dim.2), calls=%async_computation.3 | async-start | bytes 458752 | tf_op jit(solution)/shard_map/all_to_all | solution.py:771
  200.0 6.0 %collective-permute-start.6 = (f32[448,128]{1,0:T(8,128)S(1)}, f32[448,128]{1,0:T(8,128)S(1)}, u32[]{:S(2)}, u32[]{:S(2)}) collective-permute-start(f32[448,128]{1,0:T(8,128)S(1)} %bitcast.67), channel_id=1, source_target_pairs={{0,2},{1,3},{2,0},{3,1},{4,6},{5,7},{6,4},{7,5},{8,10},{9,11},{10,... | collective-permute-start | bytes 688136 | tf_op jit(solution)/shard_map/ppermute | solution.py:783
  206.1 1.9 collective-permute-start.7
